TPU v7x, 256 devices: a whole 4x4x8 slice. The times are simulated.
256 devices in a mesh: ctx: 32 (over x, z), exp: 8 (over y, core).
Axes of the slice: x: 4, y: 4, z: 8, core: 2. Of those that a mesh axis runs over, the one named last changes fastest.
Arguments:
- query_in: bfloat16 [6144, 2048], P('ctx', 'exp'), may hold values from -6 to 6
- key_in: bfloat16 [6144, 2048], P('ctx', 'exp'), may hold values from -6.5 to 6.5
- value_in: bfloat16 [6144, 4096], P('ctx', 'exp'), may hold values from -6 to 6
- gate_in: bfloat16 [6144, 4096], P('ctx', 'exp'), may hold values from -6 to 6
- decay_rate: float32 [32, 6144], P('exp', 'ctx'), may hold values from 0 to 1
- beta_logit: float32 [32, 6144], P('exp', 'ctx'), may hold values from -5 to 5
- head_gain: float32 [128], replicated, may hold values from 0.5 to 1.5
- out_proj: bfloat16 [4096, 2048], P('exp'), may hold values from -0.09375 to 0.09375
- residual_in: bfloat16 [6144, 2048], P('ctx'), may hold values from -6 to 6
- post_gain: float32 [2048], replicated, may hold values from 0.5 to 1.5
- expert_ids: int32 [6144, 10], P('ctx'), may hold values from 0 to 255, all different within a row; in each aligned block of 192 rows (0 to 191, 192 to 383, ...) at most 16 rows name the same one
- route_weight: float32 [6144, 10], P('ctx'), may hold values from 0.1 to 1
- w_gate: bfloat16 [256, 2048, 512], P(('ctx', 'exp')), may hold values from -0.125 to 0.125
- w_up: bfloat16 [256, 2048, 512], P(('ctx', 'exp')), may hold values from -0.125 to 0.125
- w_down: bfloat16 [256, 512, 2048], P(('ctx', 'exp')), may hold values from -0.25 to 0.25
Outputs:
- middle: bfloat16 [6144, 2048], P('ctx', 'exp')
- layer_out: bfloat16 [6144, 2048], P('ctx', 'exp')
Inputs may be any that keep to these rules, and one draw needn't show every extreme that they name: `expert_ids`: each token names 10 different experts; among the 192 rows of one device no expert is named more than 16 times.
All inputs are finite; a program needn't handle non-finite values.
Results may differ from a plain program's by a relative error of at most 0.017.
Values may be sent and summed in bfloat16 or wider, within the bound.
No kernel may reach another device: no remote copies, remote signals or barrier semaphores. Data moves between devices by JAX's collectives and lax.ppermute only.
A program may use at most 128 MiB of HBM per device.

v0:
```python
import math

import jax
import jax.numpy as jnp
from jax import lax
from jax.sharding import PartitionSpec as P

DK = 128
DV = 128


highest = lax.Precision.HIGHEST
eps_small = 1e-06


def from_behind(block, axis, distance):
    devices = range(lax.axis_size(axis))
    route = [(i - distance, i) for i in devices if i - distance in devices]
    return lax.ppermute(block, axis, route)


def unit_rows(field):
    return field * lax.rsqrt(jnp.sum(field * field, axis=-1, keepdims=True) + eps_small)


def matmul_heads(left, right):
    return jnp.einsum("hij,hjk->hik", left, right, precision=highest)


def block_terms(queries, keys_all, values, decays, update_rate):
    length = queries.shape[2]
    value_width = values.shape[-1]
    key_width = keys_all.shape[-1]
    log_decay = -jnp.cumsum(decays, axis=-1)
    on_or_below = jnp.tril(jnp.ones((length, length), bool))
    below = jnp.tril(jnp.ones((length, length), bool), -1)
    dispersion = jnp.where(on_or_below, log_decay[..., :, None] - log_decay[..., None, :], 0.0)
    fading = jnp.where(on_or_below, jnp.exp(dispersion), 0.0) * update_rate[..., None, :]
    inner_keys = jnp.einsum("hnld,hnmd->hnlm", keys_all, keys_all, precision=highest)
    system = jnp.eye(length, dtype=jnp.float32) + jnp.where(below, inner_keys * fading, 0.0)
    leading = jnp.exp(log_decay)[..., None]
    solved = jax.scipy.linalg.solve_triangular(
        system,
        jnp.concatenate([values, leading * keys_all], axis=-1),
        lower=True,
        unit_diagonal=True,
    )
    unique = solved[..., :value_width]
    carried = solved[..., value_width:]
    weights = jnp.einsum("hnld,hnmd->hnlm", queries, keys_all, precision=highest) * fading
    inside = jnp.einsum("hnlm,hnmv->hnlv", weights, unique, precision=highest)
    reaching = leading * queries - jnp.einsum(
        "hnlm,hnmk->hnlk", weights, carried, precision=highest
    )
    last_log = log_decay[..., -1:]
    tail_keys = (jnp.exp(last_log - log_decay) * update_rate)[..., None] * keys_all
    identity = jnp.eye(key_width, dtype=jnp.float32)
    transition = jnp.exp(log_decay[..., -1])[..., None, None] * identity - jnp.einsum(
        "hnlk,hnlj->hnkj", carried, tail_keys, precision=highest
    )
    injection = jnp.einsum("hnlv,hnlj->hnvj", unique, tail_keys, precision=highest)
    return (inside, reaching, transition, injection)


def local_prefix(transition, injection):
    head_count = transition.shape[0]
    key_width = transition.shape[2]
    value_width = injection.shape[2]
    identity = jnp.broadcast_to(
        jnp.eye(key_width, dtype=jnp.float32), (head_count, key_width, key_width)
    )
    initial = (identity, jnp.zeros((head_count, value_width, key_width), jnp.float32))

    def advance(carry, inputs):
        accum_a, accum_b = carry
        step_a, step_b = inputs
        return ((matmul_heads(accum_a, step_a), matmul_heads(accum_b, step_a) + step_b), carry)

    totals, before = lax.scan(
        advance, initial, (jnp.moveaxis(transition, 1, 0), jnp.moveaxis(injection, 1, 0))
    )
    return (totals[0], totals[1], before[0], before[1])


def slot_tables(expert_ids, route_weight, experts, slot_count):
    token_total, top_count = expert_ids.shape
    flat_ids = expert_ids.reshape(-1)
    pair_order = jnp.argsort(flat_ids, stable=True)
    ranked = flat_ids[pair_order]
    numbers = jnp.arange(experts, dtype=jnp.int32)
    starts = jnp.searchsorted(ranked, numbers, side="left")
    finish = jnp.searchsorted(ranked, numbers, side="right")
    slot_index = jnp.arange(slot_count, dtype=jnp.int32)
    occupied = (slot_index[None, :] < (finish - starts)[:, None]).astype(jnp.int32)
    pair_index = pair_order[
        jnp.minimum(starts[:, None] + slot_index[None, :], token_total * top_count - 1)
    ]
    token_of = pair_index // top_count
    weight_of = jnp.where(occupied > 0, route_weight.reshape(-1)[pair_index], 0.0)
    return (token_of, weight_of, occupied)


def run_expert(row_block, occupied, gate_weight, up_weight, down_weight):
    gate_act = jnp.dot(row_block, gate_weight, preferred_element_type=jnp.float32)
    up_act = jnp.dot(row_block, up_weight, preferred_element_type=jnp.float32)
    hidden = (jax.nn.silu(gate_act) * up_act).astype(jnp.bfloat16)
    produced = jnp.dot(hidden, down_weight, preferred_element_type=jnp.float32).astype(jnp.bfloat16)
    return jnp.where(occupied[:, None] > 0, produced, jnp.zeros_like(produced))


def prepare_rows(
    whole_rows, post_gain, token_of, weight_of, occupied, column, rows_ctx, columns, slot_count
):
    model_width = whole_rows.shape[1]
    held_all = whole_rows.astype(jnp.float32)
    normed = (
        held_all
        * lax.rsqrt(jnp.mean(held_all * held_all, axis=-1, keepdims=True) + eps_small)
        * post_gain
    ).astype(jnp.bfloat16)
    grid_tokens = lax.dynamic_index_in_dim(
        token_of.reshape(rows_ctx, columns, slot_count), column, 1, False
    )
    grid_live = lax.dynamic_index_in_dim(
        occupied.reshape(rows_ctx, columns, slot_count), column, 1, False
    )
    grid_weight = lax.dynamic_index_in_dim(
        weight_of.reshape(rows_ctx, columns, slot_count), column, 1, False
    )
    picked = jnp.where(grid_live.reshape(-1, 1) > 0, normed[grid_tokens.reshape(-1)], 0).reshape(
        rows_ctx, slot_count, model_width
    )
    return (picked, grid_live, grid_tokens, grid_weight)


def weigh_rows(returned, grid_tokens, grid_weight, length):
    model_width = returned.shape[-1]
    weighted = returned.reshape(-1, model_width).astype(jnp.float32) * grid_weight.reshape(-1, 1)
    return jnp.zeros((length, model_width), jnp.float32).at[grid_tokens.reshape(-1)].add(weighted)


def on_device(
    query_in,
    key_in,
    value_in,
    gate_in,
    decay_rate,
    beta_logit,
    head_gain,
    out_proj,
    residual_in,
    post_gain,
    expert_ids,
    route_weight,
    w_gate,
    w_up,
    w_down,
):
    length = query_in.shape[0]
    head_count = decay_rate.shape[0]
    qk_count = query_in.shape[1] // DK
    group_ratio = head_count // qk_count
    block_len = math.gcd(64, length)
    block_total = length // block_len
    queries = unit_rows(query_in.astype(jnp.float32).reshape(length, qk_count, DK)) * DK ** (-0.5)
    keys_all = unit_rows(key_in.astype(jnp.float32).reshape(length, qk_count, DK))
    queries = jnp.repeat(jnp.transpose(queries, (1, 0, 2)), group_ratio, axis=0).reshape(
        head_count, block_total, block_len, DK
    )
    keys_all = jnp.repeat(jnp.transpose(keys_all, (1, 0, 2)), group_ratio, axis=0).reshape(
        head_count, block_total, block_len, DK
    )
    values = jnp.transpose(
        value_in.astype(jnp.float32).reshape(length, head_count, DV), (1, 0, 2)
    ).reshape(head_count, block_total, block_len, DV)
    decays = decay_rate.reshape(head_count, block_total, block_len)
    update_rate = jax.nn.sigmoid(beta_logit).reshape(head_count, block_total, block_len)
    inside, reaching, transition, injection = block_terms(
        queries, keys_all, values, decays, update_rate
    )
    whole_a, whole_b, before_a, before_b = local_prefix(transition, injection)

    def pass_on(step_index, carried_state):
        leaving = matmul_heads(carried_state, whole_a) + whole_b
        return from_behind(leaving, "ctx", 1)

    entering = lax.fori_loop(0, lax.axis_size("ctx") - 1, pass_on, jnp.zeros_like(whole_b))
    starts = jnp.einsum("hvk,nhkj->hnvj", entering, before_a, precision=highest) + jnp.transpose(
        before_b, (1, 0, 2, 3)
    )
    outputs = inside + jnp.einsum("hnlk,hnvk->hnlv", reaching, starts, precision=highest)
    outputs = jnp.transpose(outputs.reshape(head_count, length, DV), (1, 0, 2))
    scaling = lax.rsqrt(jnp.mean(outputs * outputs, axis=-1, keepdims=True) + eps_small)
    gate_act = jax.nn.silu(gate_in.astype(jnp.float32).reshape(length, head_count, DV))
    gated = (
        (outputs * scaling * head_gain * gate_act)
        .astype(jnp.bfloat16)
        .reshape(length, head_count * DV)
    )
    mixed = jnp.dot(gated, out_proj, preferred_element_type=jnp.float32)
    columns = lax.axis_size("exp")
    column = lax.axis_index("exp")
    rows_ctx = lax.axis_size("ctx")
    model_width = mixed.shape[1]
    share_width = model_width // columns
    top_count = expert_ids.shape[1]
    experts = rows_ctx * columns
    slot_count = 16 * (1 + length * top_count // (experts * 16))
    token_of, weight_of, occupied = slot_tables(expert_ids, route_weight, experts, slot_count)
    summed_all = lax.psum(mixed, "exp")
    whole_rows = (residual_in.astype(jnp.float32) + summed_all).astype(jnp.bfloat16)
    middle = lax.dynamic_slice_in_dim(whole_rows, column * share_width, share_width, 1)
    picked, grid_live, grid_tokens, grid_weight = prepare_rows(
        whole_rows, post_gain, token_of, weight_of, occupied, column, rows_ctx, columns, slot_count
    )
    arrived, arrived_flags = (
        lax.all_to_all(picked, "ctx", split_axis=0, concat_axis=0, tiled=True),
        lax.all_to_all(grid_live, "ctx", split_axis=0, concat_axis=0, tiled=True),
    )
    produced = run_expert(
        arrived.reshape(-1, model_width), arrived_flags.reshape(-1), w_gate[0], w_up[0], w_down[0]
    )
    returned = lax.all_to_all(
        produced.reshape(rows_ctx, slot_count, model_width),
        "ctx",
        split_axis=0,
        concat_axis=0,
        tiled=True,
    )
    partial_mix = weigh_rows(returned, grid_tokens, grid_weight, length)
    expert_mix = lax.psum_scatter(
        partial_mix.astype(jnp.bfloat16), "exp", scatter_dimension=1, tiled=True
    ).astype(jnp.float32)
    layer_result = (middle.astype(jnp.float32) + expert_mix).astype(jnp.bfloat16)
    return (middle, layer_result)


def solution(mesh):
    in_specs = (
        P("ctx", "exp"),
        P("ctx", "exp"),
        P("ctx", "exp"),
        P("ctx", "exp"),
        P("exp", "ctx"),
        P("exp", "ctx"),
        P(),
        P("exp", None),
        P("ctx", None),
        P(),
        P("ctx", None),
        P("ctx", None),
        P(("ctx", "exp"), None, None),
        P(("ctx", "exp"), None, None),
        P(("ctx", "exp"), None, None),
    )
    out_specs = (P("ctx", "exp"), P("ctx", "exp"))
    return jax.shard_map(
        on_device, mesh=mesh, in_specs=in_specs, out_specs=out_specs, check_vma=False
    )
```

profile of v0, /device:TPU:1, one launch (start us, length us, event | category | flops | bytes accessed | tf_op | source)
XLA Modules:
  0.0 840.3 jit_solution(8236467392579077336)
XLA Ops:
  13.4 10.4 %gather_fusion.2 = s32[1920]{0:T(1024)S(1)} fusion(s32[1920]{0:T(1024)S(1)} %reshape.301, s32[2048]{0:T(1024)S(1)} %pad_clamp_fusion.2), kind=kCustom, calls=%fused_computation.2 | custom fusion | bytes 23040 | tf_op jit(solution)/shard_map/gather | solution.py:89
  23.8 19.7 %while.77 = (s32[]{:T(128)}, u32[256]{0:T(256)S(1)}, u32[256]{0:T(256)S(1)}, s32[1920]{0:T(1024)S(1)}, s32[]{:T(128)}, /*index=5*/s32[]{:T(128)}, s32[]{}) while((s32[]{:T(128)}, u32[256]{0:T(256)S(1)}, u32[256]{0:T(256)S(1)}, s32[1920]{0:T(1024)S(1)}, s32[]{:T(128)}, /*index=5*/s32[]{:T(128)}, s32[]{}) %tuple.116), condition=%wide.region_11.12_spmd.clone, body=%wide.region_10.11_spmd.clone.sunk | while | flops 4356 | bytes 16492 | solution.py:91
  43.7 23.0 %gather_fusion.3 = s32[4096]{0:T(1024)S(1)} fusion(s32[1920]{0:T(1024)S(1)} %get-tuple-element.200, s32[4096]{0:T(1024)S(1)} %broadcast_clamp_fusion.1), kind=kCustom, calls=%fused_computation.3 | custom fusion | bytes 49152 | tf_op jit(solution)/shard_map/gather | solution.py:95
  67.3 23.0 %gather_fusion.5 = f32[4096]{0:T(1024)S(1)} fusion(f32[1920]{0:T(1024)S(1)} %reshape.305, s32[4096]{0:T(1024)S(1)} %broadcast_clamp_fusion), kind=kCustom, calls=%fused_computation.5 | custom fusion | bytes 49152 | tf_op jit(solution)/shard_map/gather | solution.py:99
  90.5 19.7 %while.78 = (s32[]{:T(128)}, u32[256]{0:T(256)S(1)}, u32[256]{0:T(256)S(1)}, s32[1920]{0:T(1024)S(1)}, s32[]{:T(128)}, /*index=5*/s32[]{:T(128)}, s32[]{}) while((s32[]{:T(128)}, u32[256]{0:T(256)S(1)}, u32[256]{0:T(256)S(1)}, s32[1920]{0:T(1024)S(1)}, s32[]{:T(128)}, /*index=5*/s32[]{:T(128)}, s32[]{}) %tuple.132), condition=%wide.region_13.14_spmd.clone, body=%wide.region_12.13_spmd.clone.sunk | while | flops 4356 | bytes 16492 | solution.py:92
  111.7 12.0 %all-to-all-start = ((s32[32,1,16]{2,1,0:T(1,128)}), s32[32,1,16]{2,1,0:T(1,128)}, u32[]{:S(2)}, u32[]{:S(2)}) async-start(s32[32,1,16]{2,1,0:T(1,128)} %copy.128), calls=%async_computation | async-start | bytes 32768 | tf_op jit(solution)/shard_map/all_to_all | solution.py:218
  132.3 59.6 %custom-call.4 = f32[4,3,1,64,64]{3,4,2,1,0:T(8,128)} custom-call(f32[4,3,1,64,64]{4,3,2,1,0:T(8,128)S(1)} %fusion.42), custom_call_target="InvertDiagBlocksLowerTriangular" | custom-call | tf_op jit(solution)/shard_map/jit(_solve_triangular)/vmap(vmap())/triangular_solve | solution.py:42
  209.3 15.6 %while.76 = (s32[]{:T(128)}, f32[4,128,128]{1,2,0:T(8,128)S(1)}, f32[4,128,128]{1,2,0:T(8,128)S(1)}, f32[3,4,128,128]{2,3,1,0:T(8,128)}, f32[3,4,128,128]{2,3,1,...) while((s32[]{:T(128)}, f32[4,128,128]{1,2,0:T(8,128)S(1)}, ...), condition=%wide.region_4.5_spmd.clone, body=%wide.region_3.4_spmd.clone.sunk | while | flops 201523200 | bytes 4980864 | solution.py:79
  225.2 297.0 %while.75 = (s32[]{:T(128)}, f32[4,128,128]{2,1,0:T(8,128)S(1)}, f32[4,128,128]{2,1,0:T(8,128)S(1)}, f32[4,128,128]{2,1,0:T(8,128)S(1)}, s32[]{:T(128)}) while((s32[]{:T(128)}, f32[4,128,128]{2,1,0:T(8,128)S(1)}, f32[4,128,128]{2,1,0:T(8,128)S(1)}, f32[4,128,128]{2,1,0:T(8,128)S(1)}, s32[]{:T(128)}) %tuple.125), condition=%wide.region_6.7_spmd, body=%wide.region_5.6_spmd.sunk | while | flops 100728832 | bytes 2097253 | solution.py:187
  304.1 6.1 collective-permute-start
  389.8 5.9 collective-permute-start
  447.6 9.7 %collective-permute-start = (f32[4,128,128]{2,1,0:T(8,128)S(1)}, f32[4,128,128]{2,1,0:T(8,128)S(1)}, u32[]{:S(2)}, u32[]{:S(2)}) collective-permute-start(f32[4,128,128]{2,1,0:T(8,128)S(1)} %convolution_add_fusion.3), channel_id=1, source_target_pairs={{0,8},{8,16},{16,24},{24,32},{32,40},{40,48},{48,56},{56,64},{64,7... | collective-permute-start | bytes 786440 | tf_op jit(solution)/shard_map/while/body/eval_jaxpr/ppermute | solution.py:19
  478.8 6.1 collective-permute-start
  488.6 6.2 collective-permute-start
  498.9 6.2 collective-permute-start
  510.1 6.5 collective-permute-start
  528.5 123.7 %all-reduce.2.cloned.1.call-done = f32[192,2048]{1,0:T(8,128)} async-done(((f32[192,2048]{1,0:T(8,128)}), f32[192,2048]{1,0:T(8,128)}) %all-reduce.2.cloned.1.call-update) | async-done | bytes 1572880 | tf_op jit(solution)/shard_map/psum | solution.py:210
  661.6 9.7 %all-to-all-start.1 = ((bf16[32,16,2048]{2,1,0:T(8,128)(2,1)}), bf16[32,16,2048]{2,1,0:T(8,128)(2,1)}, u32[]{:S(2)}, u32[]{:S(2)}) async-start(bf16[32,16,2048]{2,1,0:T(8,128)(2,1)} %broadcast_select_fusion.4), calls=%async_computation.1 | async-start | bytes 4194304 | tf_op jit(solution)/shard_map/all_to_all | solution.py:217
  672.2 47.3 %all-to-all-done.1 = bf16[32,16,2048]{2,1,0:T(8,128)(2,1)} async-done(((bf16[32,16,2048]{2,1,0:T(8,128)(2,1)}), bf16[32,16,2048]{2,1,0:T(8,128)(2,1)}, u32[]{:S(2)}, u32[]{:S(2)}) %all-to-all-start.1) | async-done | bytes 2097184 | tf_op jit(solution)/shard_map/all_to_all | solution.py:217
  724.0 6.3 fusion.20
  730.3 6.1 all-to-all-start.2
  736.5 48.0 %all-to-all-done.2 = bf16[32,16,2048]{2,1,0:T(8,128)(2,1)} async-done(((bf16[32,16,2048]{2,1,0:T(8,128)(2,1)}), bf16[32,16,2048]{2,1,0:T(8,128)(2,1)}, u32[]{:S(2)}, u32[]{:S(2)}) %all-to-all-start.2) | async-done | bytes 2097184 | tf_op jit(solution)/shard_map/all_to_all | solution.py:223
  784.5 9.7 %scatter_custom_fusion = f32[192,2048]{1,0:T(8,128)} fusion(s32[512]{0:T(512)S(1)} %bitcast.148, bf16[512,2048]{1,0:T(8,128)(2,1)} %bitcast.32, f32[512]{0:T(512)S(1)} %mul.192, f32[]{:T(128)} %constant.137.clone.1), kind=kCustom, calls=%fused_computation.41 | custom fusion | flops 3145728 | bytes 3672068 | tf_op jit(solution)/shard_map/scatter-add | solution.py:139
  796.6 35.2 %reduce-scatter.2.cloned.1.call-done = bf16[192,256]{1,0:T(8,128)(2,1)} async-done(((bf16[192,2048]{1,0:T(8,128)(2,1)}), bf16[192,256]{1,0:T(8,128)(2,1)}) %reduce-scatter.2.cloned.1.call-update) | async-done | bytes 98320 | tf_op jit(solution)/shard_map/reduce_scatter | solution.py:231
  (342 shorter events, 363.1 us)
Async XLA Ops:
  111.7 549.9 %all-to-all-start = ((s32[32,1,16]{2,1,0:T(1,128)}), s32[32,1,16]{2,1,0:T(1,128)}, u32[]{:S(2)}, u32[]{:S(2)}) async-start(s32[32,1,16]{2,1,0:T(1,128)} %copy.128), calls=%async_computation | async-start | bytes 32768 | tf_op jit(solution)/shard_map/all_to_all | solution.py:218
  123.7 528.5 %all-reduce.2.cloned.1.call-start = ((), (), s32[]{:S(2)}) async-start(), calls=%async_computation.4 | async-start | bytes 3145728 | tf_op jit(solution)/shard_map/psum | solution.py:210
  282.1 9.9 %collective-permute-start = (f32[4,128,128]{2,1,0:T(8,128)S(1)}, f32[4,128,128]{2,1,0:T(8,128)S(1)}, u32[]{:S(2)}, u32[]{:S(2)}) collective-permute-start(f32[4,128,128]{2,1,0:T(8,128)S(1)} %convolution_add_fusion.3), channel_id=1, source_target_pairs={{0,8},{8,16},{16,24},{24,32},{32,40},{40,48},{48,56},{56,64},{64,7... | collective-permute-start | bytes 786440 | tf_op jit(solution)/shard_map/while/body/eval_jaxpr/ppermute | solution.py:19
  292.4 11.3 %collective-permute-start = (f32[4,128,128]{2,1,0:T(8,128)S(1)}, f32[4,128,128]{2,1,0:T(8,128)S(1)}, u32[]{:S(2)}, u32[]{:S(2)}) collective-permute-start(f32[4,128,128]{2,1,0:T(8,128)S(1)} %convolution_add_fusion.3), channel_id=1, source_target_pairs={{0,8},{8,16},{16,24},{24,32},{32,40},{40,48},{48,56},{56,64},{64,7... | collective-permute-start | bytes 786440 | tf_op jit(solution)/shard_map/while/body/eval_jaxpr/ppermute | solution.py:19
  304.1 11.5 %collective-permute-start = (f32[4,128,128]{2,1,0:T(8,128)S(1)}, f32[4,128,128]{2,1,0:T(8,128)S(1)}, u32[]{:S(2)}, u32[]{:S(2)}) collective-permute-start(f32[4,128,128]{2,1,0:T(8,128)S(1)} %convolution_add_fusion.3), channel_id=1, source_target_pairs={{0,8},{8,16},{16,24},{24,32},{32,40},{40,48},{48,56},{56,64},{64,7... | collective-permute-start | bytes 786440 | tf_op jit(solution)/shard_map/while/body/eval_jaxpr/ppermute | solution.py:19
  316.0 8.7 %collective-permute-start = (f32[4,128,128]{2,1,0:T(8,128)S(1)}, f32[4,128,128]{2,1,0:T(8,128)S(1)}, u32[]{:S(2)}, u32[]{:S(2)}) collective-permute-start(f32[4,128,128]{2,1,0:T(8,128)S(1)} %convolution_add_fusion.3), channel_id=1, source_target_pairs={{0,8},{8,16},{16,24},{24,32},{32,40},{40,48},{48,56},{56,64},{64,7... | collective-permute-start | bytes 786440 | tf_op jit(solution)/shard_map/while/body/eval_jaxpr/ppermute | solution.py:19
  333.1 8.6 %collective-permute-start = (f32[4,128,128]{2,1,0:T(8,128)S(1)}, f32[4,128,128]{2,1,0:T(8,128)S(1)}, u32[]{:S(2)}, u32[]{:S(2)}) collective-permute-start(f32[4,128,128]{2,1,0:T(8,128)S(1)} %convolution_add_fusion.3), channel_id=1, source_target_pairs={{0,8},{8,16},{16,24},{24,32},{32,40},{40,48},{48,56},{56,64},{64,7... | collective-permute-start | bytes 786440 | tf_op jit(solution)/shard_map/while/body/eval_jaxpr/ppermute | solution.py:19
  351.2 8.6 %collective-permute-start = (f32[4,128,128]{2,1,0:T(8,128)S(1)}, f32[4,128,128]{2,1,0:T(8,128)S(1)}, u32[]{:S(2)}, u32[]{:S(2)}) collective-permute-start(f32[4,128,128]{2,1,0:T(8,128)S(1)} %convolution_add_fusion.3), channel_id=1, source_target_pairs={{0,8},{8,16},{16,24},{24,32},{32,40},{40,48},{48,56},{56,64},{64,7... | collective-permute-start | bytes 786440 | tf_op jit(solution)/shard_map/while/body/eval_jaxpr/ppermute | solution.py:19
  368.9 9.3 %collective-permute-start = (f32[4,128,128]{2,1,0:T(8,128)S(1)}, f32[4,128,128]{2,1,0:T(8,128)S(1)}, u32[]{:S(2)}, u32[]{:S(2)}) collective-permute-start(f32[4,128,128]{2,1,0:T(8,128)S(1)} %convolution_add_fusion.3), channel_id=1, source_target_pairs={{0,8},{8,16},{16,24},{24,32},{32,40},{40,48},{48,56},{56,64},{64,7... | collective-permute-start | bytes 786440 | tf_op jit(solution)/shard_map/while/body/eval_jaxpr/ppermute | solution.py:19
  378.6 10.9 %collective-permute-start = (f32[4,128,128]{2,1,0:T(8,128)S(1)}, f32[4,128,128]{2,1,0:T(8,128)S(1)}, u32[]{:S(2)}, u32[]{:S(2)}) collective-permute-start(f32[4,128,128]{2,1,0:T(8,128)S(1)} %convolution_add_fusion.3), channel_id=1, source_target_pairs={{0,8},{8,16},{16,24},{24,32},{32,40},{40,48},{48,56},{56,64},{64,7... | collective-permute-start | bytes 786440 | tf_op jit(solution)/shard_map/while/body/eval_jaxpr/ppermute | solution.py:19
  389.8 11.8 %collective-permute-start = (f32[4,128,128]{2,1,0:T(8,128)S(1)}, f32[4,128,128]{2,1,0:T(8,128)S(1)}, u32[]{:S(2)}, u32[]{:S(2)}) collective-permute-start(f32[4,128,128]{2,1,0:T(8,128)S(1)} %convolution_add_fusion.3), channel_id=1, source_target_pairs={{0,8},{8,16},{16,24},{24,32},{32,40},{40,48},{48,56},{56,64},{64,7... | collective-permute-start | bytes 786440 | tf_op jit(solution)/shard_map/while/body/eval_jaxpr/ppermute | solution.py:19
  402.0 10.0 %collective-permute-start = (f32[4,128,128]{2,1,0:T(8,128)S(1)}, f32[4,128,128]{2,1,0:T(8,128)S(1)}, u32[]{:S(2)}, u32[]{:S(2)}) collective-permute-start(f32[4,128,128]{2,1,0:T(8,128)S(1)} %convolution_add_fusion.3), channel_id=1, source_target_pairs={{0,8},{8,16},{16,24},{24,32},{32,40},{40,48},{48,56},{56,64},{64,7... | collective-permute-start | bytes 786440 | tf_op jit(solution)/shard_map/while/body/eval_jaxpr/ppermute | solution.py:19
  420.5 8.6 %collective-permute-start = (f32[4,128,128]{2,1,0:T(8,128)S(1)}, f32[4,128,128]{2,1,0:T(8,128)S(1)}, u32[]{:S(2)}, u32[]{:S(2)}) collective-permute-start(f32[4,128,128]{2,1,0:T(8,128)S(1)} %convolution_add_fusion.3), channel_id=1, source_target_pairs={{0,8},{8,16},{16,24},{24,32},{32,40},{40,48},{48,56},{56,64},{64,7... | collective-permute-start | bytes 786440 | tf_op jit(solution)/shard_map/while/body/eval_jaxpr/ppermute | solution.py:19
  429.5 8.6 %collective-permute-start = (f32[4,128,128]{2,1,0:T(8,128)S(1)}, f32[4,128,128]{2,1,0:T(8,128)S(1)}, u32[]{:S(2)}, u32[]{:S(2)}) collective-permute-start(f32[4,128,128]{2,1,0:T(8,128)S(1)} %convolution_add_fusion.3), channel_id=1, source_target_pairs={{0,8},{8,16},{16,24},{24,32},{32,40},{40,48},{48,56},{56,64},{64,7... | collective-permute-start | bytes 786440 | tf_op jit(solution)/shard_map/while/body/eval_jaxpr/ppermute | solution.py:19
  438.6 8.6 %collective-permute-start = (f32[4,128,128]{2,1,0:T(8,128)S(1)}, f32[4,128,128]{2,1,0:T(8,128)S(1)}, u32[]{:S(2)}, u32[]{:S(2)}) collective-permute-start(f32[4,128,128]{2,1,0:T(8,128)S(1)} %convolution_add_fusion.3), channel_id=1, source_target_pairs={{0,8},{8,16},{16,24},{24,32},{32,40},{40,48},{48,56},{56,64},{64,7... | collective-permute-start | bytes 786440 | tf_op jit(solution)/shard_map/while/body/eval_jaxpr/ppermute | solution.py:19
  447.6 13.0 %collective-permute-start = (f32[4,128,128]{2,1,0:T(8,128)S(1)}, f32[4,128,128]{2,1,0:T(8,128)S(1)}, u32[]{:S(2)}, u32[]{:S(2)}) collective-permute-start(f32[4,128,128]{2,1,0:T(8,128)S(1)} %convolution_add_fusion.3), channel_id=1, source_target_pairs={{0,8},{8,16},{16,24},{24,32},{32,40},{40,48},{48,56},{56,64},{64,7... | collective-permute-start | bytes 786440 | tf_op jit(solution)/shard_map/while/body/eval_jaxpr/ppermute | solution.py:19
  461.0 8.6 %collective-permute-start = (f32[4,128,128]{2,1,0:T(8,128)S(1)}, f32[4,128,128]{2,1,0:T(8,128)S(1)}, u32[]{:S(2)}, u32[]{:S(2)}) collective-permute-start(f32[4,128,128]{2,1,0:T(8,128)S(1)} %convolution_add_fusion.3), channel_id=1, source_target_pairs={{0,8},{8,16},{16,24},{24,32},{32,40},{40,48},{48,56},{56,64},{64,7... | collective-permute-start | bytes 786440 | tf_op jit(solution)/shard_map/while/body/eval_jaxpr/ppermute | solution.py:19
  478.8 9.4 %collective-permute-start = (f32[4,128,128]{2,1,0:T(8,128)S(1)}, f32[4,128,128]{2,1,0:T(8,128)S(1)}, u32[]{:S(2)}, u32[]{:S(2)}) collective-permute-start(f32[4,128,128]{2,1,0:T(8,128)S(1)} %convolution_add_fusion.3), channel_id=1, source_target_pairs={{0,8},{8,16},{16,24},{24,32},{32,40},{40,48},{48,56},{56,64},{64,7... | collective-permute-start | bytes 786440 | tf_op jit(solution)/shard_map/while/body/eval_jaxpr/ppermute | solution.py:19
  488.6 9.9 %collective-permute-start = (f32[4,128,128]{2,1,0:T(8,128)S(1)}, f32[4,128,128]{2,1,0:T(8,128)S(1)}, u32[]{:S(2)}, u32[]{:S(2)}) collective-permute-start(f32[4,128,128]{2,1,0:T(8,128)S(1)} %convolution_add_fusion.3), channel_id=1, source_target_pairs={{0,8},{8,16},{16,24},{24,32},{32,40},{40,48},{48,56},{56,64},{64,7... | collective-permute-start | bytes 786440 | tf_op jit(solution)/shard_map/while/body/eval_jaxpr/ppermute | solution.py:19
  498.9 10.7 %collective-permute-start = (f32[4,128,128]{2,1,0:T(8,128)S(1)}, f32[4,128,128]{2,1,0:T(8,128)S(1)}, u32[]{:S(2)}, u32[]{:S(2)}) collective-permute-start(f32[4,128,128]{2,1,0:T(8,128)S(1)} %convolution_add_fusion.3), channel_id=1, source_target_pairs={{0,8},{8,16},{16,24},{24,32},{32,40},{40,48},{48,56},{56,64},{64,7... | collective-permute-start | bytes 786440 | tf_op jit(solution)/shard_map/while/body/eval_jaxpr/ppermute | solution.py:19
  510.1 12.1 %collective-permute-start = (f32[4,128,128]{2,1,0:T(8,128)S(1)}, f32[4,128,128]{2,1,0:T(8,128)S(1)}, u32[]{:S(2)}, u32[]{:S(2)}) collective-permute-start(f32[4,128,128]{2,1,0:T(8,128)S(1)} %convolution_add_fusion.3), channel_id=1, source_target_pairs={{0,8},{8,16},{16,24},{24,32},{32,40},{40,48},{48,56},{56,64},{64,7... | collective-permute-start | bytes 786440 | tf_op jit(solution)/shard_map/while/body/eval_jaxpr/ppermute | solution.py:19
  661.6 58.0 %all-to-all-start.1 = ((bf16[32,16,2048]{2,1,0:T(8,128)(2,1)}), bf16[32,16,2048]{2,1,0:T(8,128)(2,1)}, u32[]{:S(2)}, u32[]{:S(2)}) async-start(bf16[32,16,2048]{2,1,0:T(8,128)(2,1)} %broadcast_select_fusion.4), calls=%async_computation.1 | async-start | bytes 4194304 | tf_op jit(solution)/shard_map/all_to_all | solution.py:217
  730.3 54.3 %all-to-all-start.2 = ((bf16[32,16,2048]{2,1,0:T(8,128)(2,1)}), bf16[32,16,2048]{2,1,0:T(8,128)(2,1)}, u32[]{:S(2)}, u32[]{:S(2)}) async-start(bf16[32,16,2048]{2,1,0:T(8,128)(2,1)} %bitcast.143), calls=%async_computation.2 | async-start | bytes 4194304 | tf_op jit(solution)/shard_map/all_to_all | solution.py:223
  736.3 95.5 %reduce-scatter.2.cloned.1.call-start = ((), (), s32[]{:S(2)}) async-start(), calls=%async_computation.5 | async-start | bytes 884736 | tf_op jit(solution)/shard_map/reduce_scatter | solution.py:231
  (33 other events, 1239.3 us)
Sparse Core Ops, SparseCore 0:
  528.1 124.1 all-reduce.1
  796.7 35.0 reduce-scatter.1
where the time goes:
time: 844 us; the launch traced here: 840 us
  waiting for transfers between devices  374 us (44%)
  starting transfers between devices  192 us (23%)
  local copies, waits for them, and re-layouts  112 us (13%)
  other arithmetic  93.6 us (11%)
  matrix products  51.4 us (6%)
  between operations  14.7 us (2%)
    ppermute x31, starting transfers between devices, from_behind(): return lax.ppermute(block, axis, route)  164 us
    psum x1, waiting for transfers between devices, on_device(): summed_all = lax.psum(mixed, 'exp')  124 us
    ppermute x31, waiting for transfers between devices, from_behind(): return lax.ppermute(block, axis, route)  120 us
    another operation x3, other arithmetic, block_terms(): jax.scipy.linalg.solve_triangular(system, jnp.concatenate([values, leadin...  59.7 us
    all_to_all x1, waiting for transfers between devices, on_device(): lax.all_to_all(produced.reshape(rows_ctx, slot_count, model_width), 'ctx'...  48 us
    all_to_all x1, waiting for transfers between devices, on_device(): lax.all_to_all(picked, 'ctx', split_axis=0, concat_axis=0, tiled=True)  47.3 us
    reduce_scatter x1, waiting for transfers between devices, on_device(): lax.psum_scatter(partial_mix.astype(jnp.bfloat16), 'exp', scatter_dimensi...  35.2 us
    gather x2, local copies, waits for them, and re-layouts, slot_tables(): route_weight.reshape(-1)[pair_index]  23.1 us
  transfers between devices with their start and end apart: 36, of which 35 were waited for; matrix products, arithmetic and copies ran while one was open for 15% of the time, Pallas kernels for 0%

commit v1 on v0

v1 whole, which is shorter than its diff:
```python
import functools

import jax
import jax.numpy as jnp
from jax import lax
from jax.experimental import pallas as pl
from jax.experimental.pallas import tpu as pltpu
from jax.sharding import Mesh, PartitionSpec as P

DK = 128
DV = 128
SLOTS = 16
EPS = 1e-06
BF = jnp.bfloat16
F32 = jnp.float32
NN = ((1,), (0,))
NT = ((1,), (1,))
TN = ((0,), (0,))
VMEM_BYTES = 50 * 1024 * 1024


def mm(left, right, dims=NN):
    return lax.dot_general(
        left.astype(BF), right.astype(BF), (dims, ((), ())), preferred_element_type=F32
    )


def exact(left, right, dims=NN):
    return lax.dot_general(
        left, right, (dims, ((), ())), precision=lax.Precision.HIGHEST, preferred_element_type=F32
    )


def halves(value):
    high = value.astype(BF)
    return high, (value - high.astype(F32)).astype(BF)


def mm3(left, right, dims=NN):
    left_high, left_low = halves(left)
    right_high, right_low = halves(right)
    return (
        mm(left_high, right_high, dims)
        + mm(left_high, right_low, dims)
        + mm(left_low, right_high, dims)
    )


def silu(value):
    return value / (1.0 + jnp.exp(-value))


def call(kernel, out_shape, *operands, flops=0, moved=0, **more):
    return pl.pallas_call(
        kernel,
        out_shape=out_shape,
        compiler_params=pltpu.CompilerParams(vmem_limit_bytes=VMEM_BYTES),
        cost_estimate=pl.CostEstimate(flops=flops, bytes_accessed=moved, transcendentals=0),
        **more,
    )(*operands)


def mixer_kernel(q_ref, k_ref, v_ref, decay_ref, logit_ref, c_ref, b_ref, inside_ref, reach_ref):
    length = q_ref.shape[0]
    heads = decay_ref.shape[0]
    ratio = heads // (q_ref.shape[1] // DK)
    row = lax.broadcasted_iota(jnp.int32, (length, length), 0)
    col = lax.broadcasted_iota(jnp.int32, (length, length), 1)
    on = row >= col
    below = row > col
    eye = jnp.where(row == col, 1.0, 0.0)
    tri = jnp.where(on, 1.0, 0.0)
    rate_row = 1.0 / (1.0 + jnp.exp(-logit_ref[...]))
    log_row = -exact(decay_ref[...], tri, NT)
    log_col = -exact(tri, decay_ref[...], NT)
    rate_col = exact(eye, rate_row, NT)
    ones = jnp.ones((8, DK), F32)
    systems, weights, scales = [], [], []
    for group in range(heads // ratio):
        part = slice(group * DK, (group + 1) * DK)
        query = q_ref[:, part]
        key = k_ref[:, part]
        query_f = query.astype(F32)
        key_f = key.astype(F32)
        query_scale = lax.rsqrt(jnp.sum(query_f * query_f, axis=1, keepdims=True) + EPS) * DK**-0.5
        key_scale = lax.rsqrt(jnp.sum(key_f * key_f, axis=1, keepdims=True) + EPS)
        key_scale_row = lax.rsqrt(exact(ones, key_f * key_f, NT)[:1] + EPS)
        key_key = mm(key, key, NT) * (key_scale * key_scale_row)
        query_key = mm(query, key, NT) * (query_scale * key_scale_row)
        for head in range(group * ratio, (group + 1) * ratio):
            apart = jnp.where(on, log_col[:, head : head + 1] - log_row[head : head + 1, :], 0.0)
            fading = jnp.where(on, jnp.exp(apart), 0.0) * rate_row[head : head + 1, :]
            systems.append(jnp.where(below, key_key * fading, 0.0))
            weights.append(query_key * fading)
            scales.append((query_f * query_scale, key_f * key_scale, key_scale, key))
    inverses = [eye - jnp.where(row // 2 == col // 2, system, 0.0) for system in systems]
    size = 2
    while size < length:
        lower = (row // (2 * size) == col // (2 * size)) & (row // size > col // size)
        crossing = [
            mm(jnp.where(lower, system, 0.0), inverse)
            for system, inverse in zip(systems, inverses)
        ]
        inverses = [
            inverse - mm(inverse, cross) for inverse, cross in zip(inverses, crossing)
        ]
        size *= 2
    for head in range(heads):
        query_n, key_n, key_scale, key = scales[head]
        lead = jnp.exp(log_col[:, head : head + 1])
        value = v_ref[:, head * DV : (head + 1) * DV].astype(F32)
        target = jnp.concatenate([value, lead * key_n], axis=1)
        solved = mm(inverses[head], target)
        missing = target - solved - mm3(systems[head], solved)
        solved = solved + mm(inverses[head], missing)
        both = mm3(weights[head], solved)
        inside_ref[head] = both[:, :DV]
        reach_ref[head] = (lead * query_n - both[:, DV:]).astype(reach_ref.dtype)
        last = log_col[length - 1 : length, head : head + 1]
        tail = jnp.exp(last - log_col[:, head : head + 1]) * rate_col[:, head : head + 1] * key_scale
        high, low = halves(solved * tail)
        written = mm(high, key, TN) + mm(low, key, TN)
        c_ref[head] = written[DV:].astype(c_ref.dtype)
        b_ref[head] = written[:DV].astype(b_ref.dtype)


def scan_kernel(got_ref, enter_ref):
    blocks = got_ref.shape[0]
    rows = enter_ref.shape[1]
    state = jnp.zeros((rows, DK), F32)
    for block in range(blocks):
        enter_ref[block] = state.astype(BF)
        if block == blocks - 1:
            break
        removed = got_ref[block, :DK, :]
        added = got_ref[block, DK : DK + rows, :].astype(F32)
        marks = got_ref[block, DK + rows : DK + 2 * rows, :].astype(F32)
        fade = marks[0:1, :] + marks[1:2, :] + marks[2:3, :]
        high, low = halves(state)
        state = fade * state - (mm(high, removed) + mm(low, removed)) + added


def output_kernel(inside_ref, reach_ref, state_ref, gate_ref, gain_ref, proj_ref, out_ref):
    heads = inside_ref.shape[0]
    gated = []
    for head in range(heads):
        part = slice(head * DV, (head + 1) * DV)
        output = inside_ref[head] + mm(reach_ref[head], state_ref[head], NT)
        scaling = lax.rsqrt(jnp.mean(output * output, axis=1, keepdims=True) + EPS)
        opened = silu(gate_ref[:, part].astype(F32))
        gated.append((output * scaling * gain_ref[...] * opened).astype(BF))
    mixed = mm(jnp.concatenate(gated, axis=1), proj_ref[...])
    width = out_ref.shape[2]
    for share in range(out_ref.shape[0]):
        out_ref[share] = mixed[:, share * width : (share + 1) * width].astype(out_ref.dtype)


def route_kernel(ids_ref, ids_t_ref, weight_ref, pick_ref, mix_ref):
    blocks, length, top = ids_ref.shape
    slots = pick_ref.shape[1]
    targets = slots // SLOTS
    iota = lambda shape, dim: lax.broadcasted_iota(jnp.int32, shape, dim)
    earlier = (iota((length, length), 0) > iota((length, length), 1)).astype(BF)
    earlier_t = (iota((length, length), 0) < iota((length, length), 1)).astype(BF)
    spread = (iota((targets, slots), 1) // SLOTS == iota((targets, slots), 0)).astype(BF)
    spread_t = (iota((slots, targets), 0) // SLOTS == iota((slots, targets), 1)).astype(BF)
    number = iota((length, targets), 1)
    number_t = iota((targets, length), 0)
    slot = (iota((length, slots), 1) % SLOTS).astype(F32)
    slot_t = (iota((slots, length), 0) % SLOTS).astype(F32)

    def one(block, _):
        ids = ids_ref[block]
        ids_t = ids_t_ref[block]
        weight = weight_ref[block]
        named = jnp.zeros((length, targets), F32)
        wide = jnp.zeros((length, targets), F32)
        named_t = jnp.zeros((targets, length), F32)
        for choice in range(top):
            hit = ids[:, choice : choice + 1] == number
            named = named + jnp.where(hit, 1.0, 0.0)
            wide = wide + jnp.where(hit, weight[:, choice : choice + 1], 0.0)
            named_t = named_t + jnp.where(ids_t[choice : choice + 1, :] == number_t, 1.0, 0.0)
        place = jnp.where(named > 0.0, mm(earlier, named), -1.0)
        place_t = jnp.where(named_t > 0.0, mm(named_t, earlier_t), -1.0)
        mix_ref[block] = jnp.where(mm(place, spread) == slot, mm(wide, spread), 0.0).astype(BF)
        pick_ref[block] = jnp.where(mm(spread_t, place_t) == slot_t, 1.0, 0.0).astype(BF)
        return 0

    lax.fori_loop(0, blocks, one, 0)


def pick_kernel(pick_ref, token_ref, send_ref):
    targets = send_ref.shape[0]
    width = send_ref.shape[2]
    for block in range(pick_ref.shape[0]):
        rows = mm(pick_ref[block], token_ref[block]).astype(BF)
        send_ref[:, block * SLOTS : (block + 1) * SLOTS, :] = rows.reshape(targets, SLOTS, width)


def expert_kernel(rows_ref, gain_ref, gate_ref, up_ref, down_ref, out_ref, normed_ref):
    groups, shares, count, width = rows_ref.shape
    for group in range(groups):
        place = slice(group * count, (group + 1) * count)
        total = jnp.zeros((count, 1), F32)
        for share in range(shares):
            piece = rows_ref[group, share].astype(F32)
            total = total + jnp.sum(piece * piece, axis=1, keepdims=True)
        scaling = lax.rsqrt(total / (shares * width) + EPS)
        for share in range(shares):
            part = slice(share * width, (share + 1) * width)
            piece = rows_ref[group, share].astype(F32)
            normed_ref[place, part] = (piece * scaling * gain_ref[:, part]).astype(BF)
    normed = normed_ref[...]
    hidden = (silu(mm(normed, gate_ref[...])) * mm(normed, up_ref[...])).astype(BF)
    for share in range(shares):
        part = slice(share * width, (share + 1) * width)
        produced = mm(hidden, down_ref[:, part]).astype(BF)
        for group in range(groups):
            out_ref[group, share] = produced[group * count : (group + 1) * count]


def combine_kernel(mix_ref, rows_ref, out_ref):
    targets, _, width = rows_ref.shape
    for block in range(mix_ref.shape[0]):
        rows = rows_ref[:, block * SLOTS : (block + 1) * SLOTS, :].reshape(targets * SLOTS, width)
        out_ref[block] = mm(mix_ref[block], rows).astype(out_ref.dtype)


def swap(value, axes):
    return lax.all_to_all(value, axes, 0, 0, tiled=True)


def on_device(
    query_in,
    key_in,
    value_in,
    gate_in,
    decay_rate,
    beta_logit,
    head_gain,
    out_proj,
    residual_in,
    post_gain,
    expert_ids,
    route_weight,
    w_gate,
    w_up,
    w_down,
):
    length = query_in.shape[0]
    heads = decay_rate.shape[0]
    blocks = lax.axis_size("z")
    groups = lax.axis_size("x")
    shares = lax.axis_size("y") * lax.axis_size("c")
    share = lax.axis_index(("y", "c"))
    width = residual_in.shape[1] // shares
    count = blocks * SLOTS
    targets = groups * shares
    shape = jax.ShapeDtypeStruct

    all_ids = lax.all_gather(expert_ids, "z")
    all_weight = lax.all_gather(route_weight, "z")
    own = (all_ids // shares) % blocks == lax.axis_index("z")
    local_ids = jnp.where(own, (all_ids // (blocks * shares)) * shares + all_ids % shares, -1)
    pick, mix = call(
        route_kernel,
        (
            shape((blocks, targets * SLOTS, length), BF),
            shape((blocks, length, targets * SLOTS), BF),
        ),
        local_ids,
        jnp.swapaxes(local_ids, 1, 2),
        all_weight,
    )

    removed, added, inside, reach = call(
        mixer_kernel,
        (
            shape((heads, DK, DK), BF),
            shape((heads, DV, DK), BF),
            shape((heads, length, DV), F32),
            shape((heads, length, DK), BF),
        ),
        query_in,
        key_in,
        value_in,
        decay_rate,
        beta_logit,
    )
    ctx = groups * blocks
    cuts = ctx // heads
    rows = DV // cuts
    fade = jnp.exp(-jnp.sum(decay_rate, axis=1))
    first, second = halves(fade)
    third = (fade - first.astype(F32) - second.astype(F32)).astype(BF)
    marks = jnp.stack([first, second, third] + [jnp.zeros_like(first)] * (rows - 3), axis=1)
    marks = jnp.broadcast_to(marks[:, None, :, None], (heads, cuts, rows, DK))
    send = jnp.concatenate(
        [
            jnp.broadcast_to(removed[:, None], (heads, cuts, DK, DK)),
            added.reshape(heads, cuts, rows, DK),
            marks,
        ],
        axis=2,
    ).reshape(ctx, DK + 2 * rows, DK)
    got = swap(send, ("x", "z"))
    enter = call(scan_kernel, shape((ctx, rows, DK), BF), got)
    state = swap(enter, ("x", "z")).reshape(heads, DV, DK)

    partial = call(
        output_kernel,
        shape((shares, length, width), BF),
        inside,
        reach,
        state,
        gate_in,
        head_gain.reshape(1, DV),
        out_proj,
    )
    mixed = jnp.sum(swap(partial, ("y", "c")).astype(F32), axis=0)
    residual = lax.dynamic_slice_in_dim(residual_in, share * width, width, 1)
    middle = (residual.astype(F32) + mixed).astype(BF)

    tokens = lax.all_gather(middle, "z")
    send = call(pick_kernel, shape((targets, count, width), BF), pick, tokens)
    arrived = swap(send, ("x", "y", "c")).reshape(groups, shares, count, width)
    produced = call(
        expert_kernel,
        shape((groups, shares, count, width), BF),
        arrived,
        post_gain.reshape(1, -1),
        w_gate[0],
        w_up[0],
        w_down[0],
        scratch_shapes=[pltpu.VMEM((groups * count, shares * width), BF)],
    )
    returned = swap(produced.reshape(targets, count, width), ("x", "y", "c"))
    mixes = call(combine_kernel, shape((blocks, length, width), BF), mix, returned)
    expert_mix = jnp.sum(swap(mixes, "z").astype(F32), axis=0)
    layer_out = (middle.astype(F32) + expert_mix).astype(BF)
    return (middle, layer_out)


def solution(mesh):
    ctx, exp = mesh.devices.shape
    split = Mesh(mesh.devices.reshape(4, ctx // 4, exp // 2, 2), ("x", "z", "y", "c"))
    row, col = ("x", "z"), ("y", "c")
    in_specs = (
        P(row, col),
        P(row, col),
        P(row, col),
        P(row, col),
        P(col, row),
        P(col, row),
        P(),
        P(col, None),
        P(row, None),
        P(),
        P(row, None),
        P(row, None),
        P(row + col, None, None),
        P(row + col, None, None),
        P(row + col, None, None),
    )
    out_specs = (P(row, col), P(row, col))
    return jax.shard_map(
        on_device, mesh=split, in_specs=in_specs, out_specs=out_specs, check_vma=False
    )
```

time: 844 us -> 280 us (0.33)
  waiting for transfers between devices: 374 us -> 0.01 us
  blocking collectives: 0 us -> 227 us
  starting transfers between devices: 192 us -> 6.86 us
  local copies, waits for them, and re-layouts: 112 us -> 5.5 us
  other arithmetic: 93.6 us -> 4.32 us
  matrix products: 51.4 us -> 0 us
  Pallas kernels: 0 us -> 34.2 us
  between operations: 14.7 us -> 0.8 us
    all_to_all x0 -> x5, blocking collectives: none -> 169 us  [swap(): return lax.all_to_all(value, axes, 0, 0, tiled=True)]
    ppermute x31 -> x0, starting transfers between devices: 164 us -> none  [from_behind(): return lax.ppermute(block, axis, route)]
    psum x1 -> x0, waiting for transfers between devices: 124 us -> none  [on_device(): summed_all = lax.psum(mixed, 'exp')]
    ppermute x31 -> x0, waiting for transfers between devices: 120 us -> none  [from_behind(): return lax.ppermute(block, axis, route)]
    gather x28 -> x0, local copies, waits for them, and re-layouts: 97.9 us -> none  [the longest x2 23.1 us: slot_tables(): route_weight.reshape(-1)[pair_index]]
    all_to_all x3 -> x1, waiting for transfers between devices: 95.3 us -> 0.01 us  [swap(): return lax.all_to_all(value, axes, 0, 0, tiled=True)]
    another operation x6 -> x0, other arithmetic: 60.7 us -> none  [the longest x3 59.7 us: block_terms(): jax.scipy.linalg.solve_triangular(system, jnp.concatenate([values, leadin...]
    all_gather x0 -> x3, blocking collectives: none -> 57.7 us  [the longest x1 20.5 us: on_device(): tokens = lax.all_gather(middle, 'z')]
  transfers between devices with their start and end apart: 36 -> 1, of which waited for: 35 -> 0; matrix products, arithmetic and copies ran while one was open for 15% -> 0% of each run, Pallas kernels for 0% -> 3%
where the time goes in v1:
time: 280 us; the launch traced here: 279 us
  blocking collectives  227 us (81%)
  Pallas kernels  34.2 us (12%)
  starting transfers between devices  6.86 us (2%)
  local copies, waits for them, and re-layouts  5.5 us (2%)
  other arithmetic  4.32 us (2%)
    all_to_all x5, blocking collectives, swap(): return lax.all_to_all(value, axes, 0, 0, tiled=True)  169 us
    pallas_call x7, Pallas kernels, call(): pl.pallas_call(kernel, out_shape=out_shape, compiler_params=pltpu.Compile...  34.2 us
    all_gather x1, blocking collectives, on_device(): tokens = lax.all_gather(middle, 'z')  20.5 us
    all_gather x1, blocking collectives, on_device(): all_weight = lax.all_gather(route_weight, 'z')  19 us
    all_gather x1, blocking collectives, on_device(): all_ids = lax.all_gather(expert_ids, 'z')  18.2 us
    all_to_all x1, starting transfers between devices, swap(): return lax.all_to_all(value, axes, 0, 0, tiled=True)  6.86 us
  transfers between devices with their start and end apart: 1, of which 0 were waited for; matrix products, arithmetic and copies ran while one was open for 0% of the time, Pallas kernels for 3%

profile of v1, /device:TPU:1, one launch (start us, length us, event | category | flops | bytes accessed | tf_op | source)
XLA Modules:
  0.0 278.8 jit_solution(3865878113314955010)
XLA Ops:
  0.6 0.8 reduce_sum.27
  1.9 0.9 copy-done.2
  2.8 0.9 copy-done.3
  3.7 0.9 copy-done.4
  4.6 0.7 copy-done.5
  5.3 0.7 copy-done.7
  6.0 6.8 %shard_map.158 = (bf16[4,128,128]{2,1,0:T(8,128)(2,1)S(1)}, bf16[4,128,128]{2,1,0:T(8,128)(2,1)S(1)}, f32[4,192,128]{2,1,0:T(8,128)S(1)}, bf16[4,192,128]{2,1,0:T(8,128)(2,1)S(1)}) custom-call(bf16[192,256]{1,0:T(8,128)(2,1)S(1)} %copy-done.3, bf16[192,256]{1,0:T(8,128)(2,1)S(1)} %copy-done.4, bf16[192,512]{1,0:T(8,128)(2,1)S(1)} %copy-done.2, ...), custom_call_target="tpu_custom_call" | custom-call | tf_op jit(solution)/shard_map/pallas_call | solution.py:54
  13.4 44.3 %all_to_all.30.got_ref = bf16[32,160,128]{2,1,0:T(8,128)(2,1)S(1)} all-to-all(bf16[32,160,128]{2,1,0:T(8,128)(2,1)S(1)} %pad_maximum_fusion), channel_id=1, replica_groups=mesh['x'=4,'z'=8,'y'=4,'c'=2] {'x','z'}, dimensions={0} | all-to-all | bytes 2621440 | tf_op jit(solution)/shard_map/all_to_all | solution.py:231
  57.6 4.2 %shard_map.159 = bf16[32,16,128]{2,1,0:T(8,128)(2,1)S(1)} custom-call(bf16[32,160,128]{2,1,0:T(8,128)(2,1)S(1)} %all_to_all.30.got_ref), custom_call_target="tpu_custom_call" | custom-call | tf_op jit(solution)/shard_map/pallas_call | solution.py:54
  61.9 15.6 %all_to_all.31 = bf16[32,16,128]{2,1,0:T(8,128)(2,1)S(1)} all-to-all(bf16[32,16,128]{2,1,0:T(8,128)(2,1)S(1)} %shard_map.159), channel_id=1, replica_groups=mesh['x'=4,'z'=8,'y'=4,'c'=2] {'x','z'}, dimensions={0} | all-to-all | bytes 262144 | tf_op jit(solution)/shard_map/all_to_all | solution.py:231
  77.5 1.8 shard_map.160
  79.3 6.9 %all-to-all-start.2 = ((bf16[8,192,256]{2,1,0:T(8,128)(2,1)}), bf16[8,192,256]{2,1,0:T(8,128)(2,1)}, u32[]{:S(2)}, u32[]{:S(2)}) async-start(bf16[8,192,256]{2,1,0:T(8,128)(2,1)} %shard_map.160), calls=%async_computation.2 | async-start | bytes 1572864 | tf_op jit(solution)/shard_map/all_to_all | solution.py:231
  86.2 19.0 %all-gather.4 = f32[8,192,10]{1,2,0:T(8,128)S(1)} all-gather(f32[1,192,10]{1,2,0:T(8,128)S(1)} %bitcast.37), channel_id=3, replica_groups=mesh['x'=4,'z'=8,'y'=4,'c'=2] {'z'}, dimensions={0}, use_global_device_ids=true | all-gather | bytes 69120 | tf_op jit(solution)/shard_map/all_gather | solution.py:263
  105.5 18.2 %all-gather.3 = s32[8,192,10]{1,2,0:T(8,128)S(1)} all-gather(s32[1,192,10]{1,2,0:T(8,128)S(1)} %bitcast.38), channel_id=2, replica_groups=mesh['x'=4,'z'=8,'y'=4,'c'=2] {'z'}, dimensions={0}, use_global_device_ids=true | all-gather | bytes 69120 | tf_op jit(solution)/shard_map/all_gather | solution.py:262
  124.5 9.5 %shard_map.161 = (bf16[8,512,192]{2,1,0:T(8,128)(2,1)}, bf16[8,192,512]{2,1,0:T(8,128)(2,1)S(1)}) custom-call(s32[8,192,10]{2,1,0:T(8,128)S(1)} %copy.25.ids_ref, s32[8,10,192]{2,1,0:T(8,128)S(1)} %fusion.11.ids_t_ref, f32[8,192,10]{2,1,0:T(8,128)S(1)} %copy.26.weight_ref), custom_call_target="tpu_custom_call" | custom-call | tf_op jit(solution)/shard_map/pallas_call | solution.py:54
  134.0 1.3 convert_reduce_fusion.1
  135.2 0.9 add_convert_fusion.1
  136.2 20.5 %all-gather.2 = bf16[1536,256]{1,0:T(8,128)(2,1)S(1)} all-gather(bf16[192,256]{1,0:T(8,128)(2,1)S(1)} %add_convert_fusion.1), channel_id=4, replica_groups=mesh['x'=4,'z'=8,'y'=4,'c'=2] {'z'}, dimensions={0}, use_global_device_ids=true | all-gather | bytes 884736 | tf_op jit(solution)/shard_map/all_gather | solution.py:325
  156.6 2.3 shard_map.162
  159.0 51.0 %all_to_all.32 = bf16[32,128,256]{2,1,0:T(8,128)(2,1)} all-to-all(bf16[32,128,256]{2,1,0:T(8,128)(2,1)S(1)} %shard_map.162), channel_id=1, replica_groups=mesh['x'=4,'z'=8,'y'=4,'c'=2] {'x','y','c'}, dimensions={0} | all-to-all | bytes 4194304 | tf_op jit(solution)/shard_map/all_to_all | solution.py:231
  210.0 7.4 %shard_map.163 = bf16[4,8,128,256]{3,2,1,0:T(8,128)(2,1)S(1)} custom-call(bf16[4,8,128,256]{3,2,1,0:T(8,128)(2,1)} %bitcast.32, f32[1,2048]{1,0:T(1,128)S(1)} %bitcast.30, bf16[2048,512]{1,0:T(8,128)(2,1)} %bitcast.34, bf16[2048,512]{1,0:T(8,128)(2,1)} %bitcast.35, bf16[512,2048]{1,0:T(8,128)(2,1)} %bitcast.36), custom_call_target="tpu_custom_call" | custom-call | tf_op jit(solution)/shard_map/pallas_call | solution.py:54
  217.4 32.0 %all_to_all.33.rows_ref = bf16[32,128,256]{2,1,0:T(8,128)(2,1)} all-to-all(bf16[32,128,256]{2,1,0:T(8,128)(2,1)S(1)} %bitcast.26), channel_id=1, replica_groups=mesh['x'=4,'z'=8,'y'=4,'c'=2] {'x','y','c'}, dimensions={0} | all-to-all | bytes 4194304 | tf_op jit(solution)/shard_map/all_to_all | solution.py:231
  249.4 2.2 shard_map.164
  251.6 26.4 %all_to_all.34 = bf16[8,192,256]{2,1,0:T(8,128)(2,1)S(1)} all-to-all(bf16[8,192,256]{2,1,0:T(8,128)(2,1)S(1)} %shard_map.164), channel_id=1, replica_groups=mesh['x'=4,'z'=8,'y'=4,'c'=2] {'z'}, dimensions={0} | all-to-all | bytes 1572864 | tf_op jit(solution)/shard_map/all_to_all | solution.py:231
  (39 shorter events, 2.8 us)
Async XLA Ops:
  1.9 0.9 copy-start.2
  2.8 0.9 copy-start.3
  3.7 0.9 copy-start.4
  4.6 0.7 copy-start.5
  5.3 0.7 copy-start.7
  13.3 64.2 %copy-start = (bf16[512,2048]{1,0:T(8,128)(2,1)S(1)}, bf16[512,2048]{1,0:T(8,128)(2,1)}, u32[]{:S(2)}) copy-start(bf16[512,2048]{1,0:T(8,128)(2,1)} %proj_ref.1) | copy-start | bytes 6291460
  13.3 64.2 %copy-start.1 = (bf16[192,512]{1,0:T(8,128)(2,1)S(1)}, bf16[192,512]{1,0:T(8,128)(2,1)}, u32[]{:S(2)}) copy-start(bf16[192,512]{1,0:T(8,128)(2,1)} %gate_ref.1) | copy-start | bytes 589828
  13.3 64.2 %copy-start.8 = (f32[128]{0:T(128)S(1)}, f32[128]{0:T(128)}, u32[]{:S(2)}) copy-start(f32[128]{0:T(128)} %param.21) | copy-start | bytes 1540
  77.5 8.7 %copy-start.10 = (f32[192,10]{0,1:T(8,128)S(1)}, f32[192,10]{0,1:T(8,128)}, u32[]{:S(2)}) copy-start(f32[192,10]{0,1:T(8,128)} %param.26) | copy-start | bytes 23044
  79.3 26.2 %copy-start.11 = (s32[192,10]{0,1:T(8,128)S(1)}, s32[192,10]{0,1:T(8,128)}, u32[]{:S(2)}) copy-start(s32[192,10]{0,1:T(8,128)} %param.25) | copy-start | bytes 23044
  79.3 54.7 %all-to-all-start.2 = ((bf16[8,192,256]{2,1,0:T(8,128)(2,1)}), bf16[8,192,256]{2,1,0:T(8,128)(2,1)}, u32[]{:S(2)}, u32[]{:S(2)}) async-start(bf16[8,192,256]{2,1,0:T(8,128)(2,1)} %shard_map.160), calls=%async_computation.2 | async-start | bytes 1572864 | tf_op jit(solution)/shard_map/all_to_all | solution.py:231
  136.1 142.0 %copy-start.9 = (bf16[192,256]{1,0:T(8,128)(2,1)}, bf16[192,256]{1,0:T(8,128)(2,1)S(1)}, u32[]{:S(2)}) copy-start(bf16[192,256]{1,0:T(8,128)(2,1)S(1)} %add_convert_fusion.1) | copy-start | bytes 294916
  158.9 51.0 %copy-start.6 = (f32[2048]{0:T(1024)S(1)}, f32[2048]{0:T(1024)}, u32[]{:S(2)}) copy-start(f32[2048]{0:T(1024)} %param.24) | copy-start | bytes 24580

commit v2 on v1

--- a/solution.py
+++ b/solution.py
@@ -10,6 +10,9 @@
 DK = 128
 DV = 128
 SLOTS = 16
+MARKS = 16
+TARGETS = 32
+SHARES = 8
 EPS = 1e-06
 BF = jnp.bfloat16
 F32 = jnp.float32
@@ -44,6 +47,28 @@
         + mm(left_high, right_low, dims)
         + mm(left_low, right_high, dims)
     )
+
+
+def pieces(value):
+    first, second = halves(value)
+    third = (value - first.astype(F32) - second.astype(F32)).astype(BF)
+    row = lax.broadcasted_iota(jnp.int32, value.shape, 0)
+    return jnp.where(row == 0, first, jnp.where(row == 1, second, third))
+
+
+def joined(marks):
+    marks = marks.astype(F32)
+    return marks[0:1] + marks[1:2] + marks[2:3]
+
+
+def unpack(got, rows):
+    fade = joined(got[DK + rows : DK + rows + MARKS, :])
+    return got[:DK, :], got[DK : DK + rows, :].astype(F32), fade
+
+
+def advance(state, removed, fade):
+    high, low = halves(state)
+    return fade * state - (mm(high, removed) + mm(low, removed))
 
 
 def silu(value):
@@ -60,10 +85,17 @@
     )(*operands)
 
 
-def mixer_kernel(q_ref, k_ref, v_ref, decay_ref, logit_ref, c_ref, b_ref, inside_ref, reach_ref):
+def mixer_kernel(
+    q_ref, k_ref, v_ref, decay_ref, logit_ref, ids_ref, weight_ref, send_ref, inside_ref, reach_ref
+):
     length = q_ref.shape[0]
     heads = decay_ref.shape[0]
     ratio = heads // (q_ref.shape[1] // DK)
+    places = send_ref.shape[0]
+    cuts = places // heads
+    rows = DV // cuts
+    targets = TARGETS
+    shares = SHARES
     row = lax.broadcasted_iota(jnp.int32, (length, length), 0)
     col = lax.broadcasted_iota(jnp.int32, (length, length), 1)
     on = row >= col
@@ -120,24 +152,63 @@
         tail = jnp.exp(last - log_col[:, head : head + 1]) * rate_col[:, head : head + 1] * key_scale
         high, low = halves(solved * tail)
         written = mm(high, key, TN) + mm(low, key, TN)
-        c_ref[head] = written[DV:].astype(c_ref.dtype)
-        b_ref[head] = written[:DV].astype(b_ref.dtype)
-
-
-def scan_kernel(got_ref, enter_ref):
+        removed = written[DV:].astype(BF)
+        added = written[:DV].astype(BF)
+        fade = pieces(jnp.broadcast_to(jnp.exp(last), (MARKS, DK)))
+        for cut in range(cuts):
+            place = head * cuts + cut
+            send_ref[place, :DK, :] = removed
+            send_ref[place, DK : DK + rows, :] = added[cut * rows : (cut + 1) * rows]
+            send_ref[place, DK + rows : DK + rows + MARKS, :] = fade
+    base = DK + rows + MARKS
+    number = lax.broadcasted_iota(jnp.int32, (targets, length), 0)
+    number = (number // shares) * (places * shares) + number % shares
+    for place in range(places):
+        weight = jnp.zeros((targets, length), F32)
+        for choice in range(ids_ref.shape[0]):
+            hit = ids_ref[choice : choice + 1, :] == number + place * shares
+            weight = weight + jnp.where(hit, weight_ref[choice : choice + 1, :], 0.0)
+        weight = weight.astype(BF)
+        send_ref[place, base : base + targets, :] = weight[:, :DK]
+        send_ref[place, base + targets :, :] = jnp.concatenate(
+            [weight[: targets // 2, DK:], weight[targets // 2 :, DK:]], axis=1
+        )
+
+
+def total_kernel(got_ref, total_ref):
     blocks = got_ref.shape[0]
-    rows = enter_ref.shape[1]
+    rows = total_ref.shape[0] - DK - MARKS
+    row = lax.broadcasted_iota(jnp.int32, (DK, DK), 0)
+    col = lax.broadcasted_iota(jnp.int32, (DK, DK), 1)
+    eye = jnp.where(row == col, 1.0, 0.0)
+    whole = jnp.ones((1, DK), F32)
+    product = eye
     state = jnp.zeros((rows, DK), F32)
     for block in range(blocks):
+        removed, added, fade = unpack(got_ref[block], rows)
+        if block == 0:
+            product = fade * eye - removed.astype(F32)
+            state = added
+        else:
+            product = advance(product, removed, fade)
+            state = advance(state, removed, fade) + added
+        whole = whole * fade
+    total_ref[:DK, :] = (whole * eye - product).astype(BF)
+    total_ref[DK : DK + rows, :] = state.astype(BF)
+    total_ref[DK + rows :, :] = pieces(jnp.broadcast_to(whole, (MARKS, DK)))
+
+
+def state_kernel(here_ref, total_ref, got_ref, enter_ref):
+    blocks, rows, _ = enter_ref.shape
+    state = jnp.zeros((rows, DK), F32)
+    for group in range(total_ref.shape[0] - 1):
+        removed, added, fade = unpack(total_ref[group], rows)
+        state = jnp.where(group < here_ref[0], advance(state, removed, fade) + added, state)
+    for block in range(blocks):
         enter_ref[block] = state.astype(BF)
-        if block == blocks - 1:
-            break
-        removed = got_ref[block, :DK, :]
-        added = got_ref[block, DK : DK + rows, :].astype(F32)
-        marks = got_ref[block, DK + rows : DK + 2 * rows, :].astype(F32)
-        fade = marks[0:1, :] + marks[1:2, :] + marks[2:3, :]
-        high, low = halves(state)
-        state = fade * state - (mm(high, removed) + mm(low, removed)) + added
+        if block < blocks - 1:
+            removed, added, fade = unpack(got_ref[block], rows)
+            state = advance(state, removed, fade) + added
 
 
 def output_kernel(inside_ref, reach_ref, state_ref, gate_ref, gain_ref, proj_ref, out_ref):
@@ -155,39 +226,31 @@
         out_ref[share] = mixed[:, share * width : (share + 1) * width].astype(out_ref.dtype)
 
 
-def route_kernel(ids_ref, ids_t_ref, weight_ref, pick_ref, mix_ref):
-    blocks, length, top = ids_ref.shape
-    slots = pick_ref.shape[1]
+def route_kernel(got_ref, pick_ref, mix_ref):
+    blocks, slots, length = pick_ref.shape
     targets = slots // SLOTS
+    base = got_ref.shape[1] - targets - targets // 2
     iota = lambda shape, dim: lax.broadcasted_iota(jnp.int32, shape, dim)
     earlier = (iota((length, length), 0) > iota((length, length), 1)).astype(BF)
     earlier_t = (iota((length, length), 0) < iota((length, length), 1)).astype(BF)
+    eye = (iota((length, length), 0) == iota((length, length), 1)).astype(BF)
     spread = (iota((targets, slots), 1) // SLOTS == iota((targets, slots), 0)).astype(BF)
     spread_t = (iota((slots, targets), 0) // SLOTS == iota((slots, targets), 1)).astype(BF)
-    number = iota((length, targets), 1)
-    number_t = iota((targets, length), 0)
     slot = (iota((length, slots), 1) % SLOTS).astype(F32)
     slot_t = (iota((slots, length), 0) % SLOTS).astype(F32)
-
-    def one(block, _):
-        ids = ids_ref[block]
-        ids_t = ids_t_ref[block]
-        weight = weight_ref[block]
-        named = jnp.zeros((length, targets), F32)
-        wide = jnp.zeros((length, targets), F32)
-        named_t = jnp.zeros((targets, length), F32)
-        for choice in range(top):
-            hit = ids[:, choice : choice + 1] == number
-            named = named + jnp.where(hit, 1.0, 0.0)
-            wide = wide + jnp.where(hit, weight[:, choice : choice + 1], 0.0)
-            named_t = named_t + jnp.where(ids_t[choice : choice + 1, :] == number_t, 1.0, 0.0)
-        place = jnp.where(named > 0.0, mm(earlier, named), -1.0)
-        place_t = jnp.where(named_t > 0.0, mm(named_t, earlier_t), -1.0)
-        mix_ref[block] = jnp.where(mm(place, spread) == slot, mm(wide, spread), 0.0).astype(BF)
+    for block in range(blocks):
+        first = got_ref[block, base : base + targets, :]
+        last = got_ref[block, base + targets :, :]
+        rest = length - DK
+        last = jnp.concatenate([last[:, :rest], last[:, rest:]], axis=0)
+        weight_t = jnp.concatenate([first, last], axis=1)
+        named_t = weight_t.astype(F32) > 0.0
+        weight = mm(eye, weight_t, NT)
+        named = weight > 0.0
+        place = jnp.where(named, mm(earlier, jnp.where(named, 1.0, 0.0)), -1.0)
+        place_t = jnp.where(named_t, mm(jnp.where(named_t, 1.0, 0.0), earlier_t), -1.0)
+        mix_ref[block] = jnp.where(mm(place, spread) == slot, mm(weight, spread), 0.0).astype(BF)
         pick_ref[block] = jnp.where(mm(spread_t, place_t) == slot_t, 1.0, 0.0).astype(BF)
-        return 0
-
-    lax.fori_loop(0, blocks, one, 0)
 
 
 def pick_kernel(pick_ref, token_ref, send_ref):
@@ -259,26 +322,12 @@
     targets = groups * shares
     shape = jax.ShapeDtypeStruct
 
-    all_ids = lax.all_gather(expert_ids, "z")
-    all_weight = lax.all_gather(route_weight, "z")
-    own = (all_ids // shares) % blocks == lax.axis_index("z")
-    local_ids = jnp.where(own, (all_ids // (blocks * shares)) * shares + all_ids % shares, -1)
-    pick, mix = call(
-        route_kernel,
-        (
-            shape((blocks, targets * SLOTS, length), BF),
-            shape((blocks, length, targets * SLOTS), BF),
-        ),
-        local_ids,
-        jnp.swapaxes(local_ids, 1, 2),
-        all_weight,
-    )
-
-    removed, added, inside, reach = call(
+    rows = heads * DV // blocks
+    packed = DK + rows + MARKS + targets + targets // 2
+    send, inside, reach = call(
         mixer_kernel,
         (
-            shape((heads, DK, DK), BF),
-            shape((heads, DV, DK), BF),
+            shape((blocks, packed, DK), BF),
             shape((heads, length, DV), F32),
             shape((heads, length, DK), BF),
         ),
@@ -287,26 +336,30 @@
         value_in,
         decay_rate,
         beta_logit,
-    )
-    ctx = groups * blocks
-    cuts = ctx // heads
-    rows = DV // cuts
-    fade = jnp.exp(-jnp.sum(decay_rate, axis=1))
-    first, second = halves(fade)
-    third = (fade - first.astype(F32) - second.astype(F32)).astype(BF)
-    marks = jnp.stack([first, second, third] + [jnp.zeros_like(first)] * (rows - 3), axis=1)
-    marks = jnp.broadcast_to(marks[:, None, :, None], (heads, cuts, rows, DK))
-    send = jnp.concatenate(
-        [
-            jnp.broadcast_to(removed[:, None], (heads, cuts, DK, DK)),
-            added.reshape(heads, cuts, rows, DK),
-            marks,
-        ],
-        axis=2,
-    ).reshape(ctx, DK + 2 * rows, DK)
-    got = swap(send, ("x", "z"))
-    enter = call(scan_kernel, shape((ctx, rows, DK), BF), got)
-    state = swap(enter, ("x", "z")).reshape(heads, DV, DK)
+        expert_ids.T,
+        route_weight.T,
+    )
+    got = swap(send, "z")
+    total = call(total_kernel, shape((DK + rows + MARKS, DK), BF), got)
+    totals = swap(jnp.broadcast_to(total, (groups,) + total.shape), "x")
+    pick, mix = call(
+        route_kernel,
+        (
+            shape((blocks, targets * SLOTS, length), BF),
+            shape((blocks, length, targets * SLOTS), BF),
+        ),
+        got,
+    )
+    enter = call(
+        state_kernel,
+        shape((blocks, rows, DK), BF),
+        lax.axis_index("x").reshape(1),
+        totals,
+        got,
+        in_specs=[pl.BlockSpec(memory_space=pltpu.SMEM)]
+        + [pl.BlockSpec(memory_space=pltpu.VMEM)] * 2,
+    )
+    state = swap(enter, "z").reshape(heads, DV, DK)
 
     partial = call(
         output_kernel,

time: 280 us -> 217 us (0.78)
  blocking collectives: 227 us -> 152 us
  waiting for transfers between devices: 0.01 us -> 12.6 us
  starting transfers between devices: 6.86 us -> 13.5 us
  Pallas kernels: 34.2 us -> 28.1 us
    all_to_all x5, blocking collectives: 169 us -> 131 us  [swap(): return lax.all_to_all(value, axes, 0, 0, tiled=True)]
    all_gather x2 -> x0, blocking collectives: 37.2 us -> none  [the longest x1 19 us: on_device(): all_weight = lax.all_gather(route_weight, 'z')]
    all_to_all x1 -> x2, waiting for transfers between devices: 0.01 us -> 12.6 us  [swap(): return lax.all_to_all(value, axes, 0, 0, tiled=True)]
    all_to_all x1 -> x2, starting transfers between devices: 6.86 us -> 13.5 us  [swap(): return lax.all_to_all(value, axes, 0, 0, tiled=True)]
    pallas_call x7 -> x8, Pallas kernels: 34.2 us -> 28.1 us  [call(): pl.pallas_call(kernel, out_shape=out_shape, compiler_params=pltpu.Compile...]
    unnamed x24 -> x28, local copies, waits for them, and re-layouts: 4.13 us -> 7.27 us
  transfers between devices with their start and end apart: 1 -> 2, of which waited for: 0 -> 2; matrix products, arithmetic and copies ran while one was open for 0% -> 0% of each run, Pallas kernels for 3% -> 2%
where the time goes in v2:
time: 217 us; the launch traced here: 216 us
  blocking collectives  152 us (70%)
  Pallas kernels  28.1 us (13%)
  starting transfers between devices  13.5 us (6%)
  waiting for transfers between devices  12.6 us (6%)
  local copies, waits for them, and re-layouts  7.99 us (4%)
    all_to_all x5, blocking collectives, swap(): return lax.all_to_all(value, axes, 0, 0, tiled=True)  131 us
    pallas_call x8, Pallas kernels, call(): pl.pallas_call(kernel, out_shape=out_shape, compiler_params=pltpu.Compile...  28.1 us
    all_gather x1, blocking collectives, on_device(): tokens = lax.all_gather(middle, 'z')  20.7 us
    all_to_all x2, starting transfers between devices, swap(): return lax.all_to_all(value, axes, 0, 0, tiled=True)  13.5 us
    all_to_all x2, waiting for transfers between devices, swap(): return lax.all_to_all(value, axes, 0, 0, tiled=True)  12.6 us
    unnamed x28, local copies, waits for them, and re-layouts  7.27 us
  transfers between devices with their start and end apart: 2, of which 2 were waited for; matrix products, arithmetic and copies ran while one was open for 0% of the time, Pallas kernels for 2%

profile of v2, /device:TPU:1, one launch (start us, length us, event | category | flops | bytes accessed | tf_op | source)
XLA Modules:
  0.0 216.5 jit_solution(10443401582843827394)
XLA Ops:
  0.7 1.1 copy-done.4
  1.7 0.9 copy-done.5
  2.6 0.9 copy-done.6
  3.5 0.7 copy-done.7
  6.3 7.0 %shard_map.158 = (bf16[8,256,128]{2,1,0:T(8,128)(2,1)S(1)}, f32[4,192,128]{2,1,0:T(8,128)S(1)}, bf16[4,192,128]{2,1,0:T(8,128)(2,1)S(1)}) custom-call(bf16[192,256]{1,0:T(8,128)(2,1)S(1)} %copy-done.5, bf16[192,256]{1,0:T(8,128)(2,1)S(1)} %copy-done.6, bf16[192,512]{1,0:T(8,128)(2,1)S(1)} %copy-done.4, f32[4,192]{1,0:T(4,128)S(1)} %copy-done.10, ...), custom_call_target="tpu_custom_call" | custom-call | tf_op jit(solution)/shard_map/pallas_call | solution.py:79
  14.0 24.8 %all_to_all.35.got_ref = bf16[8,256,128]{2,1,0:T(8,128)(2,1)S(1)} all-to-all(bf16[8,256,128]{2,1,0:T(8,128)(2,1)S(1)} %get-tuple-element.9), channel_id=1, replica_groups=mesh['x'=4,'z'=8,'y'=4,'c'=2] {'z'}, dimensions={0} | all-to-all | bytes 1048576 | tf_op jit(solution)/shard_map/all_to_all | solution.py:294
  38.8 1.1 shard_map.159
  40.6 4.0 %all-to-all-start.1 = ((bf16[4,208,128]{2,1,0:T(8,128)(2,1)}), bf16[4,208,128]{2,1,0:T(8,128)(2,1)S(1)}, u32[]{:S(2)}, u32[]{:S(2)}) async-start(bf16[4,208,128]{2,1,0:T(8,128)(2,1)} %broadcast_in_dim.3), calls=%async_computation.1 | async-start | bytes 425984 | tf_op jit(solution)/shard_map/all_to_all | solution.py:294
  44.6 5.3 %all-to-all-done.1.total_ref = bf16[4,208,128]{2,1,0:T(8,128)(2,1)S(1)} async-done(((bf16[4,208,128]{2,1,0:T(8,128)(2,1)}), bf16[4,208,128]{2,1,0:T(8,128)(2,1)S(1)}, u32[]{:S(2)}, u32[]{:S(2)}) %all-to-all-start.1) | async-done | bytes 213024 | tf_op jit(solution)/shard_map/all_to_all | solution.py:294
  49.9 1.4 shard_map.160
  51.3 10.4 %all_to_all.36 = bf16[8,64,128]{2,1,0:T(8,128)(2,1)S(1)} all-to-all(bf16[8,64,128]{2,1,0:T(8,128)(2,1)S(1)} %shard_map.160), channel_id=1, replica_groups=mesh['x'=4,'z'=8,'y'=4,'c'=2] {'z'}, dimensions={0} | all-to-all | bytes 262144 | tf_op jit(solution)/shard_map/all_to_all | solution.py:294
  61.7 0.9 copy-done.3
  62.6 1.8 shard_map.161
  64.4 9.4 %all-to-all-start.3 = ((bf16[8,192,256]{2,1,0:T(8,128)(2,1)}), bf16[8,192,256]{2,1,0:T(8,128)(2,1)S(1)}, u32[]{:S(2)}, u32[]{:S(2)}) async-start(bf16[8,192,256]{2,1,0:T(8,128)(2,1)} %shard_map.161), calls=%async_computation.3 | async-start | bytes 1572864 | tf_op jit(solution)/shard_map/all_to_all | solution.py:294
  73.8 5.0 %shard_map.162 = (bf16[8,512,192]{2,1,0:T(8,128)(2,1)}, bf16[8,192,512]{2,1,0:T(8,128)(2,1)S(1)}) custom-call(bf16[8,256,128]{2,1,0:T(8,128)(2,1)S(1)} %all_to_all.35.got_ref), custom_call_target="tpu_custom_call" | custom-call | tf_op jit(solution)/shard_map/pallas_call | solution.py:79
  78.8 7.3 %all-to-all-done.3 = bf16[8,192,256]{2,1,0:T(8,128)(2,1)S(1)} async-done(((bf16[8,192,256]{2,1,0:T(8,128)(2,1)}), bf16[8,192,256]{2,1,0:T(8,128)(2,1)S(1)}, u32[]{:S(2)}, u32[]{:S(2)}) %all-to-all-start.3) | async-done | bytes 786464 | tf_op jit(solution)/shard_map/all_to_all | solution.py:294
  86.2 0.9 add_convert_fusion.1
  87.2 20.7 %all-gather = bf16[1536,256]{1,0:T(8,128)(2,1)S(1)} all-gather(bf16[192,256]{1,0:T(8,128)(2,1)S(1)} %add_convert_fusion.1), channel_id=2, replica_groups=mesh['x'=4,'z'=8,'y'=4,'c'=2] {'z'}, dimensions={0}, use_global_device_ids=true | all-gather | bytes 884736 | tf_op jit(solution)/shard_map/all_gather | solution.py:378
  107.9 2.3 %shard_map.163 = bf16[32,128,256]{2,1,0:T(8,128)(2,1)S(1)} custom-call(bf16[8,512,192]{2,1,0:T(8,128)(2,1)} %get-tuple-element.11.pick_ref, bf16[8,192,256]{2,1,0:T(8,128)(2,1)S(1)} %bitcast.13), custom_call_target="tpu_custom_call" | custom-call | tf_op jit(solution)/shard_map/pallas_call | solution.py:79
  110.2 37.9 %all_to_all.37 = bf16[32,128,256]{2,1,0:T(8,128)(2,1)} all-to-all(bf16[32,128,256]{2,1,0:T(8,128)(2,1)S(1)} %shard_map.163), channel_id=1, replica_groups=mesh['x'=4,'z'=8,'y'=4,'c'=2] {'x','y','c'}, dimensions={0} | all-to-all | bytes 4194304 | tf_op jit(solution)/shard_map/all_to_all | solution.py:294
  148.1 7.4 %shard_map.164 = bf16[4,8,128,256]{3,2,1,0:T(8,128)(2,1)S(1)} custom-call(bf16[4,8,128,256]{3,2,1,0:T(8,128)(2,1)} %bitcast.19, f32[1,2048]{1,0:T(1,128)S(1)} %bitcast.17, bf16[2048,512]{1,0:T(8,128)(2,1)} %bitcast.20, bf16[2048,512]{1,0:T(8,128)(2,1)} %bitcast.21, bf16[512,2048]{1,0:T(8,128)(2,1)} %bitcast.22), custom_call_target="tpu_custom_call" | custom-call | tf_op jit(solution)/shard_map/pallas_call | solution.py:79
  155.5 32.0 %all_to_all.38.rows_ref = bf16[32,128,256]{2,1,0:T(8,128)(2,1)} all-to-all(bf16[32,128,256]{2,1,0:T(8,128)(2,1)S(1)} %bitcast.12), channel_id=1, replica_groups=mesh['x'=4,'z'=8,'y'=4,'c'=2] {'x','y','c'}, dimensions={0} | all-to-all | bytes 4194304 | tf_op jit(solution)/shard_map/all_to_all | solution.py:294
  187.5 2.2 %shard_map.165 = bf16[8,192,256]{2,1,0:T(8,128)(2,1)S(1)} custom-call(bf16[8,192,512]{2,1,0:T(8,128)(2,1)S(1)} %get-tuple-element.10.mix_ref, bf16[32,128,256]{2,1,0:T(8,128)(2,1)} %all_to_all.38.rows_ref), custom_call_target="tpu_custom_call" | custom-call | tf_op jit(solution)/shard_map/pallas_call | solution.py:79
  189.7 26.0 %all_to_all.39 = bf16[8,192,256]{2,1,0:T(8,128)(2,1)S(1)} all-to-all(bf16[8,192,256]{2,1,0:T(8,128)(2,1)S(1)} %shard_map.165), channel_id=1, replica_groups=mesh['x'=4,'z'=8,'y'=4,'c'=2] {'z'}, dimensions={0} | all-to-all | bytes 1572864 | tf_op jit(solution)/shard_map/all_to_all | solution.py:294
  (27 shorter events, 4.4 us)
Async XLA Ops:
  0.6 61.0 %copy-start = (bf16[512,2048]{1,0:T(8,128)(2,1)S(1)}, bf16[512,2048]{1,0:T(8,128)(2,1)}, u32[]{:S(2)}) copy-start(bf16[512,2048]{1,0:T(8,128)(2,1)} %proj_ref.1) | copy-start | bytes 6291460
  0.6 61.0 %copy-start.1 = (bf16[192,512]{1,0:T(8,128)(2,1)S(1)}, bf16[192,512]{1,0:T(8,128)(2,1)}, u32[]{:S(2)}) copy-start(bf16[192,512]{1,0:T(8,128)(2,1)} %gate_ref.1) | copy-start | bytes 589828
  0.7 1.1 copy-start.4
  1.7 0.9 copy-start.5
  2.6 0.9 copy-start.6
  3.5 0.7 copy-start.7
  4.2 0.7 copy-start.8
  5.0 0.7 copy-start.10
  5.6 0.7 copy-start.11
  6.3 55.3 %copy-start.12 = (f32[128]{0:T(128)S(1)}, f32[128]{0:T(128)}, u32[]{:S(2)}) copy-start(f32[128]{0:T(128)} %param.21) | copy-start | bytes 1540
  13.3 0.7 copy-start.2
  40.6 9.3 %all-to-all-start.1 = ((bf16[4,208,128]{2,1,0:T(8,128)(2,1)}), bf16[4,208,128]{2,1,0:T(8,128)(2,1)S(1)}, u32[]{:S(2)}, u32[]{:S(2)}) async-start(bf16[4,208,128]{2,1,0:T(8,128)(2,1)} %broadcast_in_dim.3), calls=%async_computation.1 | async-start | bytes 425984 | tf_op jit(solution)/shard_map/all_to_all | solution.py:294
  61.7 0.9 copy-start.3
  64.4 21.7 %all-to-all-start.3 = ((bf16[8,192,256]{2,1,0:T(8,128)(2,1)}), bf16[8,192,256]{2,1,0:T(8,128)(2,1)S(1)}, u32[]{:S(2)}, u32[]{:S(2)}) async-start(bf16[8,192,256]{2,1,0:T(8,128)(2,1)} %shard_map.161), calls=%async_computation.3 | async-start | bytes 1572864 | tf_op jit(solution)/shard_map/all_to_all | solution.py:294
  87.1 128.7 %copy-start.13 = (bf16[192,256]{1,0:T(8,128)(2,1)}, bf16[192,256]{1,0:T(8,128)(2,1)S(1)}, u32[]{:S(2)}) copy-start(bf16[192,256]{1,0:T(8,128)(2,1)S(1)} %add_convert_fusion.1) | copy-start | bytes 294916
  110.2 37.9 %copy-start.9 = (f32[2048]{0:T(1024)S(1)}, f32[2048]{0:T(1024)}, u32[]{:S(2)}) copy-start(f32[2048]{0:T(1024)} %param.24) | copy-start | bytes 24580

commit v3 on v2

--- a/solution.py
+++ b/solution.py
@@ -19,7 +19,7 @@
 NN = ((1,), (0,))
 NT = ((1,), (1,))
 TN = ((0,), (0,))
-VMEM_BYTES = 50 * 1024 * 1024
+MIB = 1024 * 1024
 
 
 def mm(left, right, dims=NN):
@@ -75,19 +75,29 @@
     return value / (1.0 + jnp.exp(-value))
 
 
-def call(kernel, out_shape, *operands, flops=0, moved=0, **more):
+def call(kernel, out_shape, *operands, vmem, flops=0, moved=0, **more):
     return pl.pallas_call(
         kernel,
         out_shape=out_shape,
-        compiler_params=pltpu.CompilerParams(vmem_limit_bytes=VMEM_BYTES),
+        compiler_params=pltpu.CompilerParams(vmem_limit_bytes=vmem * MIB),
         cost_estimate=pl.CostEstimate(flops=flops, bytes_accessed=moved, transcendentals=0),
         **more,
     )(*operands)
 
 
-def mixer_kernel(
-    q_ref, k_ref, v_ref, decay_ref, logit_ref, ids_ref, weight_ref, send_ref, inside_ref, reach_ref
-):
+def mixer_kernel(*refs):
+    count = len(refs) // 2 - 2
+    sources, (send_ref, inside_ref, reach_ref) = refs[:count], refs[count : count + 3]
+    held, sems = refs[count + 3 : -1], refs[-1]
+    copies = [
+        pltpu.make_async_copy(source, target, sems.at[i])
+        for i, (source, target) in enumerate(zip(sources, held))
+    ]
+    for copy in copies:
+        copy.start()
+    for copy in copies:
+        copy.wait()
+    q_ref, k_ref, v_ref, decay_ref, logit_ref, ids_ref, weight_ref = held
     length = q_ref.shape[0]
     heads = decay_ref.shape[0]
     ratio = heads // (q_ref.shape[1] // DK)
@@ -198,12 +208,13 @@
     total_ref[DK + rows :, :] = pieces(jnp.broadcast_to(whole, (MARKS, DK)))
 
 
-def state_kernel(here_ref, total_ref, got_ref, enter_ref):
+def state_kernel(here_ref, got_ref, *rest):
+    totals, enter_ref = rest[:-1], rest[-1]
     blocks, rows, _ = enter_ref.shape
     state = jnp.zeros((rows, DK), F32)
-    for group in range(total_ref.shape[0] - 1):
-        removed, added, fade = unpack(total_ref[group], rows)
-        state = jnp.where(group < here_ref[0], advance(state, removed, fade) + added, state)
+    for distance in range(len(totals), 0, -1):
+        removed, added, fade = unpack(totals[distance - 1], rows)
+        state = jnp.where(distance <= here_ref[0], advance(state, removed, fade) + added, state)
     for block in range(blocks):
         enter_ref[block] = state.astype(BF)
         if block < blocks - 1:
@@ -211,7 +222,9 @@
             state = advance(state, removed, fade) + added
 
 
-def output_kernel(inside_ref, reach_ref, state_ref, gate_ref, gain_ref, proj_ref, out_ref):
+def output_kernel(
+    here_ref, inside_ref, reach_ref, state_ref, gate_ref, gain_ref, proj_ref, keep_ref, give_ref
+):
     heads = inside_ref.shape[0]
     gated = []
     for head in range(heads):
@@ -220,13 +233,17 @@
         scaling = lax.rsqrt(jnp.mean(output * output, axis=1, keepdims=True) + EPS)
         opened = silu(gate_ref[:, part].astype(F32))
         gated.append((output * scaling * gain_ref[...] * opened).astype(BF))
-    mixed = mm(jnp.concatenate(gated, axis=1), proj_ref[...])
-    width = out_ref.shape[2]
-    for share in range(out_ref.shape[0]):
-        out_ref[share] = mixed[:, share * width : (share + 1) * width].astype(out_ref.dtype)
-
-
-def route_kernel(got_ref, pick_ref, mix_ref):
+    gated = jnp.concatenate(gated, axis=1)
+    columns, _, width = keep_ref.shape
+    for distance in range(columns):
+        column = lax.rem(here_ref[0] + distance, columns)
+        for core, out_ref in ((here_ref[1], keep_ref), (1 - here_ref[1], give_ref)):
+            first = pl.multiple_of((column * 2 + core) * width, width)
+            mixed = mm(gated, proj_ref[:, pl.ds(first, width)])
+            out_ref[distance] = mixed.astype(out_ref.dtype)
+
+
+def route_kernel(here_ref, got_ref, pick_ref, mix_ref):
     blocks, slots, length = pick_ref.shape
     targets = slots // SLOTS
     base = got_ref.shape[1] - targets - targets // 2
@@ -239,8 +256,9 @@
     slot = (iota((length, slots), 1) % SLOTS).astype(F32)
     slot_t = (iota((slots, length), 0) % SLOTS).astype(F32)
     for block in range(blocks):
-        first = got_ref[block, base : base + targets, :]
-        last = got_ref[block, base + targets :, :]
+        source = lax.rem(here_ref[0] + blocks - block, blocks)
+        first = got_ref[source, base : base + targets, :]
+        last = got_ref[source, base + targets :, :]
         rest = length - DK
         last = jnp.concatenate([last[:, :rest], last[:, rest:]], axis=0)
         weight_t = jnp.concatenate([first, last], axis=1)
@@ -253,11 +271,12 @@
         pick_ref[block] = jnp.where(mm(spread_t, place_t) == slot_t, 1.0, 0.0).astype(BF)
 
 
-def pick_kernel(pick_ref, token_ref, send_ref):
+def pick_kernel(pick_ref, *rest):
+    tokens, send_ref = rest[:-1], rest[-1]
     targets = send_ref.shape[0]
     width = send_ref.shape[2]
     for block in range(pick_ref.shape[0]):
-        rows = mm(pick_ref[block], token_ref[block]).astype(BF)
+        rows = mm(pick_ref[block], tokens[block][...]).astype(BF)
         send_ref[:, block * SLOTS : (block + 1) * SLOTS, :] = rows.reshape(targets, SLOTS, width)
 
 
@@ -283,11 +302,20 @@
             out_ref[group, share] = produced[group * count : (group + 1) * count]
 
 
-def combine_kernel(mix_ref, rows_ref, out_ref):
+def combine_kernel(mix_ref, rows_ref, *outs):
     targets, _, width = rows_ref.shape
     for block in range(mix_ref.shape[0]):
         rows = rows_ref[:, block * SLOTS : (block + 1) * SLOTS, :].reshape(targets * SLOTS, width)
-        out_ref[block] = mm(mix_ref[block], rows).astype(out_ref.dtype)
+        outs[block][...] = mm(mix_ref[block], rows).astype(outs[block].dtype)
+
+
+SCALAR = pl.BlockSpec(memory_space=pltpu.SMEM)
+VECTOR = pl.BlockSpec(memory_space=pltpu.VMEM)
+
+
+def shifted(value, axis, distance):
+    size = lax.axis_size(axis)
+    return lax.ppermute(value, axis, [(i, (i + distance) % size) for i in range(size)])
 
 
 def swap(value, axes):
@@ -324,6 +352,15 @@
 
     rows = heads * DV // blocks
     packed = DK + rows + MARKS + targets + targets // 2
+    operands = (
+        query_in,
+        key_in,
+        value_in,
+        decay_rate,
+        beta_logit,
+        expert_ids.T,
+        route_weight.T,
+    )
     send, inside, reach = call(
         mixer_kernel,
         (
@@ -331,52 +368,61 @@
             shape((heads, length, DV), F32),
             shape((heads, length, DK), BF),
         ),
-        query_in,
-        key_in,
-        value_in,
-        decay_rate,
-        beta_logit,
-        expert_ids.T,
-        route_weight.T,
+        *operands,
+        vmem=24,
+        in_specs=[pl.BlockSpec(memory_space=pl.ANY)] * len(operands),
+        scratch_shapes=[pltpu.VMEM(item.shape, item.dtype) for item in operands]
+        + [pltpu.SemaphoreType.DMA((len(operands),))],
     )
     got = swap(send, "z")
-    total = call(total_kernel, shape((DK + rows + MARKS, DK), BF), got)
-    totals = swap(jnp.broadcast_to(total, (groups,) + total.shape), "x")
+    total = call(total_kernel, shape((DK + rows + MARKS, DK), BF), got, vmem=8)
+    totals = [shifted(total, "x", distance) for distance in range(1, groups)]
     pick, mix = call(
         route_kernel,
         (
             shape((blocks, targets * SLOTS, length), BF),
             shape((blocks, length, targets * SLOTS), BF),
         ),
+        lax.axis_index("z").reshape(1),
         got,
+        vmem=12,
+        in_specs=[SCALAR, VECTOR],
     )
     enter = call(
         state_kernel,
         shape((blocks, rows, DK), BF),
         lax.axis_index("x").reshape(1),
-        totals,
         got,
-        in_specs=[pl.BlockSpec(memory_space=pltpu.SMEM)]
-        + [pl.BlockSpec(memory_space=pltpu.VMEM)] * 2,
+        *totals,
+        vmem=8,
+        in_specs=[SCALAR] + [VECTOR] * (1 + len(totals)),
     )
     state = swap(enter, "z").reshape(heads, DV, DK)
 
-    partial = call(
+    here = jnp.stack([lax.axis_index("y"), lax.axis_index("c")])
+    columns = lax.axis_size("y")
+    keep, give = call(
         output_kernel,
-        shape((shares, length, width), BF),
+        (shape((columns, length, width), F32), shape((columns, length, width), BF)),
+        here,
         inside,
         reach,
         state,
         gate_in,
         head_gain.reshape(1, DV),
         out_proj,
-    )
-    mixed = jnp.sum(swap(partial, ("y", "c")).astype(F32), axis=0)
+        vmem=16,
+        in_specs=[SCALAR] + [VECTOR] * 6,
+    )
+    both = keep + shifted(give, "c", 1).astype(F32)
+    mixed = both[0]
+    for distance in range(1, columns):
+        mixed = mixed + shifted(both[distance].astype(BF), "y", distance).astype(F32)
     residual = lax.dynamic_slice_in_dim(residual_in, share * width, width, 1)
     middle = (residual.astype(F32) + mixed).astype(BF)
 
-    tokens = lax.all_gather(middle, "z")
-    send = call(pick_kernel, shape((targets, count, width), BF), pick, tokens)
+    tokens = [middle] + [shifted(middle, "z", distance) for distance in range(1, blocks)]
+    send = call(pick_kernel, shape((targets, count, width), BF), pick, *tokens, vmem=12)
     arrived = swap(send, ("x", "y", "c")).reshape(groups, shares, count, width)
     produced = call(
         expert_kernel,
@@ -386,11 +432,20 @@
         w_gate[0],
         w_up[0],
         w_down[0],
+        vmem=24,
         scratch_shapes=[pltpu.VMEM((groups * count, shares * width), BF)],
     )
     returned = swap(produced.reshape(targets, count, width), ("x", "y", "c"))
-    mixes = call(combine_kernel, shape((blocks, length, width), BF), mix, returned)
-    expert_mix = jnp.sum(swap(mixes, "z").astype(F32), axis=0)
+    mixes = call(
+        combine_kernel,
+        (shape((length, width), F32),) + (shape((length, width), BF),) * (blocks - 1),
+        mix,
+        returned,
+        vmem=16,
+    )
+    expert_mix = mixes[0]
+    for distance in range(1, blocks):
+        expert_mix = expert_mix + shifted(mixes[distance], "z", -distance).astype(F32)
     layer_out = (middle.astype(F32) + expert_mix).astype(BF)
     return (middle, layer_out)
 

time: 217 us -> 202 us (0.931)
  blocking collectives: 152 us -> 89.7 us
  waiting for transfers between devices: 12.6 us -> 45.1 us
  starting transfers between devices: 13.5 us -> 36.7 us
  Pallas kernels: 28.1 us -> 21.8 us
  local copies, waits for them, and re-layouts: 7.99 us -> 5.72 us
    all_to_all x5 -> x3, blocking collectives: 131 us -> 89.7 us  [swap(): return lax.all_to_all(value, axes, 0, 0, tiled=True)]
    ppermute x0 -> x21, waiting for transfers between devices: none -> 37.3 us  [shifted(): lax.ppermute(value, axis, [(i, (i + distance) % size) for i in range(size)])]
    ppermute x0 -> x21, starting transfers between devices: none -> 33.4 us  [shifted(): lax.ppermute(value, axis, [(i, (i + distance) % size) for i in range(size)])]
    all_gather x1 -> x0, blocking collectives: 20.7 us -> none  [on_device(): tokens = lax.all_gather(middle, 'z')]
    all_to_all x2 -> x1, starting transfers between devices: 13.5 us -> 3.37 us  [swap(): return lax.all_to_all(value, axes, 0, 0, tiled=True)]
    pallas_call x8, Pallas kernels: 28.1 us -> 21.8 us  [call(): pl.pallas_call(kernel, out_shape=out_shape, compiler_params=pltpu.Compile...]
    all_to_all x2 -> x1, waiting for transfers between devices: 12.6 us -> 7.75 us  [swap(): return lax.all_to_all(value, axes, 0, 0, tiled=True)]
    unnamed x28 -> x30, local copies, waits for them, and re-layouts: 7.27 us -> 5.7 us
  transfers between devices with their start and end apart: 2 -> 22, of which waited for: 2 -> 13; matrix products, arithmetic and copies ran while one was open for 0% -> 0% of each run, Pallas kernels for 2% -> 2%
where the time goes in v3:
time: 202 us
  blocking collectives  89.7 us (44%)
  waiting for transfers between devices  45.1 us (22%)
  starting transfers between devices  36.7 us (18%)
  Pallas kernels  21.8 us (11%)
  local copies, waits for them, and re-layouts  5.72 us (3%)
    all_to_all x3, blocking collectives, swap(): return lax.all_to_all(value, axes, 0, 0, tiled=True)  89.7 us
    ppermute x21, waiting for transfers between devices, shifted(): lax.ppermute(value, axis, [(i, (i + distance) % size) for i in range(size)])  37.3 us
    ppermute x21, starting transfers between devices, shifted(): lax.ppermute(value, axis, [(i, (i + distance) % size) for i in range(size)])  33.4 us
    pallas_call x8, Pallas kernels, call(): pl.pallas_call(kernel, out_shape=out_shape, compiler_params=pltpu.Compile...  21.8 us
    all_to_all x1, waiting for transfers between devices, swap(): return lax.all_to_all(value, axes, 0, 0, tiled=True)  7.75 us
    unnamed x30, local copies, waits for them, and re-layouts  5.7 us
  transfers between devices with their start and end apart: 22, of which 13 were waited for; matrix products, arithmetic and copies ran while one was open for 0% of the time, Pallas kernels for 2%

profile of v3, /device:TPU:1, one launch (start us, length us, event | category | flops | bytes accessed | tf_op | source)
XLA Modules:
  0.0 201.8 jit_solution(11467419840123447864)
XLA Ops:
  6.3 7.6 %shard_map.158 = (bf16[8,256,128]{2,1,0:T(8,128)(2,1)S(1)}, f32[4,192,128]{2,1,0:T(8,128)S(1)}, bf16[4,192,128]{2,1,0:T(8,128)(2,1)S(1)}) custom-call(bf16[192,256]{1,0:T(8,128)(2,1)S(1)} %copy-done.7, bf16[192,256]{1,0:T(8,128)(2,1)S(1)} %copy-done.8, bf16[192,512]{1,0:T(8,128)(2,1)S(1)} %copy-done.5, f32[4,192]{1,0:T(4,128)S(1)} %copy-done.12, ...), custom_call_target="tpu_custom_call" | custom-call | tf_op jit(solution)/shard_map/pallas_call | solution.py:79
  13.9 24.8 %all_to_all.20.got_ref = bf16[8,256,128]{2,1,0:T(8,128)(2,1)S(1)} all-to-all(bf16[8,256,128]{2,1,0:T(8,128)(2,1)S(1)} %get-tuple-element.19), channel_id=1, replica_groups=mesh['x'=4,'z'=8,'y'=4,'c'=2] {'z'}, dimensions={0} | all-to-all | bytes 1048576 | tf_op jit(solution)/shard_map/all_to_all | solution.py:322
  39.8 2.6 %collective-permute-start.2 = (bf16[208,128]{1,0:T(8,128)(2,1)S(1)}, bf16[208,128]{1,0:T(8,128)(2,1)S(1)}, u32[]{:S(2)}, u32[]{:S(2)}) collective-permute-start(bf16[208,128]{1,0:T(8,128)(2,1)S(1)} %shard_map.159), channel_id=1, source_target_pairs={{0,192},{64,0},{128,64},{192,128},{1,193},{65,1},{129,65},{193,129... | collective-permute-start | bytes 159752 | tf_op jit(solution)/shard_map/ppermute | solution.py:318
  43.6 3.4 %collective-permute-done.1.rest_1_ = bf16[208,128]{1,0:T(8,128)(2,1)} collective-permute-done((bf16[208,128]{1,0:T(8,128)(2,1)S(1)}, bf16[208,128]{1,0:T(8,128)(2,1)}, u32[]{:S(2)}, u32[]{:S(2)}) %collective-permute-start.1) | collective-permute-done | bytes 53280 | tf_op jit(solution)/shard_map/ppermute | solution.py:318
  47.5 2.9 %shard_map.160 = bf16[8,64,128]{2,1,0:T(8,128)(2,1)} custom-call(s32[1]{0:T(128)} %bitcast.4.here_ref, bf16[8,256,128]{2,1,0:T(8,128)(2,1)S(1)} %all_to_all.20.got_ref, bf16[208,128]{1,0:T(8,128)(2,1)} %collective-permute-done.rest_0_, bf16[208,128]{1,0:T(8,128)(2,1)} %collective-permute-done.1.rest_1_, bf16[208,128]{1,0:T(8,128)(2,1)S(1)} %collective-permute-done.2.rest_2_), custom_call_target="tpu_custom_call" | custom-call | tf_op jit(solution)/shard_map/pallas_call | solution.py:79
  50.4 3.4 %all-to-all-start.1 = ((bf16[8,64,128]{2,1,0:T(8,128)(2,1)}), bf16[8,64,128]{2,1,0:T(8,128)(2,1)S(1)}, u32[]{:S(2)}, u32[]{:S(2)}) async-start(bf16[8,64,128]{2,1,0:T(8,128)(2,1)} %shard_map.160), calls=%async_computation.1 | async-start | bytes 262144 | tf_op jit(solution)/shard_map/all_to_all | solution.py:322
  53.9 7.8 %all-to-all-done.1 = bf16[8,64,128]{2,1,0:T(8,128)(2,1)S(1)} async-done(((bf16[8,64,128]{2,1,0:T(8,128)(2,1)}), bf16[8,64,128]{2,1,0:T(8,128)(2,1)S(1)}, u32[]{:S(2)}, u32[]{:S(2)}) %all-to-all-start.1) | async-done | bytes 131104 | tf_op jit(solution)/shard_map/all_to_all | solution.py:322
  63.1 5.1 %collective-permute-start.3 = (bf16[4,192,256]{2,1,0:T(8,128)(2,1)S(1)}, bf16[4,192,256]{2,1,0:T(8,128)(2,1)S(1)}, u32[]{:S(2)}, u32[]{:S(2)}) collective-permute-start(bf16[4,192,256]{2,1,0:T(8,128)(2,1)S(1)} %get-tuple-element.21), channel_id=1, source_target_pairs={{0,1},{1,0},{2,3},{3,2},{4,5},{5,4},{6,7},{7,6},{8,9},{9,8},{10,11... | collective-permute-start | bytes 1179656 | tf_op jit(solution)/shard_map/ppermute | solution.py:318
  72.6 1.6 collective-permute-start.5
  75.2 3.0 %collective-permute-done.5 = bf16[192,256]{1,0:T(8,128)(2,1)S(1)} collective-permute-done((bf16[192,256]{1,0:T(8,128)(2,1)S(1)}, bf16[192,256]{1,0:T(8,128)(2,1)S(1)}, u32[]{:S(2)}, u32[]{:S(2)}) %collective-permute-start.5) | collective-permute-done | bytes 98336 | tf_op jit(solution)/shard_map/ppermute | solution.py:318
  79.4 3.2 %collective-permute-start.11 = (bf16[192,256]{1,0:T(8,128)(2,1)S(1)}, bf16[192,256]{1,0:T(8,128)(2,1)S(1)}, u32[]{:S(2)}, u32[]{:S(2)}) collective-permute-start(bf16[192,256]{1,0:T(8,128)(2,1)S(1)} %fusion.4.rest_0_), channel_id=1, source_target_pairs={{0,40},{8,48},{16,56},{24,0},{32,8},{40,16},{48,24},{56,32},{1,41}... | collective-permute-start | bytes 294920 | tf_op jit(solution)/shard_map/ppermute | solution.py:318
  82.6 2.4 %collective-permute-start.10 = (bf16[192,256]{1,0:T(8,128)(2,1)S(1)}, bf16[192,256]{1,0:T(8,128)(2,1)S(1)}, u32[]{:S(2)}, u32[]{:S(2)}) collective-permute-start(bf16[192,256]{1,0:T(8,128)(2,1)S(1)} %fusion.4.rest_0_), channel_id=1, source_target_pairs={{0,32},{8,40},{16,48},{24,56},{32,0},{40,8},{48,16},{56,24},{1,33}... | collective-permute-start | bytes 294920 | tf_op jit(solution)/shard_map/ppermute | solution.py:318
  84.9 2.3 %collective-permute-start.9 = (bf16[192,256]{1,0:T(8,128)(2,1)S(1)}, bf16[192,256]{1,0:T(8,128)(2,1)S(1)}, u32[]{:S(2)}, u32[]{:S(2)}) collective-permute-start(bf16[192,256]{1,0:T(8,128)(2,1)S(1)} %fusion.4.rest_0_), channel_id=1, source_target_pairs={{0,24},{8,32},{16,40},{24,48},{32,56},{40,0},{48,8},{56,16},{1,25}... | collective-permute-start | bytes 294920 | tf_op jit(solution)/shard_map/ppermute | solution.py:318
  88.4 3.6 %shard_map.162 = (bf16[8,512,192]{2,1,0:T(8,128)(2,1)S(1)}, bf16[8,192,512]{2,1,0:T(8,128)(2,1)S(1)}) custom-call(s32[1]{0:T(128)} %bitcast.11.here_ref, bf16[8,256,128]{2,1,0:T(8,128)(2,1)S(1)} %all_to_all.20.got_ref), custom_call_target="tpu_custom_call" | custom-call | tf_op jit(solution)/shard_map/pallas_call | solution.py:79
  92.0 8.1 %collective-permute-done.9.rest_3_ = bf16[192,256]{1,0:T(8,128)(2,1)S(1)} collective-permute-done((bf16[192,256]{1,0:T(8,128)(2,1)S(1)}, bf16[192,256]{1,0:T(8,128)(2,1)S(1)}, u32[]{:S(2)}, u32[]{:S(2)}) %collective-permute-start.9) | collective-permute-done | bytes 98336 | tf_op jit(solution)/shard_map/ppermute | solution.py:318
  100.1 4.7 %collective-permute-done.7.rest_1_ = bf16[192,256]{1,0:T(8,128)(2,1)S(1)} collective-permute-done((bf16[192,256]{1,0:T(8,128)(2,1)S(1)}, bf16[192,256]{1,0:T(8,128)(2,1)S(1)}, u32[]{:S(2)}, u32[]{:S(2)}) %collective-permute-start.7) | collective-permute-done | bytes 98336 | tf_op jit(solution)/shard_map/ppermute | solution.py:318
  105.5 33.0 %all_to_all.21 = bf16[32,128,256]{2,1,0:T(8,128)(2,1)S(1)} all-to-all(bf16[32,128,256]{2,1,0:T(8,128)(2,1)S(1)} %shard_map.163), channel_id=1, replica_groups=mesh['x'=4,'z'=8,'y'=4,'c'=2] {'x','y','c'}, dimensions={0} | all-to-all | bytes 4194304 | tf_op jit(solution)/shard_map/all_to_all | solution.py:322
  138.5 4.0 %shard_map.164 = bf16[4,8,128,256]{3,2,1,0:T(8,128)(2,1)S(1)} custom-call(bf16[4,8,128,256]{3,2,1,0:T(8,128)(2,1)S(1)} %bitcast.32, f32[1,2048]{1,0:T(1,128)S(1)} %bitcast.40, bf16[2048,512]{1,0:T(8,128)(2,1)S(1)} %bitcast.34, bf16[2048,512]{1,0:T(8,128)(2,1)S(1)} %bitcast.35, bf16[512,2048]{1,0:T(8,128)(2,1)S(1)} %bitcast.36), custom_call_target="tpu_custom_call" | custom-call | tf_op jit(solution)/shard_map/pallas_call | solution.py:79
  142.5 31.9 %all_to_all.22.rows_ref = bf16[32,128,256]{2,1,0:T(8,128)(2,1)S(1)} all-to-all(bf16[32,128,256]{2,1,0:T(8,128)(2,1)S(1)} %bitcast.33), channel_id=1, replica_groups=mesh['x'=4,'z'=8,'y'=4,'c'=2] {'x','y','c'}, dimensions={0} | all-to-all | bytes 4194304 | tf_op jit(solution)/shard_map/all_to_all | solution.py:322
  176.4 2.2 %collective-permute-start.16 = (bf16[192,256]{1,0:T(8,128)(2,1)S(1)}, bf16[192,256]{1,0:T(8,128)(2,1)S(1)}, u32[]{:S(2)}, u32[]{:S(2)}) collective-permute-start(bf16[192,256]{1,0:T(8,128)(2,1)S(1)} %get-tuple-element.27), channel_id=1, source_target_pairs={{0,40},{8,48},{16,56},{24,0},{32,8},{40,16},{48,24},{56,32},{1,41}... | collective-permute-start | bytes 294920 | tf_op jit(solution)/shard_map/ppermute | solution.py:318
  178.7 3.1 %collective-permute-start.17 = (bf16[192,256]{1,0:T(8,128)(2,1)S(1)}, bf16[192,256]{1,0:T(8,128)(2,1)S(1)}, u32[]{:S(2)}, u32[]{:S(2)}) collective-permute-start(bf16[192,256]{1,0:T(8,128)(2,1)S(1)} %get-tuple-element.28), channel_id=1, source_target_pairs={{0,32},{8,40},{16,48},{24,56},{32,0},{40,8},{48,16},{56,24},{1,33}... | collective-permute-start | bytes 294920 | tf_op jit(solution)/shard_map/ppermute | solution.py:318
  182.8 2.4 %collective-permute-start.19 = (bf16[192,256]{1,0:T(8,128)(2,1)S(1)}, bf16[192,256]{1,0:T(8,128)(2,1)S(1)}, u32[]{:S(2)}, u32[]{:S(2)}) collective-permute-start(bf16[192,256]{1,0:T(8,128)(2,1)S(1)} %get-tuple-element.30), channel_id=1, source_target_pairs={{0,16},{8,24},{16,32},{24,40},{32,48},{40,56},{48,0},{56,8},{1,17}... | collective-permute-start | bytes 294920 | tf_op jit(solution)/shard_map/ppermute | solution.py:318
  186.2 9.6 %collective-permute-done.18 = bf16[192,256]{1,0:T(8,128)(2,1)S(1)} collective-permute-done((bf16[192,256]{1,0:T(8,128)(2,1)S(1)}, bf16[192,256]{1,0:T(8,128)(2,1)S(1)}, u32[]{:S(2)}, u32[]{:S(2)}) %collective-permute-start.18) | collective-permute-done | bytes 98336 | tf_op jit(solution)/shard_map/ppermute | solution.py:318
  197.1 4.0 %collective-permute-done.20 = bf16[192,256]{1,0:T(8,128)(2,1)S(1)} collective-permute-done((bf16[192,256]{1,0:T(8,128)(2,1)S(1)}, bf16[192,256]{1,0:T(8,128)(2,1)S(1)}, u32[]{:S(2)}, u32[]{:S(2)}) %collective-permute-start.20) | collective-permute-done | bytes 98336 | tf_op jit(solution)/shard_map/ppermute | solution.py:318
  (66 shorter events, 24.7 us)
Async XLA Ops:
  0.6 61.0 %copy-start = (bf16[512,2048]{1,0:T(8,128)(2,1)S(1)}, bf16[512,2048]{1,0:T(8,128)(2,1)}, u32[]{:S(2)}) copy-start(bf16[512,2048]{1,0:T(8,128)(2,1)} %proj_ref.1) | copy-start | bytes 6291460
  39.8 3.8 %collective-permute-start.2 = (bf16[208,128]{1,0:T(8,128)(2,1)S(1)}, bf16[208,128]{1,0:T(8,128)(2,1)S(1)}, u32[]{:S(2)}, u32[]{:S(2)}) collective-permute-start(bf16[208,128]{1,0:T(8,128)(2,1)S(1)} %shard_map.159), channel_id=1, source_target_pairs={{0,192},{64,0},{128,64},{192,128},{1,193},{65,1},{129,65},{193,129... | collective-permute-start | bytes 159752 | tf_op jit(solution)/shard_map/ppermute | solution.py:318
  42.4 4.6 %collective-permute-start.1 = (bf16[208,128]{1,0:T(8,128)(2,1)S(1)}, bf16[208,128]{1,0:T(8,128)(2,1)}, u32[]{:S(2)}, u32[]{:S(2)}) collective-permute-start(bf16[208,128]{1,0:T(8,128)(2,1)S(1)} %shard_map.159), channel_id=1, source_target_pairs={{0,128},{64,192},{128,0},{192,64},{1,129},{65,193},{129,1},{193,65... | collective-permute-start | bytes 159752 | tf_op jit(solution)/shard_map/ppermute | solution.py:318
  42.9 4.7 %collective-permute-start = (bf16[208,128]{1,0:T(8,128)(2,1)S(1)}, bf16[208,128]{1,0:T(8,128)(2,1)}, u32[]{:S(2)}, u32[]{:S(2)}) collective-permute-start(bf16[208,128]{1,0:T(8,128)(2,1)S(1)} %shard_map.159), channel_id=1, source_target_pairs={{0,64},{64,128},{128,192},{192,0},{1,65},{65,129},{129,193},{193,1... | collective-permute-start | bytes 159752 | tf_op jit(solution)/shard_map/ppermute | solution.py:318
  50.4 11.2 %all-to-all-start.1 = ((bf16[8,64,128]{2,1,0:T(8,128)(2,1)}), bf16[8,64,128]{2,1,0:T(8,128)(2,1)S(1)}, u32[]{:S(2)}, u32[]{:S(2)}) async-start(bf16[8,64,128]{2,1,0:T(8,128)(2,1)} %shard_map.160), calls=%async_computation.1 | async-start | bytes 262144 | tf_op jit(solution)/shard_map/all_to_all | solution.py:322
  63.1 6.5 %collective-permute-start.3 = (bf16[4,192,256]{2,1,0:T(8,128)(2,1)S(1)}, bf16[4,192,256]{2,1,0:T(8,128)(2,1)S(1)}, u32[]{:S(2)}, u32[]{:S(2)}) collective-permute-start(bf16[4,192,256]{2,1,0:T(8,128)(2,1)S(1)} %get-tuple-element.21), channel_id=1, source_target_pairs={{0,1},{1,0},{2,3},{3,2},{4,5},{5,4},{6,7},{7,6},{8,9},{9,8},{10,11... | collective-permute-start | bytes 1179656 | tf_op jit(solution)/shard_map/ppermute | solution.py:318
  69.7 5.4 %collective-permute-start.4 = (bf16[192,256]{1,0:T(8,128)(2,1)S(1)}, bf16[192,256]{1,0:T(8,128)(2,1)S(1)}, u32[]{:S(2)}, u32[]{:S(2)}) collective-permute-start(bf16[192,256]{1,0:T(8,128)(2,1)S(1)} %get-tuple-element.34), channel_id=1, source_target_pairs={{0,2},{2,4},{4,6},{6,0},{1,3},{3,5},{5,7},{7,1},{8,10},{10,12},{12... | collective-permute-start | bytes 294920 | tf_op jit(solution)/shard_map/ppermute | solution.py:318
  71.1 4.1 %collective-permute-start.6 = (bf16[192,256]{1,0:T(8,128)(2,1)S(1)}, bf16[192,256]{1,0:T(8,128)(2,1)S(1)}, u32[]{:S(2)}, u32[]{:S(2)}) collective-permute-start(bf16[192,256]{1,0:T(8,128)(2,1)S(1)} %get-tuple-element.35), channel_id=1, source_target_pairs={{0,6},{2,0},{4,2},{6,4},{1,7},{3,1},{5,3},{7,5},{8,14},{10,8},{12,... | collective-permute-start | bytes 294920 | tf_op jit(solution)/shard_map/ppermute | solution.py:318
  72.6 5.5 %collective-permute-start.5 = (bf16[192,256]{1,0:T(8,128)(2,1)S(1)}, bf16[192,256]{1,0:T(8,128)(2,1)S(1)}, u32[]{:S(2)}, u32[]{:S(2)}) collective-permute-start(bf16[192,256]{1,0:T(8,128)(2,1)S(1)} %get-tuple-element.36), channel_id=1, source_target_pairs={{0,4},{2,6},{4,0},{6,2},{1,5},{3,7},{5,1},{7,3},{8,12},{10,14},{12... | collective-permute-start | bytes 294920 | tf_op jit(solution)/shard_map/ppermute | solution.py:318
  79.1 122.0 %copy-start.4 = (bf16[192,256]{1,0:T(8,128)(2,1)}, bf16[192,256]{1,0:T(8,128)(2,1)S(1)}, u32[]{:S(2)}) copy-start(bf16[192,256]{1,0:T(8,128)(2,1)S(1)} %fusion.4.rest_0_) | copy-start | bytes 294916
  79.1 8.1 %collective-permute-start.13 = (bf16[192,256]{1,0:T(8,128)(2,1)S(1)}, bf16[192,256]{1,0:T(8,128)(2,1)S(1)}, u32[]{:S(2)}, u32[]{:S(2)}) collective-permute-start(bf16[192,256]{1,0:T(8,128)(2,1)S(1)} %fusion.4.rest_0_), channel_id=1, source_target_pairs={{0,56},{8,0},{16,8},{24,16},{32,24},{40,32},{48,40},{56,48},{1,57}... | collective-permute-start | bytes 294920 | tf_op jit(solution)/shard_map/ppermute | solution.py:318
  79.2 9.2 %collective-permute-start.12 = (bf16[192,256]{1,0:T(8,128)(2,1)S(1)}, bf16[192,256]{1,0:T(8,128)(2,1)S(1)}, u32[]{:S(2)}, u32[]{:S(2)}) collective-permute-start(bf16[192,256]{1,0:T(8,128)(2,1)S(1)} %fusion.4.rest_0_), channel_id=1, source_target_pairs={{0,48},{8,56},{16,0},{24,8},{32,16},{40,24},{48,32},{56,40},{1,49}... | collective-permute-start | bytes 294920 | tf_op jit(solution)/shard_map/ppermute | solution.py:318
  79.4 12.6 %collective-permute-start.11 = (bf16[192,256]{1,0:T(8,128)(2,1)S(1)}, bf16[192,256]{1,0:T(8,128)(2,1)S(1)}, u32[]{:S(2)}, u32[]{:S(2)}) collective-permute-start(bf16[192,256]{1,0:T(8,128)(2,1)S(1)} %fusion.4.rest_0_), channel_id=1, source_target_pairs={{0,40},{8,48},{16,56},{24,0},{32,8},{40,16},{48,24},{56,32},{1,41}... | collective-permute-start | bytes 294920 | tf_op jit(solution)/shard_map/ppermute | solution.py:318
  82.6 9.4 %collective-permute-start.10 = (bf16[192,256]{1,0:T(8,128)(2,1)S(1)}, bf16[192,256]{1,0:T(8,128)(2,1)S(1)}, u32[]{:S(2)}, u32[]{:S(2)}) collective-permute-start(bf16[192,256]{1,0:T(8,128)(2,1)S(1)} %fusion.4.rest_0_), channel_id=1, source_target_pairs={{0,32},{8,40},{16,48},{24,56},{32,0},{40,8},{48,16},{56,24},{1,33}... | collective-permute-start | bytes 294920 | tf_op jit(solution)/shard_map/ppermute | solution.py:318
  84.9 15.1 %collective-permute-start.9 = (bf16[192,256]{1,0:T(8,128)(2,1)S(1)}, bf16[192,256]{1,0:T(8,128)(2,1)S(1)}, u32[]{:S(2)}, u32[]{:S(2)}) collective-permute-start(bf16[192,256]{1,0:T(8,128)(2,1)S(1)} %fusion.4.rest_0_), channel_id=1, source_target_pairs={{0,24},{8,32},{16,40},{24,48},{32,56},{40,0},{48,8},{56,16},{1,25}... | collective-permute-start | bytes 294920 | tf_op jit(solution)/shard_map/ppermute | solution.py:318
  87.2 12.9 %collective-permute-start.8 = (bf16[192,256]{1,0:T(8,128)(2,1)S(1)}, bf16[192,256]{1,0:T(8,128)(2,1)S(1)}, u32[]{:S(2)}, u32[]{:S(2)}) collective-permute-start(bf16[192,256]{1,0:T(8,128)(2,1)S(1)} %fusion.4.rest_0_), channel_id=1, source_target_pairs={{0,16},{8,24},{16,32},{24,40},{32,48},{40,56},{48,0},{56,8},{1,17}... | collective-permute-start | bytes 294920 | tf_op jit(solution)/shard_map/ppermute | solution.py:318
  88.4 16.4 %collective-permute-start.7 = (bf16[192,256]{1,0:T(8,128)(2,1)S(1)}, bf16[192,256]{1,0:T(8,128)(2,1)S(1)}, u32[]{:S(2)}, u32[]{:S(2)}) collective-permute-start(bf16[192,256]{1,0:T(8,128)(2,1)S(1)} %fusion.4.rest_0_), channel_id=1, source_target_pairs={{0,8},{8,16},{16,24},{24,32},{32,40},{40,48},{48,56},{56,0},{1,9},... | collective-permute-start | bytes 294920 | tf_op jit(solution)/shard_map/ppermute | solution.py:318
  175.0 7.8 %collective-permute-start.14 = (bf16[192,256]{1,0:T(8,128)(2,1)S(1)}, bf16[192,256]{1,0:T(8,128)(2,1)S(1)}, u32[]{:S(2)}, u32[]{:S(2)}) collective-permute-start(bf16[192,256]{1,0:T(8,128)(2,1)S(1)} %get-tuple-element.25), channel_id=1, source_target_pairs={{0,56},{8,0},{16,8},{24,16},{32,24},{40,32},{48,40},{56,48},{1,57}... | collective-permute-start | bytes 294920 | tf_op jit(solution)/shard_map/ppermute | solution.py:318
  175.1 10.0 %collective-permute-start.15 = (bf16[192,256]{1,0:T(8,128)(2,1)S(1)}, bf16[192,256]{1,0:T(8,128)(2,1)S(1)}, u32[]{:S(2)}, u32[]{:S(2)}) collective-permute-start(bf16[192,256]{1,0:T(8,128)(2,1)S(1)} %get-tuple-element.26), channel_id=1, source_target_pairs={{0,48},{8,56},{16,0},{24,8},{32,16},{40,24},{48,32},{56,40},{1,49}... | collective-permute-start | bytes 294920 | tf_op jit(solution)/shard_map/ppermute | solution.py:318
  176.4 9.4 %collective-permute-start.16 = (bf16[192,256]{1,0:T(8,128)(2,1)S(1)}, bf16[192,256]{1,0:T(8,128)(2,1)S(1)}, u32[]{:S(2)}, u32[]{:S(2)}) collective-permute-start(bf16[192,256]{1,0:T(8,128)(2,1)S(1)} %get-tuple-element.27), channel_id=1, source_target_pairs={{0,40},{8,48},{16,56},{24,0},{32,8},{40,16},{48,24},{56,32},{1,41}... | collective-permute-start | bytes 294920 | tf_op jit(solution)/shard_map/ppermute | solution.py:318
  178.7 7.5 %collective-permute-start.17 = (bf16[192,256]{1,0:T(8,128)(2,1)S(1)}, bf16[192,256]{1,0:T(8,128)(2,1)S(1)}, u32[]{:S(2)}, u32[]{:S(2)}) collective-permute-start(bf16[192,256]{1,0:T(8,128)(2,1)S(1)} %get-tuple-element.28), channel_id=1, source_target_pairs={{0,32},{8,40},{16,48},{24,56},{32,0},{40,8},{48,16},{56,24},{1,33}... | collective-permute-start | bytes 294920 | tf_op jit(solution)/shard_map/ppermute | solution.py:318
  181.8 13.9 %collective-permute-start.18 = (bf16[192,256]{1,0:T(8,128)(2,1)S(1)}, bf16[192,256]{1,0:T(8,128)(2,1)S(1)}, u32[]{:S(2)}, u32[]{:S(2)}) collective-permute-start(bf16[192,256]{1,0:T(8,128)(2,1)S(1)} %get-tuple-element.29), channel_id=1, source_target_pairs={{0,24},{8,32},{16,40},{24,48},{32,56},{40,0},{48,8},{56,16},{1,25}... | collective-permute-start | bytes 294920 | tf_op jit(solution)/shard_map/ppermute | solution.py:318
  182.8 14.4 %collective-permute-start.19 = (bf16[192,256]{1,0:T(8,128)(2,1)S(1)}, bf16[192,256]{1,0:T(8,128)(2,1)S(1)}, u32[]{:S(2)}, u32[]{:S(2)}) collective-permute-start(bf16[192,256]{1,0:T(8,128)(2,1)S(1)} %get-tuple-element.30), channel_id=1, source_target_pairs={{0,16},{8,24},{16,32},{24,40},{32,48},{40,56},{48,0},{56,8},{1,17}... | collective-permute-start | bytes 294920 | tf_op jit(solution)/shard_map/ppermute | solution.py:318
  185.1 16.0 %collective-permute-start.20 = (bf16[192,256]{1,0:T(8,128)(2,1)S(1)}, bf16[192,256]{1,0:T(8,128)(2,1)S(1)}, u32[]{:S(2)}, u32[]{:S(2)}) collective-permute-start(bf16[192,256]{1,0:T(8,128)(2,1)S(1)} %get-tuple-element.31), channel_id=1, source_target_pairs={{0,8},{8,16},{16,24},{24,32},{32,40},{40,48},{48,56},{56,0},{1,9},... | collective-permute-start | bytes 294920 | tf_op jit(solution)/shard_map/ppermute | solution.py:318
  (13 other events, 249.2 us)

commit v4 on v3

--- a/solution.py
+++ b/solution.py
@@ -11,7 +11,6 @@
 DV = 128
 SLOTS = 16
 MARKS = 16
-TARGETS = 32
 SHARES = 8
 EPS = 1e-06
 BF = jnp.bfloat16
@@ -85,10 +84,7 @@
     )(*operands)
 
 
-def mixer_kernel(*refs):
-    count = len(refs) // 2 - 2
-    sources, (send_ref, inside_ref, reach_ref) = refs[:count], refs[count : count + 3]
-    held, sems = refs[count + 3 : -1], refs[-1]
+def brought(sources, held, sems):
     copies = [
         pltpu.make_async_copy(source, target, sems.at[i])
         for i, (source, target) in enumerate(zip(sources, held))
@@ -97,44 +93,60 @@
         copy.start()
     for copy in copies:
         copy.wait()
-    q_ref, k_ref, v_ref, decay_ref, logit_ref, ids_ref, weight_ref = held
-    length = q_ref.shape[0]
-    heads = decay_ref.shape[0]
-    ratio = heads // (q_ref.shape[1] // DK)
-    places = send_ref.shape[0]
-    cuts = places // heads
-    rows = DV // cuts
-    targets = TARGETS
-    shares = SHARES
+
+
+def key_norms(key):
+    key_f = key.astype(F32)
+    square = key_f * key_f
+    scale = lax.rsqrt(jnp.sum(square, axis=1, keepdims=True) + EPS)
+    scale_row = lax.rsqrt(exact(jnp.ones((8, DK), F32), square, NT)[:1] + EPS)
+    return scale, scale_row
+
+
+def order(length):
     row = lax.broadcasted_iota(jnp.int32, (length, length), 0)
     col = lax.broadcasted_iota(jnp.int32, (length, length), 1)
+    return row, col
+
+
+def faded(on, log_col, log_row, rate_row):
+    apart = jnp.where(on, log_col - log_row, 0.0)
+    return jnp.where(on, jnp.exp(apart), 0.0) * rate_row
+
+
+def logs(decay, on):
+    tri = jnp.where(on, 1.0, 0.0)
+    return -exact(decay, tri, NT), -exact(tri, decay, NT)
+
+
+def solve_kernel(*refs):
+    count = (len(refs) - 3) // 2
+    sources, (send_ref, solved_ref) = refs[:count], refs[count : count + 2]
+    held, sems = refs[count + 2 : -1], refs[-1]
+    brought(sources, held, sems)
+    k_ref, v_ref, decay_ref, logit_ref = held
+    length = k_ref.shape[0]
+    heads = decay_ref.shape[0]
+    ratio = heads // (k_ref.shape[1] // DK)
+    cuts = send_ref.shape[0] // heads
+    rows = DV // cuts
+    row, col = order(length)
     on = row >= col
     below = row > col
     eye = jnp.where(row == col, 1.0, 0.0)
-    tri = jnp.where(on, 1.0, 0.0)
     rate_row = 1.0 / (1.0 + jnp.exp(-logit_ref[...]))
-    log_row = -exact(decay_ref[...], tri, NT)
-    log_col = -exact(tri, decay_ref[...], NT)
+    log_row, log_col = logs(decay_ref[...], on)
     rate_col = exact(eye, rate_row, NT)
-    ones = jnp.ones((8, DK), F32)
-    systems, weights, scales = [], [], []
+    systems, keys = [], []
     for group in range(heads // ratio):
-        part = slice(group * DK, (group + 1) * DK)
-        query = q_ref[:, part]
-        key = k_ref[:, part]
-        query_f = query.astype(F32)
-        key_f = key.astype(F32)
-        query_scale = lax.rsqrt(jnp.sum(query_f * query_f, axis=1, keepdims=True) + EPS) * DK**-0.5
-        key_scale = lax.rsqrt(jnp.sum(key_f * key_f, axis=1, keepdims=True) + EPS)
-        key_scale_row = lax.rsqrt(exact(ones, key_f * key_f, NT)[:1] + EPS)
-        key_key = mm(key, key, NT) * (key_scale * key_scale_row)
-        query_key = mm(query, key, NT) * (query_scale * key_scale_row)
+        key = k_ref[:, group * DK : (group + 1) * DK]
+        scale, scale_row = key_norms(key)
+        key_key = mm(key, key, NT) * (scale * scale_row)
         for head in range(group * ratio, (group + 1) * ratio):
-            apart = jnp.where(on, log_col[:, head : head + 1] - log_row[head : head + 1, :], 0.0)
-            fading = jnp.where(on, jnp.exp(apart), 0.0) * rate_row[head : head + 1, :]
+            pick = slice(head, head + 1)
+            fading = faded(on, log_col[:, pick], log_row[pick], rate_row[pick])
             systems.append(jnp.where(below, key_key * fading, 0.0))
-            weights.append(query_key * fading)
-            scales.append((query_f * query_scale, key_f * key_scale, key_scale, key))
+            keys.append((key, scale))
     inverses = [eye - jnp.where(row // 2 == col // 2, system, 0.0) for system in systems]
     size = 2
     while size < length:
@@ -147,20 +159,23 @@
             inverse - mm(inverse, cross) for inverse, cross in zip(inverses, crossing)
         ]
         size *= 2
+    targets = []
     for head in range(heads):
-        query_n, key_n, key_scale, key = scales[head]
+        key, scale = keys[head]
         lead = jnp.exp(log_col[:, head : head + 1])
         value = v_ref[:, head * DV : (head + 1) * DV].astype(F32)
-        target = jnp.concatenate([value, lead * key_n], axis=1)
-        solved = mm(inverses[head], target)
-        missing = target - solved - mm3(systems[head], solved)
-        solved = solved + mm(inverses[head], missing)
-        both = mm3(weights[head], solved)
-        inside_ref[head] = both[:, :DV]
-        reach_ref[head] = (lead * query_n - both[:, DV:]).astype(reach_ref.dtype)
+        targets.append(jnp.concatenate([value, lead * scale * key.astype(F32)], axis=1))
+    firsts = [mm(inverses[head], targets[head]) for head in range(heads)]
+    missing = [
+        targets[head] - firsts[head] - mm3(systems[head], firsts[head]) for head in range(heads)
+    ]
+    solutions = [firsts[head] + mm(inverses[head], missing[head]) for head in range(heads)]
+    for head in range(heads):
+        key, scale = keys[head]
+        solved_ref[head] = solutions[head]
         last = log_col[length - 1 : length, head : head + 1]
-        tail = jnp.exp(last - log_col[:, head : head + 1]) * rate_col[:, head : head + 1] * key_scale
-        high, low = halves(solved * tail)
+        tail = jnp.exp(last - log_col[:, head : head + 1]) * rate_col[:, head : head + 1] * scale
+        high, low = halves(solutions[head] * tail)
         written = mm(high, key, TN) + mm(low, key, TN)
         removed = written[DV:].astype(BF)
         added = written[:DV].astype(BF)
@@ -169,18 +184,46 @@
             place = head * cuts + cut
             send_ref[place, :DK, :] = removed
             send_ref[place, DK : DK + rows, :] = added[cut * rows : (cut + 1) * rows]
-            send_ref[place, DK + rows : DK + rows + MARKS, :] = fade
-    base = DK + rows + MARKS
+            send_ref[place, DK + rows :, :] = fade
+
+
+def inner_kernel(
+    q_ref, k_ref, decay_ref, logit_ref, solved_ref, ids_ref, weight_ref, inside_ref, reach_ref, route_ref
+):
+    length = q_ref.shape[0]
+    heads = decay_ref.shape[0]
+    ratio = heads // (q_ref.shape[1] // DK)
+    row, col = order(length)
+    on = row >= col
+    rate_row = 1.0 / (1.0 + jnp.exp(-logit_ref[...]))
+    log_row, log_col = logs(decay_ref[...], on)
+    for group in range(heads // ratio):
+        part = slice(group * DK, (group + 1) * DK)
+        query = q_ref[:, part]
+        key = k_ref[:, part]
+        query_f = query.astype(F32)
+        query_scale = lax.rsqrt(jnp.sum(query_f * query_f, axis=1, keepdims=True) + EPS) * DK**-0.5
+        _, scale_row = key_norms(key)
+        query_key = mm(query, key, NT) * (query_scale * scale_row)
+        for head in range(group * ratio, (group + 1) * ratio):
+            pick = slice(head, head + 1)
+            weight = query_key * faded(on, log_col[:, pick], log_row[pick], rate_row[pick])
+            both = mm3(weight, solved_ref[head])
+            inside_ref[head] = both[:, :DV]
+            reach = jnp.exp(log_col[:, pick]) * query_scale * query_f - both[:, DV:]
+            reach_ref[head] = reach.astype(BF)
+    places, packed, _ = route_ref.shape
+    targets = packed * 2 // 3
     number = lax.broadcasted_iota(jnp.int32, (targets, length), 0)
-    number = (number // shares) * (places * shares) + number % shares
+    number = (number // SHARES) * (places * SHARES) + number % SHARES
     for place in range(places):
         weight = jnp.zeros((targets, length), F32)
         for choice in range(ids_ref.shape[0]):
-            hit = ids_ref[choice : choice + 1, :] == number + place * shares
+            hit = ids_ref[choice : choice + 1, :] == number + place * SHARES
             weight = weight + jnp.where(hit, weight_ref[choice : choice + 1, :], 0.0)
         weight = weight.astype(BF)
-        send_ref[place, base : base + targets, :] = weight[:, :DK]
-        send_ref[place, base + targets :, :] = jnp.concatenate(
+        route_ref[place, :targets, :] = weight[:, :DK]
+        route_ref[place, targets:, :] = jnp.concatenate(
             [weight[: targets // 2, DK:], weight[targets // 2 :, DK:]], axis=1
         )
 
@@ -208,15 +251,17 @@
     total_ref[DK + rows :, :] = pieces(jnp.broadcast_to(whole, (MARKS, DK)))
 
 
-def state_kernel(here_ref, got_ref, *rest):
+def state_kernel(here_ref, got_ref, route_ref, *rest):
     totals, enter_ref = rest[:-1], rest[-1]
-    blocks, rows, _ = enter_ref.shape
+    blocks = enter_ref.shape[0]
+    rows = enter_ref.shape[1] - route_ref.shape[1]
+    enter_ref[:, rows:, :] = route_ref[...]
     state = jnp.zeros((rows, DK), F32)
     for distance in range(len(totals), 0, -1):
         removed, added, fade = unpack(totals[distance - 1], rows)
         state = jnp.where(distance <= here_ref[0], advance(state, removed, fade) + added, state)
     for block in range(blocks):
-        enter_ref[block] = state.astype(BF)
+        enter_ref[block, :rows, :] = state.astype(BF)
         if block < blocks - 1:
             removed, added, fade = unpack(got_ref[block], rows)
             state = advance(state, removed, fade) + added
@@ -229,7 +274,10 @@
     gated = []
     for head in range(heads):
         part = slice(head * DV, (head + 1) * DV)
-        output = inside_ref[head] + mm(reach_ref[head], state_ref[head], NT)
+        cuts = state_ref.shape[0] // heads
+        places = range(head * cuts, (head + 1) * cuts)
+        state = jnp.concatenate([state_ref[place, : DV // cuts] for place in places], axis=0)
+        output = inside_ref[head] + mm(reach_ref[head], state, NT)
         scaling = lax.rsqrt(jnp.mean(output * output, axis=1, keepdims=True) + EPS)
         opened = silu(gate_ref[:, part].astype(F32))
         gated.append((output * scaling * gain_ref[...] * opened).astype(BF))
@@ -275,8 +323,14 @@
     tokens, send_ref = rest[:-1], rest[-1]
     targets = send_ref.shape[0]
     width = send_ref.shape[2]
-    for block in range(pick_ref.shape[0]):
-        rows = mm(pick_ref[block], tokens[block][...]).astype(BF)
+    blocks = pick_ref.shape[0]
+    far = blocks // 2
+    for block in range(blocks):
+        place = block if block <= far else block + 1
+        token = tokens[place][...]
+        if block == far:
+            token = jnp.concatenate([token, tokens[place + 1][...]], axis=0)
+        rows = mm(pick_ref[block], token).astype(BF)
         send_ref[:, block * SLOTS : (block + 1) * SLOTS, :] = rows.reshape(targets, SLOTS, width)
 
 
@@ -320,6 +374,31 @@
 
 def swap(value, axes):
     return lax.all_to_all(value, axes, 0, 0, tiled=True)
+
+
+def spread_out(value, axis):
+    half = value.shape[0] // 2
+    right = [value, shifted(value, axis, 1), shifted(value, axis, 2)]
+    left = [shifted(value, axis, -1), shifted(value, axis, -2)]
+    right.append(shifted(right[2], axis, 1))
+    left.append(shifted(left[1], axis, -1))
+    far = [shifted(right[2][:half], axis, 2), shifted(left[1][half:], axis, -2)]
+    return right + far + left[::-1]
+
+
+def gathered_sum(parts, axis):
+    def passed(value, distance):
+        return shifted(value.astype(BF), axis, distance).astype(F32)
+
+    half = parts[4].shape[0] // 2
+    first = passed(parts[4][:half], -2)
+    last = passed(parts[4][half:], 2)
+    left = parts[2] + passed(parts[3], -1)
+    right = parts[6] + passed(parts[5], 1)
+    left = jnp.concatenate([left[:half] + first, left[half:]], axis=0)
+    right = jnp.concatenate([right[:half], right[half:] + last], axis=0)
+    near = passed(parts[1], -1) + passed(parts[7], 1)
+    return parts[0] + near + (passed(left, -2) + passed(right, 2))
 
 
 def on_device(
@@ -351,32 +430,52 @@
     shape = jax.ShapeDtypeStruct
 
     rows = heads * DV // blocks
-    packed = DK + rows + MARKS + targets + targets // 2
-    operands = (
-        query_in,
-        key_in,
-        value_in,
-        decay_rate,
-        beta_logit,
-        expert_ids.T,
-        route_weight.T,
-    )
-    send, inside, reach = call(
-        mixer_kernel,
+    extra = targets + targets // 2
+    operands = (key_in, value_in, decay_rate, beta_logit)
+    send, solved = call(
+        solve_kernel,
         (
-            shape((blocks, packed, DK), BF),
-            shape((heads, length, DV), F32),
-            shape((heads, length, DK), BF),
+            shape((blocks, DK + rows + MARKS, DK), BF),
+            shape((heads, length, DV + DK), F32),
         ),
         *operands,
         vmem=24,
-        in_specs=[pl.BlockSpec(memory_space=pl.ANY)] * len(operands),
+        in_specs=[pl.BlockSpec(memory_space=pltpu.HBM)] * len(operands),
         scratch_shapes=[pltpu.VMEM(item.shape, item.dtype) for item in operands]
         + [pltpu.SemaphoreType.DMA((len(operands),))],
     )
     got = swap(send, "z")
+    inside, reach, route = call(
+        inner_kernel,
+        (
+            shape((heads, length, DV), F32),
+            shape((heads, length, DK), BF),
+            shape((blocks, extra, DK), BF),
+        ),
+        query_in,
+        key_in,
+        decay_rate,
+        beta_logit,
+        solved,
+        expert_ids.T,
+        route_weight.T,
+        vmem=16,
+        flops=2 * 10**9,
+        moved=3 * 10**6,
+    )
     total = call(total_kernel, shape((DK + rows + MARKS, DK), BF), got, vmem=8)
     totals = [shifted(total, "x", distance) for distance in range(1, groups)]
+    enter = call(
+        state_kernel,
+        shape((blocks, rows + extra, DK), BF),
+        lax.axis_index("x").reshape(1),
+        got,
+        route,
+        *totals,
+        vmem=8,
+        in_specs=[SCALAR] + [VECTOR] * (2 + len(totals)),
+    )
+    back = swap(enter, "z")
     pick, mix = call(
         route_kernel,
         (
@@ -384,20 +483,12 @@
             shape((blocks, length, targets * SLOTS), BF),
         ),
         lax.axis_index("z").reshape(1),
-        got,
+        back,
         vmem=12,
+        flops=10**9,
+        moved=4 * 10**6,
         in_specs=[SCALAR, VECTOR],
     )
-    enter = call(
-        state_kernel,
-        shape((blocks, rows, DK), BF),
-        lax.axis_index("x").reshape(1),
-        got,
-        *totals,
-        vmem=8,
-        in_specs=[SCALAR] + [VECTOR] * (1 + len(totals)),
-    )
-    state = swap(enter, "z").reshape(heads, DV, DK)
 
     here = jnp.stack([lax.axis_index("y"), lax.axis_index("c")])
     columns = lax.axis_size("y")
@@ -407,7 +498,7 @@
         here,
         inside,
         reach,
-        state,
+        back,
         gate_in,
         head_gain.reshape(1, DV),
         out_proj,
@@ -421,7 +512,7 @@
     residual = lax.dynamic_slice_in_dim(residual_in, share * width, width, 1)
     middle = (residual.astype(F32) + mixed).astype(BF)
 
-    tokens = [middle] + [shifted(middle, "z", distance) for distance in range(1, blocks)]
+    tokens = spread_out(middle, "z")
     send = call(pick_kernel, shape((targets, count, width), BF), pick, *tokens, vmem=12)
     arrived = swap(send, ("x", "y", "c")).reshape(groups, shares, count, width)
     produced = call(
@@ -438,14 +529,12 @@
     returned = swap(produced.reshape(targets, count, width), ("x", "y", "c"))
     mixes = call(
         combine_kernel,
-        (shape((length, width), F32),) + (shape((length, width), BF),) * (blocks - 1),
+        tuple(shape((length, width), F32 if i in (0, 2, 6) else BF) for i in range(blocks)),
         mix,
         returned,
         vmem=16,
     )
-    expert_mix = mixes[0]
-    for distance in range(1, blocks):
-        expert_mix = expert_mix + shifted(mixes[distance], "z", -distance).astype(F32)
+    expert_mix = gathered_sum(mixes, "z")
     layer_out = (middle.astype(F32) + expert_mix).astype(BF)
     return (middle, layer_out)
 

time: 202 us -> 184 us (0.911)
  waiting for transfers between devices: 45.1 us -> 25.5 us
  blocking collectives: 89.7 us -> 92.2 us
    ppermute x21 -> x23, waiting for transfers between devices: 37.3 us -> 16.6 us  [shifted(): lax.ppermute(value, axis, [(i, (i + distance) % size) for i in range(size)])]
    all_to_all x3, blocking collectives: 89.7 us -> 92.2 us  [swap(): return lax.all_to_all(value, axes, 0, 0, tiled=True)]
    ppermute x21 -> x23, starting transfers between devices: 33.4 us -> 32.3 us  [shifted(): lax.ppermute(value, axis, [(i, (i + distance) % size) for i in range(size)])]
    pallas_call x8 -> x9, Pallas kernels: 21.8 us -> 21.5 us  [call(): pl.pallas_call(kernel, out_shape=out_shape, compiler_params=pltpu.Compile...]
  transfers between devices with their start and end apart: 22 -> 24, of which waited for: 13 -> 10; matrix products, arithmetic and copies ran while one was open for 0% -> 0% of each run, Pallas kernels for 2% -> 3%
where the time goes in v4:
time: 184 us; the launch traced here: 183 us
  blocking collectives  92.2 us (50%)
  starting transfers between devices  35.7 us (19%)
  waiting for transfers between devices  25.5 us (14%)
  Pallas kernels  21.5 us (12%)
  local copies, waits for them, and re-layouts  5.61 us (3%)
  other arithmetic  1.95 us (1%)
    all_to_all x3, blocking collectives, swap(): return lax.all_to_all(value, axes, 0, 0, tiled=True)  92.2 us
    ppermute x23, starting transfers between devices, shifted(): lax.ppermute(value, axis, [(i, (i + distance) % size) for i in range(size)])  32.3 us
    pallas_call x9, Pallas kernels, call(): pl.pallas_call(kernel, out_shape=out_shape, compiler_params=pltpu.Compile...  21.5 us
    ppermute x23, waiting for transfers between devices, shifted(): lax.ppermute(value, axis, [(i, (i + distance) % size) for i in range(size)])  16.6 us
    all_to_all x1, waiting for transfers between devices, swap(): return lax.all_to_all(value, axes, 0, 0, tiled=True)  8.82 us
    unnamed x30, local copies, waits for them, and re-layouts  5.55 us
  transfers between devices with their start and end apart: 24, of which 10 were waited for; matrix products, arithmetic and copies ran while one was open for 0% of the time, Pallas kernels for 3%

profile of v4, /device:TPU:1, one launch (start us, length us, event | category | flops | bytes accessed | tf_op | source)
XLA Modules:
  0.0 183.4 jit_solution(7194253403156100759)
XLA Ops:
  3.8 5.0 %shard_map.158 = (bf16[8,208,128]{2,1,0:T(8,128)(2,1)S(1)}, f32[4,192,256]{2,1,0:T(8,128)S(1)}) custom-call(bf16[192,256]{1,0:T(8,128)(2,1)S(1)} %copy-done.7, bf16[192,512]{1,0:T(8,128)(2,1)S(1)} %copy-done.6, f32[4,192]{1,0:T(4,128)S(1)} %copy-done.9, f32[4,192]{1,0:T(4,128)S(1)} %copy-done.10), custom_call_target="tpu_custom_call" | custom-call | tf_op jit(solution)/shard_map/pallas_call | solution.py:78
  8.8 22.7 %all_to_all.20.got_ref = bf16[8,208,128]{2,1,0:T(8,128)(2,1)S(1)} all-to-all(bf16[8,208,128]{2,1,0:T(8,128)(2,1)S(1)} %get-tuple-element.22), channel_id=1, replica_groups=mesh['x'=4,'z'=8,'y'=4,'c'=2] {'z'}, dimensions={0} | all-to-all | bytes 851968 | tf_op jit(solution)/shard_map/all_to_all | solution.py:376
  31.5 1.7 shard_map.160
  33.2 2.5 %collective-permute-start.2 = (bf16[208,128]{1,0:T(8,128)(2,1)}, bf16[208,128]{1,0:T(8,128)(2,1)S(1)}, u32[]{:S(2)}, u32[]{:S(2)}) collective-permute-start(bf16[208,128]{1,0:T(8,128)(2,1)} %shard_map.160), channel_id=1, source_target_pairs={{0,192},{64,0},{128,64},{192,128},{1,193},{65,1},{129,65},{193,129... | collective-permute-start | bytes 159752 | tf_op jit(solution)/shard_map/ppermute | solution.py:372
  39.1 1.6 shard_map.159
  41.0 2.9 %shard_map.161 = bf16[8,112,128]{2,1,0:T(8,128)(2,1)} custom-call(s32[1]{0:T(128)} %bitcast.4.here_ref, bf16[8,208,128]{2,1,0:T(8,128)(2,1)S(1)} %all_to_all.20.got_ref, bf16[8,48,128]{2,1,0:T(8,128)(2,1)S(1)} %get-tuple-element.23.route_ref, bf16[208,128]{1,0:T(8,128)(2,1)} %collective-permute-done.rest_0_, ...), custom_call_target="tpu_custom_call" | custom-call | tf_op jit(solution)/shard_map/pallas_call | solution.py:78
  43.9 3.4 %all-to-all-start.1 = ((bf16[8,112,128]{2,1,0:T(8,128)(2,1)}), bf16[8,112,128]{2,1,0:T(8,128)(2,1)S(1)}, u32[]{:S(2)}, u32[]{:S(2)}) async-start(bf16[8,112,128]{2,1,0:T(8,128)(2,1)} %shard_map.161), calls=%async_computation.1 | async-start | bytes 458752 | tf_op jit(solution)/shard_map/all_to_all | solution.py:376
  47.4 8.8 %all-to-all-done.1.state_ref.got_ref = bf16[8,112,128]{2,1,0:T(8,128)(2,1)S(1)} async-done(((bf16[8,112,128]{2,1,0:T(8,128)(2,1)}), bf16[8,112,128]{2,1,0:T(8,128)(2,1)S(1)}, u32[]{:S(2)}, u32[]{:S(2)}) %all-to-all-start.1) | async-done | bytes 229408 | tf_op jit(solution)/shard_map/all_to_all | solution.py:376
  57.7 5.2 %collective-permute-start.3 = (bf16[4,192,256]{2,1,0:T(8,128)(2,1)S(1)}, bf16[4,192,256]{2,1,0:T(8,128)(2,1)S(1)}, u32[]{:S(2)}, u32[]{:S(2)}) collective-permute-start(bf16[4,192,256]{2,1,0:T(8,128)(2,1)S(1)} %get-tuple-element.25), channel_id=1, source_target_pairs={{0,1},{1,0},{2,3},{3,2},{4,5},{5,4},{6,7},{7,6},{8,9},{9,8},{10,11... | collective-permute-start | bytes 1179656 | tf_op jit(solution)/shard_map/ppermute | solution.py:372
  65.7 1.5 collective-permute-start.6
  67.2 1.6 collective-permute-start.5
  69.7 2.7 %collective-permute-done.5 = bf16[192,256]{1,0:T(8,128)(2,1)S(1)} collective-permute-done((bf16[192,256]{1,0:T(8,128)(2,1)S(1)}, bf16[192,256]{1,0:T(8,128)(2,1)S(1)}, u32[]{:S(2)}, u32[]{:S(2)}) %collective-permute-start.5) | collective-permute-done | bytes 98336 | tf_op jit(solution)/shard_map/ppermute | solution.py:372
  73.5 2.4 %collective-permute-start.8 = (bf16[192,256]{1,0:T(8,128)(2,1)S(1)}, bf16[192,256]{1,0:T(8,128)(2,1)S(1)}, u32[]{:S(2)}, u32[]{:S(2)}) collective-permute-start(bf16[192,256]{1,0:T(8,128)(2,1)S(1)} %fusion.4.rest_0_), channel_id=1, source_target_pairs={{0,16},{8,24},{16,32},{24,40},{32,48},{40,56},{48,0},{56,8},{1,17}... | collective-permute-start | bytes 294920 | tf_op jit(solution)/shard_map/ppermute | solution.py:372
  77.3 1.4 collective-permute-done.11.rest_7_
  81.7 1.6 collective-permute-start.10
  83.3 3.6 %shard_map.163 = (bf16[8,512,192]{2,1,0:T(8,128)(2,1)S(1)}, bf16[8,192,512]{2,1,0:T(8,128)(2,1)S(1)}) custom-call(s32[1]{0:T(128)} %bitcast.10.here_ref, bf16[8,112,128]{2,1,0:T(8,128)(2,1)S(1)} %all-to-all-done.1.state_ref.got_ref), custom_call_target="tpu_custom_call" | custom-call | flops 1000000000 | bytes 4000000 | tf_op jit(solution)/shard_map/pallas_call | solution.py:78
  87.8 37.6 %all_to_all.21 = bf16[32,128,256]{2,1,0:T(8,128)(2,1)S(1)} all-to-all(bf16[32,128,256]{2,1,0:T(8,128)(2,1)S(1)} %shard_map.164), channel_id=1, replica_groups=mesh['x'=4,'z'=8,'y'=4,'c'=2] {'x','y','c'}, dimensions={0} | all-to-all | bytes 4194304 | tf_op jit(solution)/shard_map/all_to_all | solution.py:376
  125.4 4.0 %shard_map.165 = bf16[4,8,128,256]{3,2,1,0:T(8,128)(2,1)S(1)} custom-call(bf16[4,8,128,256]{3,2,1,0:T(8,128)(2,1)S(1)} %bitcast.31, f32[1,2048]{1,0:T(1,128)S(1)} %bitcast.36, bf16[2048,512]{1,0:T(8,128)(2,1)S(1)} %bitcast.33, bf16[2048,512]{1,0:T(8,128)(2,1)S(1)} %bitcast.34, bf16[512,2048]{1,0:T(8,128)(2,1)S(1)} %bitcast.35), custom_call_target="tpu_custom_call" | custom-call | tf_op jit(solution)/shard_map/pallas_call | solution.py:78
  129.4 31.9 %all_to_all.22.rows_ref = bf16[32,128,256]{2,1,0:T(8,128)(2,1)S(1)} all-to-all(bf16[32,128,256]{2,1,0:T(8,128)(2,1)S(1)} %bitcast.32), channel_id=1, replica_groups=mesh['x'=4,'z'=8,'y'=4,'c'=2] {'x','y','c'}, dimensions={0} | all-to-all | bytes 4194304 | tf_op jit(solution)/shard_map/all_to_all | solution.py:376
  161.9 2.7 %collective-permute-start.17 = (bf16[192,256]{1,0:T(8,128)(2,1)S(1)}, bf16[192,256]{1,0:T(8,128)(2,1)S(1)}, u32[]{:S(2)}, u32[]{:S(2)}) collective-permute-start(bf16[192,256]{1,0:T(8,128)(2,1)S(1)} %get-tuple-element.32), channel_id=1, source_target_pairs={{0,56},{8,0},{16,8},{24,16},{32,24},{40,32},{48,40},{56,48},{1,57}... | collective-permute-start | bytes 294920 | tf_op jit(solution)/shard_map/ppermute | solution.py:372
  164.6 2.6 %collective-permute-start.18 = (bf16[96,256]{1,0:T(8,128)(2,1)S(1)}, bf16[96,256]{1,0:T(8,128)(2,1)S(1)}, u32[]{:S(2)}, u32[]{:S(2)}) collective-permute-start(bf16[96,256]{1,0:T(8,128)(2,1)S(1)} %get-tuple-element.41), channel_id=1, source_target_pairs={{0,48},{8,56},{16,0},{24,8},{32,16},{40,24},{48,32},{56,40},{1,49}... | collective-permute-start | bytes 147464 | tf_op jit(solution)/shard_map/ppermute | solution.py:372
  170.2 3.1 %collective-permute-start.19 = (bf16[192,256]{1,0:T(8,128)(2,1)S(1)}, bf16[192,256]{1,0:T(8,128)(2,1)S(1)}, u32[]{:S(2)}, u32[]{:S(2)}) collective-permute-start(bf16[192,256]{1,0:T(8,128)(2,1)S(1)} %pad_maximum_fusion), channel_id=1, source_target_pairs={{0,48},{8,56},{16,0},{24,8},{32,16},{40,24},{48,32},{56,40},{1,49}... | collective-permute-start | bytes 294920 | tf_op jit(solution)/shard_map/ppermute | solution.py:372
  173.4 3.0 %collective-permute-done.20 = bf16[192,256]{1,0:T(8,128)(2,1)S(1)} collective-permute-done((bf16[192,256]{1,0:T(8,128)(2,1)S(1)}, bf16[192,256]{1,0:T(8,128)(2,1)S(1)}, u32[]{:S(2)}, u32[]{:S(2)}) %collective-permute-start.20) | collective-permute-done | bytes 98336 | tf_op jit(solution)/shard_map/ppermute | solution.py:372
  176.6 6.0 %collective-permute-done.22 = bf16[192,256]{1,0:T(8,128)(2,1)S(1)} collective-permute-done((bf16[192,256]{1,0:T(8,128)(2,1)S(1)}, bf16[192,256]{1,0:T(8,128)(2,1)S(1)}, u32[]{:S(2)}, u32[]{:S(2)}) %collective-permute-start.22) | collective-permute-done | bytes 98336 | tf_op jit(solution)/shard_map/ppermute | solution.py:372
  (82 shorter events, 22.9 us)
Async XLA Ops:
  33.2 7.6 %collective-permute-start.2 = (bf16[208,128]{1,0:T(8,128)(2,1)}, bf16[208,128]{1,0:T(8,128)(2,1)S(1)}, u32[]{:S(2)}, u32[]{:S(2)}) collective-permute-start(bf16[208,128]{1,0:T(8,128)(2,1)} %shard_map.160), channel_id=1, source_target_pairs={{0,192},{64,0},{128,64},{192,128},{1,193},{65,1},{129,65},{193,129... | collective-permute-start | bytes 159752 | tf_op jit(solution)/shard_map/ppermute | solution.py:372
  35.6 5.1 %collective-permute-start.1 = (bf16[208,128]{1,0:T(8,128)(2,1)}, bf16[208,128]{1,0:T(8,128)(2,1)S(1)}, u32[]{:S(2)}, u32[]{:S(2)}) collective-permute-start(bf16[208,128]{1,0:T(8,128)(2,1)} %shard_map.160), channel_id=1, source_target_pairs={{0,128},{64,192},{128,0},{192,64},{1,129},{65,193},{129,1},{193,65... | collective-permute-start | bytes 159752 | tf_op jit(solution)/shard_map/ppermute | solution.py:372
  36.2 4.9 %collective-permute-start = (bf16[208,128]{1,0:T(8,128)(2,1)}, bf16[208,128]{1,0:T(8,128)(2,1)}, u32[]{:S(2)}, u32[]{:S(2)}) collective-permute-start(bf16[208,128]{1,0:T(8,128)(2,1)} %shard_map.160), channel_id=1, source_target_pairs={{0,64},{64,128},{128,192},{192,0},{1,65},{65,129},{129,193},{193,1... | collective-permute-start | bytes 159752 | tf_op jit(solution)/shard_map/ppermute | solution.py:372
  43.9 12.3 %all-to-all-start.1 = ((bf16[8,112,128]{2,1,0:T(8,128)(2,1)}), bf16[8,112,128]{2,1,0:T(8,128)(2,1)S(1)}, u32[]{:S(2)}, u32[]{:S(2)}) async-start(bf16[8,112,128]{2,1,0:T(8,128)(2,1)} %shard_map.161), calls=%async_computation.1 | async-start | bytes 458752 | tf_op jit(solution)/shard_map/all_to_all | solution.py:376
  57.7 6.5 %collective-permute-start.3 = (bf16[4,192,256]{2,1,0:T(8,128)(2,1)S(1)}, bf16[4,192,256]{2,1,0:T(8,128)(2,1)S(1)}, u32[]{:S(2)}, u32[]{:S(2)}) collective-permute-start(bf16[4,192,256]{2,1,0:T(8,128)(2,1)S(1)} %get-tuple-element.25), channel_id=1, source_target_pairs={{0,1},{1,0},{2,3},{3,2},{4,5},{5,4},{6,7},{7,6},{8,9},{9,8},{10,11... | collective-permute-start | bytes 1179656 | tf_op jit(solution)/shard_map/ppermute | solution.py:372
  64.4 5.4 %collective-permute-start.4 = (bf16[192,256]{1,0:T(8,128)(2,1)S(1)}, bf16[192,256]{1,0:T(8,128)(2,1)S(1)}, u32[]{:S(2)}, u32[]{:S(2)}) collective-permute-start(bf16[192,256]{1,0:T(8,128)(2,1)S(1)} %get-tuple-element.38), channel_id=1, source_target_pairs={{0,2},{2,4},{4,6},{6,0},{1,3},{3,5},{5,7},{7,1},{8,10},{10,12},{12... | collective-permute-start | bytes 294920 | tf_op jit(solution)/shard_map/ppermute | solution.py:372
  65.7 4.0 %collective-permute-start.6 = (bf16[192,256]{1,0:T(8,128)(2,1)S(1)}, bf16[192,256]{1,0:T(8,128)(2,1)S(1)}, u32[]{:S(2)}, u32[]{:S(2)}) collective-permute-start(bf16[192,256]{1,0:T(8,128)(2,1)S(1)} %get-tuple-element.39), channel_id=1, source_target_pairs={{0,6},{2,0},{4,2},{6,4},{1,7},{3,1},{5,3},{7,5},{8,14},{10,8},{12,... | collective-permute-start | bytes 294920 | tf_op jit(solution)/shard_map/ppermute | solution.py:372
  67.2 5.2 %collective-permute-start.5 = (bf16[192,256]{1,0:T(8,128)(2,1)S(1)}, bf16[192,256]{1,0:T(8,128)(2,1)S(1)}, u32[]{:S(2)}, u32[]{:S(2)}) collective-permute-start(bf16[192,256]{1,0:T(8,128)(2,1)S(1)} %get-tuple-element.40), channel_id=1, source_target_pairs={{0,4},{2,6},{4,0},{6,2},{1,5},{3,7},{5,1},{7,3},{8,12},{10,14},{12... | collective-permute-start | bytes 294920 | tf_op jit(solution)/shard_map/ppermute | solution.py:372
  73.4 5.4 %collective-permute-start.11 = (bf16[192,256]{1,0:T(8,128)(2,1)S(1)}, bf16[192,256]{1,0:T(8,128)(2,1)S(1)}, u32[]{:S(2)}, u32[]{:S(2)}) collective-permute-start(bf16[192,256]{1,0:T(8,128)(2,1)S(1)} %fusion.4.rest_0_), channel_id=1, source_target_pairs={{0,48},{8,56},{16,0},{24,8},{32,16},{40,24},{48,32},{56,40},{1,49}... | collective-permute-start | bytes 294920 | tf_op jit(solution)/shard_map/ppermute | solution.py:372
  73.5 6.1 %collective-permute-start.8 = (bf16[192,256]{1,0:T(8,128)(2,1)S(1)}, bf16[192,256]{1,0:T(8,128)(2,1)S(1)}, u32[]{:S(2)}, u32[]{:S(2)}) collective-permute-start(bf16[192,256]{1,0:T(8,128)(2,1)S(1)} %fusion.4.rest_0_), channel_id=1, source_target_pairs={{0,16},{8,24},{16,32},{24,40},{32,48},{40,56},{48,0},{56,8},{1,17}... | collective-permute-start | bytes 294920 | tf_op jit(solution)/shard_map/ppermute | solution.py:372
  75.8 5.9 %collective-permute-start.14 = (bf16[192,256]{1,0:T(8,128)(2,1)S(1)}, bf16[192,256]{1,0:T(8,128)(2,1)S(1)}, u32[]{:S(2)}, u32[]{:S(2)}) collective-permute-start(bf16[192,256]{1,0:T(8,128)(2,1)S(1)} %fusion.4.rest_0_), channel_id=1, source_target_pairs={{0,56},{8,0},{16,8},{24,16},{32,24},{40,32},{48,40},{56,48},{1,57}... | collective-permute-start | bytes 294920 | tf_op jit(solution)/shard_map/ppermute | solution.py:372
  76.6 10.3 %collective-permute-start.7 = (bf16[192,256]{1,0:T(8,128)(2,1)S(1)}, bf16[192,256]{1,0:T(8,128)(2,1)S(1)}, u32[]{:S(2)}, u32[]{:S(2)}) collective-permute-start(bf16[192,256]{1,0:T(8,128)(2,1)S(1)} %fusion.4.rest_0_), channel_id=1, source_target_pairs={{0,8},{8,16},{16,24},{24,32},{32,40},{40,48},{48,56},{56,0},{1,9},... | collective-permute-start | bytes 294920 | tf_op jit(solution)/shard_map/ppermute | solution.py:372
  78.7 8.2 %collective-permute-start.13 = (bf16[192,256]{1,0:T(8,128)(2,1)S(1)}, bf16[192,256]{1,0:T(8,128)(2,1)S(1)}, u32[]{:S(2)}, u32[]{:S(2)}) collective-permute-start(bf16[192,256]{1,0:T(8,128)(2,1)S(1)} %collective-permute-done.11.rest_7_), channel_id=1, source_target_pairs={{0,56},{8,0},{16,8},{24,16},{32,24},{40,32},{48,40},{56,48},{1,57}... | collective-permute-start | bytes 294920 | tf_op jit(solution)/shard_map/ppermute | solution.py:372
  79.6 7.4 %collective-permute-start.9 = (bf16[192,256]{1,0:T(8,128)(2,1)S(1)}, bf16[192,256]{1,0:T(8,128)(2,1)S(1)}, u32[]{:S(2)}, u32[]{:S(2)}) collective-permute-start(bf16[192,256]{1,0:T(8,128)(2,1)S(1)} %collective-permute-done.8.rest_2_), channel_id=1, source_target_pairs={{0,8},{8,16},{16,24},{24,32},{32,40},{40,48},{48,56},{56,0},{1,9},... | collective-permute-start | bytes 294920 | tf_op jit(solution)/shard_map/ppermute | solution.py:372
  80.9 6.1 %collective-permute-start.12 = (bf16[96,256]{1,0:T(8,128)(2,1)S(1)}, bf16[96,256]{1,0:T(8,128)(2,1)S(1)}, u32[]{:S(2)}, u32[]{:S(2)}) collective-permute-start(bf16[96,256]{1,0:T(8,128)(2,1)S(1)} %slice.58), channel_id=1, source_target_pairs={{0,48},{8,56},{16,0},{24,8},{32,16},{40,24},{48,32},{56,40},{1,49}... | collective-permute-start | bytes 147464 | tf_op jit(solution)/shard_map/ppermute | solution.py:372
  81.7 5.3 %collective-permute-start.10 = (bf16[96,256]{1,0:T(8,128)(2,1)S(1)}, bf16[96,256]{1,0:T(8,128)(2,1)S(1)}, u32[]{:S(2)}, u32[]{:S(2)}) collective-permute-start(bf16[96,256]{1,0:T(8,128)(2,1)S(1)} %slice.57), channel_id=1, source_target_pairs={{0,16},{8,24},{16,32},{24,40},{32,48},{40,56},{48,0},{56,8},{1,17}... | collective-permute-start | bytes 147464 | tf_op jit(solution)/shard_map/ppermute | solution.py:372
  161.9 6.8 %collective-permute-start.17 = (bf16[192,256]{1,0:T(8,128)(2,1)S(1)}, bf16[192,256]{1,0:T(8,128)(2,1)S(1)}, u32[]{:S(2)}, u32[]{:S(2)}) collective-permute-start(bf16[192,256]{1,0:T(8,128)(2,1)S(1)} %get-tuple-element.32), channel_id=1, source_target_pairs={{0,56},{8,0},{16,8},{24,16},{32,24},{40,32},{48,40},{56,48},{1,57}... | collective-permute-start | bytes 294920 | tf_op jit(solution)/shard_map/ppermute | solution.py:372
  164.6 5.6 %collective-permute-start.18 = (bf16[96,256]{1,0:T(8,128)(2,1)S(1)}, bf16[96,256]{1,0:T(8,128)(2,1)S(1)}, u32[]{:S(2)}, u32[]{:S(2)}) collective-permute-start(bf16[96,256]{1,0:T(8,128)(2,1)S(1)} %get-tuple-element.41), channel_id=1, source_target_pairs={{0,48},{8,56},{16,0},{24,8},{32,16},{40,24},{48,32},{56,40},{1,49}... | collective-permute-start | bytes 147464 | tf_op jit(solution)/shard_map/ppermute | solution.py:372
  167.1 9.3 %collective-permute-start.21 = (bf16[96,256]{1,0:T(8,128)(2,1)S(1)}, bf16[96,256]{1,0:T(8,128)(2,1)S(1)}, u32[]{:S(2)}, u32[]{:S(2)}) collective-permute-start(bf16[96,256]{1,0:T(8,128)(2,1)S(1)} %get-tuple-element.42), channel_id=1, source_target_pairs={{0,16},{8,24},{16,32},{24,40},{32,48},{40,56},{48,0},{56,8},{1,17}... | collective-permute-start | bytes 147464 | tf_op jit(solution)/shard_map/ppermute | solution.py:372
  167.2 9.4 %collective-permute-start.15 = (bf16[192,256]{1,0:T(8,128)(2,1)S(1)}, bf16[192,256]{1,0:T(8,128)(2,1)S(1)}, u32[]{:S(2)}, u32[]{:S(2)}) collective-permute-start(bf16[192,256]{1,0:T(8,128)(2,1)S(1)} %get-tuple-element.29), channel_id=1, source_target_pairs={{0,56},{8,0},{16,8},{24,16},{32,24},{40,32},{48,40},{56,48},{1,57}... | collective-permute-start | bytes 294920 | tf_op jit(solution)/shard_map/ppermute | solution.py:372
  168.2 8.3 %collective-permute-start.16 = (bf16[192,256]{1,0:T(8,128)(2,1)S(1)}, bf16[192,256]{1,0:T(8,128)(2,1)S(1)}, u32[]{:S(2)}, u32[]{:S(2)}) collective-permute-start(bf16[192,256]{1,0:T(8,128)(2,1)S(1)} %get-tuple-element.30), channel_id=1, source_target_pairs={{0,8},{8,16},{16,24},{24,32},{32,40},{40,48},{48,56},{56,0},{1,9},... | collective-permute-start | bytes 294920 | tf_op jit(solution)/shard_map/ppermute | solution.py:372
  168.6 7.8 %collective-permute-start.20 = (bf16[192,256]{1,0:T(8,128)(2,1)S(1)}, bf16[192,256]{1,0:T(8,128)(2,1)S(1)}, u32[]{:S(2)}, u32[]{:S(2)}) collective-permute-start(bf16[192,256]{1,0:T(8,128)(2,1)S(1)} %get-tuple-element.35), channel_id=1, source_target_pairs={{0,8},{8,16},{16,24},{24,32},{32,40},{40,48},{48,56},{56,0},{1,9},... | collective-permute-start | bytes 294920 | tf_op jit(solution)/shard_map/ppermute | solution.py:372
  170.2 6.4 %collective-permute-start.19 = (bf16[192,256]{1,0:T(8,128)(2,1)S(1)}, bf16[192,256]{1,0:T(8,128)(2,1)S(1)}, u32[]{:S(2)}, u32[]{:S(2)}) collective-permute-start(bf16[192,256]{1,0:T(8,128)(2,1)S(1)} %pad_maximum_fusion), channel_id=1, source_target_pairs={{0,48},{8,56},{16,0},{24,8},{32,16},{40,24},{48,32},{56,40},{1,49}... | collective-permute-start | bytes 294920 | tf_op jit(solution)/shard_map/ppermute | solution.py:372
  176.5 6.2 %collective-permute-start.22 = (bf16[192,256]{1,0:T(8,128)(2,1)S(1)}, bf16[192,256]{1,0:T(8,128)(2,1)S(1)}, u32[]{:S(2)}, u32[]{:S(2)}) collective-permute-start(bf16[192,256]{1,0:T(8,128)(2,1)S(1)} %pad_maximum_fusion.1), channel_id=1, source_target_pairs={{0,16},{8,24},{16,32},{24,40},{32,48},{40,56},{48,0},{56,8},{1,17}... | collective-permute-start | bytes 294920 | tf_op jit(solution)/shard_map/ppermute | solution.py:372
  (15 other events, 317.5 us)

commit v5 on v4

--- a/solution.py
+++ b/solution.py
@@ -228,7 +228,8 @@
         )
 
 
-def total_kernel(got_ref, total_ref):
+def total_kernel(got_ref, after_ref, total_ref):
+    del after_ref
     blocks = got_ref.shape[0]
     rows = total_ref.shape[0] - DK - MARKS
     row = lax.broadcasted_iota(jnp.int32, (DK, DK), 0)
@@ -268,7 +269,7 @@
 
 
 def output_kernel(
-    here_ref, inside_ref, reach_ref, state_ref, gate_ref, gain_ref, proj_ref, keep_ref, give_ref
+    here_ref, inside_ref, reach_ref, state_ref, gate_ref, gain_ref, proj_ref, rest_ref, keep_ref, give_ref
 ):
     heads = inside_ref.shape[0]
     gated = []
@@ -284,10 +285,12 @@
     gated = jnp.concatenate(gated, axis=1)
     columns, _, width = keep_ref.shape
     for distance in range(columns):
-        column = lax.rem(here_ref[0] + distance, columns)
-        for core, out_ref in ((here_ref[1], keep_ref), (1 - here_ref[1], give_ref)):
+        column = lax.rem(here_ref[2] + distance, columns)
+        for core, out_ref in ((here_ref[3], keep_ref), (1 - here_ref[3], give_ref)):
             first = pl.multiple_of((column * 2 + core) * width, width)
             mixed = mm(gated, proj_ref[:, pl.ds(first, width)])
+            if distance == 0 and out_ref is keep_ref:
+                mixed = mixed + rest_ref[:, pl.ds(first, width)].astype(F32)
             out_ref[distance] = mixed.astype(out_ref.dtype)
 
 
@@ -304,7 +307,7 @@
     slot = (iota((length, slots), 1) % SLOTS).astype(F32)
     slot_t = (iota((slots, length), 0) % SLOTS).astype(F32)
     for block in range(blocks):
-        source = lax.rem(here_ref[0] + blocks - block, blocks)
+        source = lax.rem(here_ref[1] + blocks - block, blocks)
         first = got_ref[source, base : base + targets, :]
         last = got_ref[source, base + targets :, :]
         rest = length - DK
@@ -323,14 +326,8 @@
     tokens, send_ref = rest[:-1], rest[-1]
     targets = send_ref.shape[0]
     width = send_ref.shape[2]
-    blocks = pick_ref.shape[0]
-    far = blocks // 2
-    for block in range(blocks):
-        place = block if block <= far else block + 1
-        token = tokens[place][...]
-        if block == far:
-            token = jnp.concatenate([token, tokens[place + 1][...]], axis=0)
-        rows = mm(pick_ref[block], token).astype(BF)
+    for block in range(pick_ref.shape[0]):
+        rows = mm(pick_ref[block], tokens[block][...]).astype(BF)
         send_ref[:, block * SLOTS : (block + 1) * SLOTS, :] = rows.reshape(targets, SLOTS, width)
 
 
@@ -365,6 +362,8 @@
 
 SCALAR = pl.BlockSpec(memory_space=pltpu.SMEM)
 VECTOR = pl.BlockSpec(memory_space=pltpu.VMEM)
+UNREAD = pl.BlockSpec(memory_space=pl.ANY)
+REMOTE = pl.BlockSpec(memory_space=pltpu.HBM)
 
 
 def shifted(value, axis, distance):
@@ -377,26 +376,20 @@
 
 
 def spread_out(value, axis):
-    half = value.shape[0] // 2
     right = [value, shifted(value, axis, 1), shifted(value, axis, 2)]
     left = [shifted(value, axis, -1), shifted(value, axis, -2)]
     right.append(shifted(right[2], axis, 1))
     left.append(shifted(left[1], axis, -1))
-    far = [shifted(right[2][:half], axis, 2), shifted(left[1][half:], axis, -2)]
-    return right + far + left[::-1]
+    right.append(shifted(right[2], axis, 2))
+    return right + left[::-1]
 
 
 def gathered_sum(parts, axis):
     def passed(value, distance):
         return shifted(value.astype(BF), axis, distance).astype(F32)
 
-    half = parts[4].shape[0] // 2
-    first = passed(parts[4][:half], -2)
-    last = passed(parts[4][half:], 2)
-    left = parts[2] + passed(parts[3], -1)
+    left = parts[2] + passed(parts[3], -1) + passed(parts[4], -2)
     right = parts[6] + passed(parts[5], 1)
-    left = jnp.concatenate([left[:half] + first, left[half:]], axis=0)
-    right = jnp.concatenate([right[:half], right[half:] + last], axis=0)
     near = passed(parts[1], -1) + passed(parts[7], 1)
     return parts[0] + near + (passed(left, -2) + passed(right, 2))
 
@@ -423,7 +416,6 @@
     blocks = lax.axis_size("z")
     groups = lax.axis_size("x")
     shares = lax.axis_size("y") * lax.axis_size("c")
-    share = lax.axis_index(("y", "c"))
     width = residual_in.shape[1] // shares
     count = blocks * SLOTS
     targets = groups * shares
@@ -431,6 +423,7 @@
 
     rows = heads * DV // blocks
     extra = targets + targets // 2
+    here = jnp.stack([lax.axis_index(axis) for axis in ("x", "z", "y", "c")])
     operands = (key_in, value_in, decay_rate, beta_logit)
     send, solved = call(
         solve_kernel,
@@ -439,8 +432,8 @@
             shape((heads, length, DV + DK), F32),
         ),
         *operands,
-        vmem=24,
-        in_specs=[pl.BlockSpec(memory_space=pltpu.HBM)] * len(operands),
+        vmem=62,
+        in_specs=[REMOTE] * len(operands),
         scratch_shapes=[pltpu.VMEM(item.shape, item.dtype) for item in operands]
         + [pltpu.SemaphoreType.DMA((len(operands),))],
     )
@@ -463,12 +456,19 @@
         flops=2 * 10**9,
         moved=3 * 10**6,
     )
-    total = call(total_kernel, shape((DK + rows + MARKS, DK), BF), got, vmem=8)
+    total = call(
+        total_kernel,
+        shape((DK + rows + MARKS, DK), BF),
+        got,
+        route,
+        vmem=8,
+        in_specs=[VECTOR, UNREAD],
+    )
     totals = [shifted(total, "x", distance) for distance in range(1, groups)]
     enter = call(
         state_kernel,
         shape((blocks, rows + extra, DK), BF),
-        lax.axis_index("x").reshape(1),
+        here,
         got,
         route,
         *totals,
@@ -482,7 +482,7 @@
             shape((blocks, targets * SLOTS, length), BF),
             shape((blocks, length, targets * SLOTS), BF),
         ),
-        lax.axis_index("z").reshape(1),
+        here,
         back,
         vmem=12,
         flops=10**9,
@@ -490,7 +490,6 @@
         in_specs=[SCALAR, VECTOR],
     )
 
-    here = jnp.stack([lax.axis_index("y"), lax.axis_index("c")])
     columns = lax.axis_size("y")
     keep, give = call(
         output_kernel,
@@ -502,15 +501,15 @@
         gate_in,
         head_gain.reshape(1, DV),
         out_proj,
+        residual_in,
         vmem=16,
-        in_specs=[SCALAR] + [VECTOR] * 6,
+        in_specs=[SCALAR] + [VECTOR] * 7,
     )
     both = keep + shifted(give, "c", 1).astype(F32)
     mixed = both[0]
     for distance in range(1, columns):
         mixed = mixed + shifted(both[distance].astype(BF), "y", distance).astype(F32)
-    residual = lax.dynamic_slice_in_dim(residual_in, share * width, width, 1)
-    middle = (residual.astype(F32) + mixed).astype(BF)
+    middle = mixed.astype(BF)
 
     tokens = spread_out(middle, "z")
     send = call(pick_kernel, shape((targets, count, width), BF), pick, *tokens, vmem=12)

time: 184 us -> 177 us (0.962)
  blocking collectives: 92.2 us -> 80.6 us
  waiting for transfers between devices: 25.5 us -> 29.6 us
  starting transfers between devices: 35.7 us -> 33.6 us
    all_to_all x3, blocking collectives: 92.2 us -> 80.6 us  [swap(): return lax.all_to_all(value, axes, 0, 0, tiled=True)]
    ppermute x23 -> x21, starting transfers between devices: 32.3 us -> 24.6 us  [shifted(): lax.ppermute(value, axis, [(i, (i + distance) % size) for i in range(size)])]
    ppermute x23 -> x21, waiting for transfers between devices: 16.6 us -> 23.3 us  [shifted(): lax.ppermute(value, axis, [(i, (i + distance) % size) for i in range(size)])]
    all_to_all x1, starting transfers between devices: 3.4 us -> 9.03 us  [swap(): return lax.all_to_all(value, axes, 0, 0, tiled=True)]
    all_to_all x1, waiting for transfers between devices: 8.82 us -> 6.3 us  [swap(): return lax.all_to_all(value, axes, 0, 0, tiled=True)]
    unnamed x30 -> x40, local copies, waits for them, and re-layouts: 5.55 us -> 7.17 us
  transfers between devices with their start and end apart: 24 -> 22, of which waited for: 10 -> 14; matrix products, arithmetic and copies ran while one was open for 0% -> 0% of each run, Pallas kernels for 3% -> 3%
where the time goes in v5:
time: 177 us; the launch traced here: 175 us
  blocking collectives  80.6 us (46%)
  starting transfers between devices  33.6 us (19%)
  waiting for transfers between devices  29.6 us (17%)
  Pallas kernels  21.8 us (12%)
  local copies, waits for them, and re-layouts  7.19 us (4%)
    all_to_all x3, blocking collectives, swap(): return lax.all_to_all(value, axes, 0, 0, tiled=True)  80.6 us
    ppermute x21, starting transfers between devices, shifted(): lax.ppermute(value, axis, [(i, (i + distance) % size) for i in range(size)])  24.6 us
    ppermute x21, waiting for transfers between devices, shifted(): lax.ppermute(value, axis, [(i, (i + distance) % size) for i in range(size)])  23.3 us
    pallas_call x9, Pallas kernels, call(): pl.pallas_call(kernel, out_shape=out_shape, compiler_params=pltpu.Compile...  21.8 us
    all_to_all x1, starting transfers between devices, swap(): return lax.all_to_all(value, axes, 0, 0, tiled=True)  9.03 us
    unnamed x40, local copies, waits for them, and re-layouts  7.17 us
    all_to_all x1, waiting for transfers between devices, swap(): return lax.all_to_all(value, axes, 0, 0, tiled=True)  6.3 us
  transfers between devices with their start and end apart: 22, of which 14 were waited for; matrix products, arithmetic and copies ran while one was open for 0% of the time, Pallas kernels for 3%

profile of v5, /device:TPU:1, one launch (start us, length us, event | category | flops | bytes accessed | tf_op | source)
XLA Modules:
  0.0 174.7 jit_solution(12343918171086990223)
XLA Ops:
  0.6 6.4 %shard_map.158 = (bf16[8,208,128]{2,1,0:T(8,128)(2,1)}, f32[4,192,256]{2,1,0:T(8,128)}) custom-call(bf16[192,256]{1,0:T(8,128)(2,1)} %k_ref.1, bf16[192,512]{1,0:T(8,128)(2,1)} %refs_1_.1, f32[4,192]{1,0:T(4,128)} %decay_ref.1, f32[4,192]{1,0:T(4,128)} %logit_ref.1), custom_call_target="tpu_custom_call" | custom-call | tf_op jit(solution)/shard_map/pallas_call | solution.py:78
  7.0 9.0 %all-to-all-start = ((bf16[8,208,128]{2,1,0:T(8,128)(2,1)}), bf16[8,208,128]{2,1,0:T(8,128)(2,1)S(1)}, u32[]{:S(2)}, u32[]{:S(2)}) async-start(bf16[8,208,128]{2,1,0:T(8,128)(2,1)} %get-tuple-element.22), calls=%async_computation | async-start | bytes 851968 | tf_op jit(solution)/shard_map/all_to_all | solution.py:375
  21.8 1.6 shard_map.159
  24.8 6.3 %all-to-all-done.got_ref = bf16[8,208,128]{2,1,0:T(8,128)(2,1)S(1)} async-done(((bf16[8,208,128]{2,1,0:T(8,128)(2,1)}), bf16[8,208,128]{2,1,0:T(8,128)(2,1)S(1)}, u32[]{:S(2)}, u32[]{:S(2)}) %all-to-all-start) | async-done | bytes 426016 | tf_op jit(solution)/shard_map/all_to_all | solution.py:375
  32.2 2.6 %collective-permute-start.2 = (bf16[208,128]{1,0:T(8,128)(2,1)S(1)}, bf16[208,128]{1,0:T(8,128)(2,1)S(1)}, u32[]{:S(2)}, u32[]{:S(2)}) collective-permute-start(bf16[208,128]{1,0:T(8,128)(2,1)S(1)} %shard_map.160), channel_id=1, source_target_pairs={{0,192},{64,0},{128,64},{192,128},{1,193},{65,1},{129,65},{193,129... | collective-permute-start | bytes 159752 | tf_op jit(solution)/shard_map/ppermute | solution.py:371
  36.0 3.3 %collective-permute-done.1.rest_1_ = bf16[208,128]{1,0:T(8,128)(2,1)S(1)} collective-permute-done((bf16[208,128]{1,0:T(8,128)(2,1)S(1)}, bf16[208,128]{1,0:T(8,128)(2,1)S(1)}, u32[]{:S(2)}, u32[]{:S(2)}) %collective-permute-start.1) | collective-permute-done | bytes 53280 | tf_op jit(solution)/shard_map/ppermute | solution.py:371
  39.8 1.9 %shard_map.161 = bf16[8,112,128]{2,1,0:T(8,128)(2,1)S(1)} custom-call(s32[4]{0:T(128)S(1)} %pad_add_fusion.here_ref, bf16[8,208,128]{2,1,0:T(8,128)(2,1)S(1)} %all-to-all-done.got_ref, bf16[8,48,128]{2,1,0:T(8,128)(2,1)S(1)} %get-tuple-element.23.after_ref.route_ref, bf16[208,128]{1,0:T(8,128)(2,1)S(1)} %collective-permute-done.rest_0_, ...), custom_call_target="tpu_custom_call" | custom-call | tf_op jit(solution)/shard_map/pallas_call | solution.py:78
  41.8 11.4 %all_to_all.20.state_ref.got_ref = bf16[8,112,128]{2,1,0:T(8,128)(2,1)S(1)} all-to-all(bf16[8,112,128]{2,1,0:T(8,128)(2,1)S(1)} %shard_map.161), channel_id=1, replica_groups=mesh['x'=4,'z'=8,'y'=4,'c'=2] {'z'}, dimensions={0} | all-to-all | bytes 458752 | tf_op jit(solution)/shard_map/all_to_all | solution.py:375
  54.7 3.9 %collective-permute-start.3 = (bf16[4,192,256]{2,1,0:T(8,128)(2,1)S(1)}, bf16[4,192,256]{2,1,0:T(8,128)(2,1)S(1)}, u32[]{:S(2)}, u32[]{:S(2)}) collective-permute-start(bf16[4,192,256]{2,1,0:T(8,128)(2,1)S(1)} %get-tuple-element.25), channel_id=1, source_target_pairs={{0,1},{1,0},{2,3},{3,2},{4,5},{5,4},{6,7},{7,6},{8,9},{9,8},{10,11... | collective-permute-start | bytes 1179656 | tf_op jit(solution)/shard_map/ppermute | solution.py:371
  61.4 1.5 collective-permute-start.6
  62.9 1.6 collective-permute-start.5
  65.4 2.7 %collective-permute-done.5 = bf16[192,256]{1,0:T(8,128)(2,1)S(1)} collective-permute-done((bf16[192,256]{1,0:T(8,128)(2,1)S(1)}, bf16[192,256]{1,0:T(8,128)(2,1)S(1)}, u32[]{:S(2)}, u32[]{:S(2)}) %collective-permute-start.5) | collective-permute-done | bytes 98336 | tf_op jit(solution)/shard_map/ppermute | solution.py:371
  68.3 2.4 %collective-permute-start.8 = (bf16[192,256]{1,0:T(8,128)(2,1)S(1)}, bf16[192,256]{1,0:T(8,128)(2,1)S(1)}, u32[]{:S(2)}, u32[]{:S(2)}) collective-permute-start(bf16[192,256]{1,0:T(8,128)(2,1)S(1)} %fusion.3.rest_0_), channel_id=1, source_target_pairs={{0,16},{8,24},{16,32},{24,40},{32,48},{40,56},{48,0},{56,8},{1,17}... | collective-permute-start | bytes 294920 | tf_op jit(solution)/shard_map/ppermute | solution.py:371
  72.1 1.7 collective-permute-done.11.rest_6_
  75.1 1.6 collective-permute-start.9
  76.7 4.1 %shard_map.163 = (bf16[8,512,192]{2,1,0:T(8,128)(2,1)S(1)}, bf16[8,192,512]{2,1,0:T(8,128)(2,1)S(1)}) custom-call(s32[4]{0:T(128)S(1)} %pad_add_fusion.here_ref, bf16[8,112,128]{2,1,0:T(8,128)(2,1)S(1)} %all_to_all.20.state_ref.got_ref), custom_call_target="tpu_custom_call" | custom-call | flops 1000000000 | bytes 4000000 | tf_op jit(solution)/shard_map/pallas_call | solution.py:78
  80.9 1.7 collective-permute-done.9.rest_3_
  83.4 37.3 %all_to_all.21 = bf16[32,128,256]{2,1,0:T(8,128)(2,1)S(1)} all-to-all(bf16[32,128,256]{2,1,0:T(8,128)(2,1)S(1)} %shard_map.164), channel_id=1, replica_groups=mesh['x'=4,'z'=8,'y'=4,'c'=2] {'x','y','c'}, dimensions={0} | all-to-all | bytes 4194304 | tf_op jit(solution)/shard_map/all_to_all | solution.py:375
  120.7 3.9 %shard_map.165 = bf16[4,8,128,256]{3,2,1,0:T(8,128)(2,1)S(1)} custom-call(bf16[4,8,128,256]{3,2,1,0:T(8,128)(2,1)S(1)} %bitcast.29, f32[1,2048]{1,0:T(1,128)S(1)} %bitcast.34, bf16[2048,512]{1,0:T(8,128)(2,1)S(1)} %bitcast.31, bf16[2048,512]{1,0:T(8,128)(2,1)S(1)} %bitcast.32, bf16[512,2048]{1,0:T(8,128)(2,1)S(1)} %bitcast.33), custom_call_target="tpu_custom_call" | custom-call | tf_op jit(solution)/shard_map/pallas_call | solution.py:78
  124.7 31.9 %all_to_all.22.rows_ref = bf16[32,128,256]{2,1,0:T(8,128)(2,1)S(1)} all-to-all(bf16[32,128,256]{2,1,0:T(8,128)(2,1)S(1)} %bitcast.30), channel_id=1, replica_groups=mesh['x'=4,'z'=8,'y'=4,'c'=2] {'x','y','c'}, dimensions={0} | all-to-all | bytes 4194304 | tf_op jit(solution)/shard_map/all_to_all | solution.py:375
  157.5 1.8 %collective-permute-start.17 = (bf16[192,256]{1,0:T(8,128)(2,1)S(1)}, bf16[192,256]{1,0:T(8,128)(2,1)S(1)}, u32[]{:S(2)}, u32[]{:S(2)}) collective-permute-start(bf16[192,256]{1,0:T(8,128)(2,1)S(1)} %get-tuple-element.33), channel_id=1, source_target_pairs={{0,48},{8,56},{16,0},{24,8},{32,16},{40,24},{48,32},{56,40},{1,49}... | collective-permute-start | bytes 294920 | tf_op jit(solution)/shard_map/ppermute | solution.py:371
  161.6 3.0 %collective-permute-done.17 = bf16[192,256]{1,0:T(8,128)(2,1)S(1)} collective-permute-done((bf16[192,256]{1,0:T(8,128)(2,1)S(1)}, bf16[192,256]{1,0:T(8,128)(2,1)S(1)}, u32[]{:S(2)}, u32[]{:S(2)}) %collective-permute-start.17) | collective-permute-done | bytes 98336 | tf_op jit(solution)/shard_map/ppermute | solution.py:371
  164.7 2.0 %collective-permute-start.18 = (bf16[192,256]{1,0:T(8,128)(2,1)S(1)}, bf16[192,256]{1,0:T(8,128)(2,1)S(1)}, u32[]{:S(2)}, u32[]{:S(2)}) collective-permute-start(bf16[192,256]{1,0:T(8,128)(2,1)S(1)} %add_convert_fusion.2), channel_id=1, source_target_pairs={{0,48},{8,56},{16,0},{24,8},{32,16},{40,24},{48,32},{56,40},{1,49}... | collective-permute-start | bytes 294920 | tf_op jit(solution)/shard_map/ppermute | solution.py:371
  169.2 4.8 %collective-permute-done.20 = bf16[192,256]{1,0:T(8,128)(2,1)S(1)} collective-permute-done((bf16[192,256]{1,0:T(8,128)(2,1)S(1)}, bf16[192,256]{1,0:T(8,128)(2,1)S(1)}, u32[]{:S(2)}, u32[]{:S(2)}) %collective-permute-start.20) | collective-permute-done | bytes 98336 | tf_op jit(solution)/shard_map/ppermute | solution.py:371
  (79 shorter events, 25.3 us)
Async XLA Ops:
  7.0 24.1 %all-to-all-start = ((bf16[8,208,128]{2,1,0:T(8,128)(2,1)}), bf16[8,208,128]{2,1,0:T(8,128)(2,1)S(1)}, u32[]{:S(2)}, u32[]{:S(2)}) async-start(bf16[8,208,128]{2,1,0:T(8,128)(2,1)} %get-tuple-element.22), calls=%async_computation | async-start | bytes 851968 | tf_op jit(solution)/shard_map/all_to_all | solution.py:375
  32.2 3.8 %collective-permute-start.2 = (bf16[208,128]{1,0:T(8,128)(2,1)S(1)}, bf16[208,128]{1,0:T(8,128)(2,1)S(1)}, u32[]{:S(2)}, u32[]{:S(2)}) collective-permute-start(bf16[208,128]{1,0:T(8,128)(2,1)S(1)} %shard_map.160), channel_id=1, source_target_pairs={{0,192},{64,0},{128,64},{192,128},{1,193},{65,1},{129,65},{193,129... | collective-permute-start | bytes 159752 | tf_op jit(solution)/shard_map/ppermute | solution.py:371
  34.8 4.5 %collective-permute-start.1 = (bf16[208,128]{1,0:T(8,128)(2,1)S(1)}, bf16[208,128]{1,0:T(8,128)(2,1)S(1)}, u32[]{:S(2)}, u32[]{:S(2)}) collective-permute-start(bf16[208,128]{1,0:T(8,128)(2,1)S(1)} %shard_map.160), channel_id=1, source_target_pairs={{0,128},{64,192},{128,0},{192,64},{1,129},{65,193},{129,1},{193,65... | collective-permute-start | bytes 159752 | tf_op jit(solution)/shard_map/ppermute | solution.py:371
  35.3 4.5 %collective-permute-start = (bf16[208,128]{1,0:T(8,128)(2,1)S(1)}, bf16[208,128]{1,0:T(8,128)(2,1)S(1)}, u32[]{:S(2)}, u32[]{:S(2)}) collective-permute-start(bf16[208,128]{1,0:T(8,128)(2,1)S(1)} %shard_map.160), channel_id=1, source_target_pairs={{0,64},{64,128},{128,192},{192,0},{1,65},{65,129},{129,193},{193,1... | collective-permute-start | bytes 159752 | tf_op jit(solution)/shard_map/ppermute | solution.py:371
  54.7 5.2 %collective-permute-start.3 = (bf16[4,192,256]{2,1,0:T(8,128)(2,1)S(1)}, bf16[4,192,256]{2,1,0:T(8,128)(2,1)S(1)}, u32[]{:S(2)}, u32[]{:S(2)}) collective-permute-start(bf16[4,192,256]{2,1,0:T(8,128)(2,1)S(1)} %get-tuple-element.25), channel_id=1, source_target_pairs={{0,1},{1,0},{2,3},{3,2},{4,5},{5,4},{6,7},{7,6},{8,9},{9,8},{10,11... | collective-permute-start | bytes 1179656 | tf_op jit(solution)/shard_map/ppermute | solution.py:371
  60.0 5.4 %collective-permute-start.4 = (bf16[192,256]{1,0:T(8,128)(2,1)S(1)}, bf16[192,256]{1,0:T(8,128)(2,1)S(1)}, u32[]{:S(2)}, u32[]{:S(2)}) collective-permute-start(bf16[192,256]{1,0:T(8,128)(2,1)S(1)} %get-tuple-element.38), channel_id=1, source_target_pairs={{0,2},{2,4},{4,6},{6,0},{1,3},{3,5},{5,7},{7,1},{8,10},{10,12},{12... | collective-permute-start | bytes 294920 | tf_op jit(solution)/shard_map/ppermute | solution.py:371
  61.4 4.0 %collective-permute-start.6 = (bf16[192,256]{1,0:T(8,128)(2,1)S(1)}, bf16[192,256]{1,0:T(8,128)(2,1)S(1)}, u32[]{:S(2)}, u32[]{:S(2)}) collective-permute-start(bf16[192,256]{1,0:T(8,128)(2,1)S(1)} %get-tuple-element.39), channel_id=1, source_target_pairs={{0,6},{2,0},{4,2},{6,4},{1,7},{3,1},{5,3},{7,5},{8,14},{10,8},{12,... | collective-permute-start | bytes 294920 | tf_op jit(solution)/shard_map/ppermute | solution.py:371
  62.9 5.2 %collective-permute-start.5 = (bf16[192,256]{1,0:T(8,128)(2,1)S(1)}, bf16[192,256]{1,0:T(8,128)(2,1)S(1)}, u32[]{:S(2)}, u32[]{:S(2)}) collective-permute-start(bf16[192,256]{1,0:T(8,128)(2,1)S(1)} %get-tuple-element.40), channel_id=1, source_target_pairs={{0,4},{2,6},{4,0},{6,2},{1,5},{3,7},{5,1},{7,3},{8,12},{10,14},{12... | collective-permute-start | bytes 294920 | tf_op jit(solution)/shard_map/ppermute | solution.py:371
  68.2 105.8 %copy-start.4 = (bf16[192,256]{1,0:T(8,128)(2,1)}, bf16[192,256]{1,0:T(8,128)(2,1)S(1)}, u32[]{:S(2)}) copy-start(bf16[192,256]{1,0:T(8,128)(2,1)S(1)} %fusion.3.rest_0_) | copy-start | bytes 294916
  68.2 5.6 %collective-permute-start.11 = (bf16[192,256]{1,0:T(8,128)(2,1)S(1)}, bf16[192,256]{1,0:T(8,128)(2,1)S(1)}, u32[]{:S(2)}, u32[]{:S(2)}) collective-permute-start(bf16[192,256]{1,0:T(8,128)(2,1)S(1)} %fusion.3.rest_0_), channel_id=1, source_target_pairs={{0,48},{8,56},{16,0},{24,8},{32,16},{40,24},{48,32},{56,40},{1,49}... | collective-permute-start | bytes 294920 | tf_op jit(solution)/shard_map/ppermute | solution.py:371
  68.3 6.4 %collective-permute-start.8 = (bf16[192,256]{1,0:T(8,128)(2,1)S(1)}, bf16[192,256]{1,0:T(8,128)(2,1)S(1)}, u32[]{:S(2)}, u32[]{:S(2)}) collective-permute-start(bf16[192,256]{1,0:T(8,128)(2,1)S(1)} %fusion.3.rest_0_), channel_id=1, source_target_pairs={{0,16},{8,24},{16,32},{24,40},{32,48},{40,56},{48,0},{56,8},{1,17}... | collective-permute-start | bytes 294920 | tf_op jit(solution)/shard_map/ppermute | solution.py:371
  70.6 10.3 %collective-permute-start.13 = (bf16[192,256]{1,0:T(8,128)(2,1)S(1)}, bf16[192,256]{1,0:T(8,128)(2,1)S(1)}, u32[]{:S(2)}, u32[]{:S(2)}) collective-permute-start(bf16[192,256]{1,0:T(8,128)(2,1)S(1)} %fusion.3.rest_0_), channel_id=1, source_target_pairs={{0,56},{8,0},{16,8},{24,16},{32,24},{40,32},{48,40},{56,48},{1,57}... | collective-permute-start | bytes 294920 | tf_op jit(solution)/shard_map/ppermute | solution.py:371
  72.0 8.9 %collective-permute-start.7 = (bf16[192,256]{1,0:T(8,128)(2,1)S(1)}, bf16[192,256]{1,0:T(8,128)(2,1)S(1)}, u32[]{:S(2)}, u32[]{:S(2)}) collective-permute-start(bf16[192,256]{1,0:T(8,128)(2,1)S(1)} %fusion.3.rest_0_), channel_id=1, source_target_pairs={{0,8},{8,16},{16,24},{24,32},{32,40},{40,48},{48,56},{56,0},{1,9},... | collective-permute-start | bytes 294920 | tf_op jit(solution)/shard_map/ppermute | solution.py:371
  73.8 7.1 %collective-permute-start.12 = (bf16[192,256]{1,0:T(8,128)(2,1)S(1)}, bf16[192,256]{1,0:T(8,128)(2,1)S(1)}, u32[]{:S(2)}, u32[]{:S(2)}) collective-permute-start(bf16[192,256]{1,0:T(8,128)(2,1)S(1)} %collective-permute-done.11.rest_6_), channel_id=1, source_target_pairs={{0,56},{8,0},{16,8},{24,16},{32,24},{40,32},{48,40},{56,48},{1,57}... | collective-permute-start | bytes 294920 | tf_op jit(solution)/shard_map/ppermute | solution.py:371
  74.7 6.2 %collective-permute-start.10 = (bf16[192,256]{1,0:T(8,128)(2,1)S(1)}, bf16[192,256]{1,0:T(8,128)(2,1)S(1)}, u32[]{:S(2)}, u32[]{:S(2)}) collective-permute-start(bf16[192,256]{1,0:T(8,128)(2,1)S(1)} %collective-permute-done.8.rest_2_), channel_id=1, source_target_pairs={{0,16},{8,24},{16,32},{24,40},{32,48},{40,56},{48,0},{56,8},{1,17}... | collective-permute-start | bytes 294920 | tf_op jit(solution)/shard_map/ppermute | solution.py:371
  75.1 7.6 %collective-permute-start.9 = (bf16[192,256]{1,0:T(8,128)(2,1)S(1)}, bf16[192,256]{1,0:T(8,128)(2,1)S(1)}, u32[]{:S(2)}, u32[]{:S(2)}) collective-permute-start(bf16[192,256]{1,0:T(8,128)(2,1)S(1)} %collective-permute-done.8.rest_2_), channel_id=1, source_target_pairs={{0,8},{8,16},{16,24},{24,32},{32,40},{40,48},{48,56},{56,0},{1,9},... | collective-permute-start | bytes 294920 | tf_op jit(solution)/shard_map/ppermute | solution.py:371
  82.6 38.1 %copy-start.3 = (bf16[1,512,2048]{2,1,0:T(8,128)(2,1)S(1)}, bf16[1,512,2048]{2,1,0:T(8,128)(2,1)}, u32[]{:S(2)}) copy-start(bf16[1,512,2048]{2,1,0:T(8,128)(2,1)} %param.29) | copy-start | bytes 6291460
  157.2 4.5 %collective-permute-start.16 = (bf16[192,256]{1,0:T(8,128)(2,1)S(1)}, bf16[192,256]{1,0:T(8,128)(2,1)S(1)}, u32[]{:S(2)}, u32[]{:S(2)}) collective-permute-start(bf16[192,256]{1,0:T(8,128)(2,1)S(1)} %get-tuple-element.32), channel_id=1, source_target_pairs={{0,56},{8,0},{16,8},{24,16},{32,24},{40,32},{48,40},{56,48},{1,57}... | collective-permute-start | bytes 294920 | tf_op jit(solution)/shard_map/ppermute | solution.py:371
  157.5 7.2 %collective-permute-start.17 = (bf16[192,256]{1,0:T(8,128)(2,1)S(1)}, bf16[192,256]{1,0:T(8,128)(2,1)S(1)}, u32[]{:S(2)}, u32[]{:S(2)}) collective-permute-start(bf16[192,256]{1,0:T(8,128)(2,1)S(1)} %get-tuple-element.33), channel_id=1, source_target_pairs={{0,48},{8,56},{16,0},{24,8},{32,16},{40,24},{48,32},{56,40},{1,49}... | collective-permute-start | bytes 294920 | tf_op jit(solution)/shard_map/ppermute | solution.py:371
  159.3 8.5 %collective-permute-start.14 = (bf16[192,256]{1,0:T(8,128)(2,1)S(1)}, bf16[192,256]{1,0:T(8,128)(2,1)S(1)}, u32[]{:S(2)}, u32[]{:S(2)}) collective-permute-start(bf16[192,256]{1,0:T(8,128)(2,1)S(1)} %get-tuple-element.29), channel_id=1, source_target_pairs={{0,56},{8,0},{16,8},{24,16},{32,24},{40,32},{48,40},{56,48},{1,57}... | collective-permute-start | bytes 294920 | tf_op jit(solution)/shard_map/ppermute | solution.py:371
  160.7 7.1 %collective-permute-start.15 = (bf16[192,256]{1,0:T(8,128)(2,1)S(1)}, bf16[192,256]{1,0:T(8,128)(2,1)S(1)}, u32[]{:S(2)}, u32[]{:S(2)}) collective-permute-start(bf16[192,256]{1,0:T(8,128)(2,1)S(1)} %get-tuple-element.30), channel_id=1, source_target_pairs={{0,8},{8,16},{16,24},{24,32},{32,40},{40,48},{48,56},{56,0},{1,9},... | collective-permute-start | bytes 294920 | tf_op jit(solution)/shard_map/ppermute | solution.py:371
  160.8 6.5 %collective-permute-start.19 = (bf16[192,256]{1,0:T(8,128)(2,1)S(1)}, bf16[192,256]{1,0:T(8,128)(2,1)S(1)}, u32[]{:S(2)}, u32[]{:S(2)}) collective-permute-start(bf16[192,256]{1,0:T(8,128)(2,1)S(1)} %get-tuple-element.35), channel_id=1, source_target_pairs={{0,8},{8,16},{16,24},{24,32},{32,40},{40,48},{48,56},{56,0},{1,9},... | collective-permute-start | bytes 294920 | tf_op jit(solution)/shard_map/ppermute | solution.py:371
  164.7 4.4 %collective-permute-start.18 = (bf16[192,256]{1,0:T(8,128)(2,1)S(1)}, bf16[192,256]{1,0:T(8,128)(2,1)S(1)}, u32[]{:S(2)}, u32[]{:S(2)}) collective-permute-start(bf16[192,256]{1,0:T(8,128)(2,1)S(1)} %add_convert_fusion.2), channel_id=1, source_target_pairs={{0,48},{8,56},{16,0},{24,8},{32,16},{40,24},{48,32},{56,40},{1,49}... | collective-permute-start | bytes 294920 | tf_op jit(solution)/shard_map/ppermute | solution.py:371
  167.3 6.7 %collective-permute-start.20 = (bf16[192,256]{1,0:T(8,128)(2,1)S(1)}, bf16[192,256]{1,0:T(8,128)(2,1)S(1)}, u32[]{:S(2)}, u32[]{:S(2)}) collective-permute-start(bf16[192,256]{1,0:T(8,128)(2,1)S(1)} %add_convert_fusion.1), channel_id=1, source_target_pairs={{0,16},{8,24},{16,32},{24,40},{32,48},{40,56},{48,0},{56,8},{1,17}... | collective-permute-start | bytes 294920 | tf_op jit(solution)/shard_map/ppermute | solution.py:371
  (18 other events, 276.8 us)

commit v6 on v5

--- a/solution.py
+++ b/solution.py
@@ -380,7 +380,7 @@
     left = [shifted(value, axis, -1), shifted(value, axis, -2)]
     right.append(shifted(right[2], axis, 1))
     left.append(shifted(left[1], axis, -1))
-    right.append(shifted(right[2], axis, 2))
+    left.append(shifted(left[1], axis, -2))
     return right + left[::-1]
 
 
@@ -390,7 +390,8 @@
 
     left = parts[2] + passed(parts[3], -1) + passed(parts[4], -2)
     right = parts[6] + passed(parts[5], 1)
-    near = passed(parts[1], -1) + passed(parts[7], 1)
+    right, first, last = lax.optimization_barrier((right, parts[1], parts[7]))
+    near = passed(first, -1) + passed(last, 1)
     return parts[0] + near + (passed(left, -2) + passed(right, 2))
 
 

time: 177 us -> 174 us (0.983)
  waiting for transfers between devices: 29.6 us -> 25.7 us
  starting transfers between devices: 33.6 us -> 36.6 us
    ppermute x21, waiting for transfers between devices: 23.3 us -> 19.5 us  [shifted(): lax.ppermute(value, axis, [(i, (i + distance) % size) for i in range(size)])]
    ppermute x21, starting transfers between devices: 24.6 us -> 27.6 us  [shifted(): lax.ppermute(value, axis, [(i, (i + distance) % size) for i in range(size)])]
  transfers between devices with their start and end apart: 22 -> 22, of which waited for: 14 -> 12; matrix products, arithmetic and copies ran while one was open for 0% -> 0% of each run, Pallas kernels for 3% -> 3%
where the time goes in v6:
time: 174 us; the launch traced here: 173 us
  blocking collectives  79.8 us (46%)
  starting transfers between devices  36.6 us (21%)
  waiting for transfers between devices  25.7 us (15%)
  Pallas kernels  21.8 us (13%)
  local copies, waits for them, and re-layouts  7.19 us (4%)
    all_to_all x3, blocking collectives, swap(): return lax.all_to_all(value, axes, 0, 0, tiled=True)  79.8 us
    ppermute x21, starting transfers between devices, shifted(): lax.ppermute(value, axis, [(i, (i + distance) % size) for i in range(size)])  27.6 us
    pallas_call x9, Pallas kernels, call(): pl.pallas_call(kernel, out_shape=out_shape, compiler_params=pltpu.Compile...  21.8 us
    ppermute x21, waiting for transfers between devices, shifted(): lax.ppermute(value, axis, [(i, (i + distance) % size) for i in range(size)])  19.5 us
    all_to_all x1, starting transfers between devices, swap(): return lax.all_to_all(value, axes, 0, 0, tiled=True)  9.03 us
    unnamed x40, local copies, waits for them, and re-layouts  7.17 us
    all_to_all x1, waiting for transfers between devices, swap(): return lax.all_to_all(value, axes, 0, 0, tiled=True)  6.3 us
  transfers between devices with their start and end apart: 22, of which 12 were waited for; matrix products, arithmetic and copies ran while one was open for 0% of the time, Pallas kernels for 3%

profile of v6, /device:TPU:1, one launch (start us, length us, event | category | flops | bytes accessed | tf_op | source)
XLA Modules:
  0.0 173.0 jit_solution(10377512279580314961)
XLA Ops:
  0.6 6.4 %shard_map.158 = (bf16[8,208,128]{2,1,0:T(8,128)(2,1)}, f32[4,192,256]{2,1,0:T(8,128)}) custom-call(bf16[192,256]{1,0:T(8,128)(2,1)} %k_ref.1, bf16[192,512]{1,0:T(8,128)(2,1)} %refs_1_.1, f32[4,192]{1,0:T(4,128)} %decay_ref.1, f32[4,192]{1,0:T(4,128)} %logit_ref.1), custom_call_target="tpu_custom_call" | custom-call | tf_op jit(solution)/shard_map/pallas_call | solution.py:78
  7.0 9.0 %all-to-all-start = ((bf16[8,208,128]{2,1,0:T(8,128)(2,1)}), bf16[8,208,128]{2,1,0:T(8,128)(2,1)S(1)}, u32[]{:S(2)}, u32[]{:S(2)}) async-start(bf16[8,208,128]{2,1,0:T(8,128)(2,1)} %get-tuple-element.25), calls=%async_computation | async-start | bytes 851968 | tf_op jit(solution)/shard_map/all_to_all | solution.py:375
  21.8 1.6 shard_map.159
  24.8 6.3 %all-to-all-done.got_ref = bf16[8,208,128]{2,1,0:T(8,128)(2,1)S(1)} async-done(((bf16[8,208,128]{2,1,0:T(8,128)(2,1)}), bf16[8,208,128]{2,1,0:T(8,128)(2,1)S(1)}, u32[]{:S(2)}, u32[]{:S(2)}) %all-to-all-start) | async-done | bytes 426016 | tf_op jit(solution)/shard_map/all_to_all | solution.py:375
  32.2 2.6 %collective-permute-start.2 = (bf16[208,128]{1,0:T(8,128)(2,1)S(1)}, bf16[208,128]{1,0:T(8,128)(2,1)S(1)}, u32[]{:S(2)}, u32[]{:S(2)}) collective-permute-start(bf16[208,128]{1,0:T(8,128)(2,1)S(1)} %shard_map.160), channel_id=1, source_target_pairs={{0,192},{64,0},{128,64},{192,128},{1,193},{65,1},{129,65},{193,129... | collective-permute-start | bytes 159752 | tf_op jit(solution)/shard_map/ppermute | solution.py:371
  36.0 3.3 %collective-permute-done.1.rest_1_ = bf16[208,128]{1,0:T(8,128)(2,1)S(1)} collective-permute-done((bf16[208,128]{1,0:T(8,128)(2,1)S(1)}, bf16[208,128]{1,0:T(8,128)(2,1)S(1)}, u32[]{:S(2)}, u32[]{:S(2)}) %collective-permute-start.1) | collective-permute-done | bytes 53280 | tf_op jit(solution)/shard_map/ppermute | solution.py:371
  39.8 1.9 %shard_map.161 = bf16[8,112,128]{2,1,0:T(8,128)(2,1)S(1)} custom-call(s32[4]{0:T(128)S(1)} %pad_add_fusion.here_ref, bf16[8,208,128]{2,1,0:T(8,128)(2,1)S(1)} %all-to-all-done.got_ref, bf16[8,48,128]{2,1,0:T(8,128)(2,1)S(1)} %get-tuple-element.26.after_ref.route_ref, bf16[208,128]{1,0:T(8,128)(2,1)S(1)} %collective-permute-done.rest_0_, ...), custom_call_target="tpu_custom_call" | custom-call | tf_op jit(solution)/shard_map/pallas_call | solution.py:78
  41.8 11.4 %all_to_all.20.state_ref.got_ref = bf16[8,112,128]{2,1,0:T(8,128)(2,1)S(1)} all-to-all(bf16[8,112,128]{2,1,0:T(8,128)(2,1)S(1)} %shard_map.161), channel_id=1, replica_groups=mesh['x'=4,'z'=8,'y'=4,'c'=2] {'z'}, dimensions={0} | all-to-all | bytes 458752 | tf_op jit(solution)/shard_map/all_to_all | solution.py:375
  54.7 3.9 %collective-permute-start.3 = (bf16[4,192,256]{2,1,0:T(8,128)(2,1)S(1)}, bf16[4,192,256]{2,1,0:T(8,128)(2,1)S(1)}, u32[]{:S(2)}, u32[]{:S(2)}) collective-permute-start(bf16[4,192,256]{2,1,0:T(8,128)(2,1)S(1)} %get-tuple-element.28), channel_id=1, source_target_pairs={{0,1},{1,0},{2,3},{3,2},{4,5},{5,4},{6,7},{7,6},{8,9},{9,8},{10,11... | collective-permute-start | bytes 1179656 | tf_op jit(solution)/shard_map/ppermute | solution.py:371
  61.4 1.5 collective-permute-start.6
  62.9 1.6 collective-permute-start.5
  65.4 2.7 %collective-permute-done.5 = bf16[192,256]{1,0:T(8,128)(2,1)S(1)} collective-permute-done((bf16[192,256]{1,0:T(8,128)(2,1)S(1)}, bf16[192,256]{1,0:T(8,128)(2,1)S(1)}, u32[]{:S(2)}, u32[]{:S(2)}) %collective-permute-start.5) | collective-permute-done | bytes 98336 | tf_op jit(solution)/shard_map/ppermute | solution.py:371
  68.3 2.4 %collective-permute-start.8 = (bf16[192,256]{1,0:T(8,128)(2,1)S(1)}, bf16[192,256]{1,0:T(8,128)(2,1)S(1)}, u32[]{:S(2)}, u32[]{:S(2)}) collective-permute-start(bf16[192,256]{1,0:T(8,128)(2,1)S(1)} %fusion.3.rest_0_), channel_id=1, source_target_pairs={{0,16},{8,24},{16,32},{24,40},{32,48},{40,56},{48,0},{56,8},{1,17}... | collective-permute-start | bytes 294920 | tf_op jit(solution)/shard_map/ppermute | solution.py:371
  72.1 1.7 collective-permute-done.10.rest_6_
  74.7 1.6 collective-permute-start.9
  76.3 4.1 %shard_map.163 = (bf16[8,512,192]{2,1,0:T(8,128)(2,1)S(1)}, bf16[8,192,512]{2,1,0:T(8,128)(2,1)S(1)}) custom-call(s32[4]{0:T(128)S(1)} %pad_add_fusion.here_ref, bf16[8,112,128]{2,1,0:T(8,128)(2,1)S(1)} %all_to_all.20.state_ref.got_ref), custom_call_target="tpu_custom_call" | custom-call | flops 1000000000 | bytes 4000000 | tf_op jit(solution)/shard_map/pallas_call | solution.py:78
  81.8 36.4 %all_to_all.21 = bf16[32,128,256]{2,1,0:T(8,128)(2,1)S(1)} all-to-all(bf16[32,128,256]{2,1,0:T(8,128)(2,1)S(1)} %shard_map.164), channel_id=1, replica_groups=mesh['x'=4,'z'=8,'y'=4,'c'=2] {'x','y','c'}, dimensions={0} | all-to-all | bytes 4194304 | tf_op jit(solution)/shard_map/all_to_all | solution.py:375
  118.3 3.9 %shard_map.165 = bf16[4,8,128,256]{3,2,1,0:T(8,128)(2,1)S(1)} custom-call(bf16[4,8,128,256]{3,2,1,0:T(8,128)(2,1)S(1)} %bitcast.29, f32[1,2048]{1,0:T(1,128)S(1)} %bitcast.34, bf16[2048,512]{1,0:T(8,128)(2,1)S(1)} %bitcast.31, bf16[2048,512]{1,0:T(8,128)(2,1)S(1)} %bitcast.32, bf16[512,2048]{1,0:T(8,128)(2,1)S(1)} %bitcast.33), custom_call_target="tpu_custom_call" | custom-call | tf_op jit(solution)/shard_map/pallas_call | solution.py:78
  122.2 31.9 %all_to_all.22.rows_ref = bf16[32,128,256]{2,1,0:T(8,128)(2,1)S(1)} all-to-all(bf16[32,128,256]{2,1,0:T(8,128)(2,1)S(1)} %bitcast.30), channel_id=1, replica_groups=mesh['x'=4,'z'=8,'y'=4,'c'=2] {'x','y','c'}, dimensions={0} | all-to-all | bytes 4194304 | tf_op jit(solution)/shard_map/all_to_all | solution.py:375
  154.7 1.6 collective-permute-start.14
  162.5 1.9 %collective-permute-done.18 = bf16[192,256]{1,0:T(8,128)(2,1)S(1)} collective-permute-done((bf16[192,256]{1,0:T(8,128)(2,1)S(1)}, bf16[192,256]{1,0:T(8,128)(2,1)S(1)}, u32[]{:S(2)}, u32[]{:S(2)}) %collective-permute-start.18) | collective-permute-done | bytes 98336 | tf_op jit(solution)/shard_map/ppermute | solution.py:371
  164.5 2.8 %collective-permute-start.19 = (bf16[192,256]{1,0:T(8,128)(2,1)S(1)}, bf16[192,256]{1,0:T(8,128)(2,1)S(1)}, u32[]{:S(2)}, u32[]{:S(2)}) collective-permute-start(bf16[192,256]{1,0:T(8,128)(2,1)S(1)} %add_convert_fusion.1), channel_id=1, source_target_pairs={{0,48},{8,56},{16,0},{24,8},{32,16},{40,24},{48,32},{56,40},{1,49}... | collective-permute-start | bytes 294920 | tf_op jit(solution)/shard_map/ppermute | solution.py:371
  167.2 1.9 %collective-permute-done.20 = bf16[192,256]{1,0:T(8,128)(2,1)S(1)} collective-permute-done((bf16[192,256]{1,0:T(8,128)(2,1)S(1)}, bf16[192,256]{1,0:T(8,128)(2,1)S(1)}, u32[]{:S(2)}, u32[]{:S(2)}) %collective-permute-start.20) | collective-permute-done | bytes 98336 | tf_op jit(solution)/shard_map/ppermute | solution.py:371
  169.1 3.2 %collective-permute-done.19 = bf16[192,256]{1,0:T(8,128)(2,1)S(1)} collective-permute-done((bf16[192,256]{1,0:T(8,128)(2,1)S(1)}, bf16[192,256]{1,0:T(8,128)(2,1)S(1)}, u32[]{:S(2)}, u32[]{:S(2)}) %collective-permute-start.19) | collective-permute-done | bytes 98336 | tf_op jit(solution)/shard_map/ppermute | solution.py:371
  (79 shorter events, 26.7 us)
Async XLA Ops:
  7.0 24.1 %all-to-all-start = ((bf16[8,208,128]{2,1,0:T(8,128)(2,1)}), bf16[8,208,128]{2,1,0:T(8,128)(2,1)S(1)}, u32[]{:S(2)}, u32[]{:S(2)}) async-start(bf16[8,208,128]{2,1,0:T(8,128)(2,1)} %get-tuple-element.25), calls=%async_computation | async-start | bytes 851968 | tf_op jit(solution)/shard_map/all_to_all | solution.py:375
  32.2 3.8 %collective-permute-start.2 = (bf16[208,128]{1,0:T(8,128)(2,1)S(1)}, bf16[208,128]{1,0:T(8,128)(2,1)S(1)}, u32[]{:S(2)}, u32[]{:S(2)}) collective-permute-start(bf16[208,128]{1,0:T(8,128)(2,1)S(1)} %shard_map.160), channel_id=1, source_target_pairs={{0,192},{64,0},{128,64},{192,128},{1,193},{65,1},{129,65},{193,129... | collective-permute-start | bytes 159752 | tf_op jit(solution)/shard_map/ppermute | solution.py:371
  34.8 4.5 %collective-permute-start.1 = (bf16[208,128]{1,0:T(8,128)(2,1)S(1)}, bf16[208,128]{1,0:T(8,128)(2,1)S(1)}, u32[]{:S(2)}, u32[]{:S(2)}) collective-permute-start(bf16[208,128]{1,0:T(8,128)(2,1)S(1)} %shard_map.160), channel_id=1, source_target_pairs={{0,128},{64,192},{128,0},{192,64},{1,129},{65,193},{129,1},{193,65... | collective-permute-start | bytes 159752 | tf_op jit(solution)/shard_map/ppermute | solution.py:371
  35.3 4.5 %collective-permute-start = (bf16[208,128]{1,0:T(8,128)(2,1)S(1)}, bf16[208,128]{1,0:T(8,128)(2,1)S(1)}, u32[]{:S(2)}, u32[]{:S(2)}) collective-permute-start(bf16[208,128]{1,0:T(8,128)(2,1)S(1)} %shard_map.160), channel_id=1, source_target_pairs={{0,64},{64,128},{128,192},{192,0},{1,65},{65,129},{129,193},{193,1... | collective-permute-start | bytes 159752 | tf_op jit(solution)/shard_map/ppermute | solution.py:371
  54.7 5.2 %collective-permute-start.3 = (bf16[4,192,256]{2,1,0:T(8,128)(2,1)S(1)}, bf16[4,192,256]{2,1,0:T(8,128)(2,1)S(1)}, u32[]{:S(2)}, u32[]{:S(2)}) collective-permute-start(bf16[4,192,256]{2,1,0:T(8,128)(2,1)S(1)} %get-tuple-element.28), channel_id=1, source_target_pairs={{0,1},{1,0},{2,3},{3,2},{4,5},{5,4},{6,7},{7,6},{8,9},{9,8},{10,11... | collective-permute-start | bytes 1179656 | tf_op jit(solution)/shard_map/ppermute | solution.py:371
  60.0 5.4 %collective-permute-start.4 = (bf16[192,256]{1,0:T(8,128)(2,1)S(1)}, bf16[192,256]{1,0:T(8,128)(2,1)S(1)}, u32[]{:S(2)}, u32[]{:S(2)}) collective-permute-start(bf16[192,256]{1,0:T(8,128)(2,1)S(1)} %get-tuple-element.44), channel_id=1, source_target_pairs={{0,2},{2,4},{4,6},{6,0},{1,3},{3,5},{5,7},{7,1},{8,10},{10,12},{12... | collective-permute-start | bytes 294920 | tf_op jit(solution)/shard_map/ppermute | solution.py:371
  61.4 4.0 %collective-permute-start.6 = (bf16[192,256]{1,0:T(8,128)(2,1)S(1)}, bf16[192,256]{1,0:T(8,128)(2,1)S(1)}, u32[]{:S(2)}, u32[]{:S(2)}) collective-permute-start(bf16[192,256]{1,0:T(8,128)(2,1)S(1)} %get-tuple-element.45), channel_id=1, source_target_pairs={{0,6},{2,0},{4,2},{6,4},{1,7},{3,1},{5,3},{7,5},{8,14},{10,8},{12,... | collective-permute-start | bytes 294920 | tf_op jit(solution)/shard_map/ppermute | solution.py:371
  62.9 5.2 %collective-permute-start.5 = (bf16[192,256]{1,0:T(8,128)(2,1)S(1)}, bf16[192,256]{1,0:T(8,128)(2,1)S(1)}, u32[]{:S(2)}, u32[]{:S(2)}) collective-permute-start(bf16[192,256]{1,0:T(8,128)(2,1)S(1)} %get-tuple-element.46), channel_id=1, source_target_pairs={{0,4},{2,6},{4,0},{6,2},{1,5},{3,7},{5,1},{7,3},{8,12},{10,14},{12... | collective-permute-start | bytes 294920 | tf_op jit(solution)/shard_map/ppermute | solution.py:371
  68.2 104.1 %copy-start.4 = (bf16[192,256]{1,0:T(8,128)(2,1)}, bf16[192,256]{1,0:T(8,128)(2,1)S(1)}, u32[]{:S(2)}) copy-start(bf16[192,256]{1,0:T(8,128)(2,1)S(1)} %fusion.3.rest_0_) | copy-start | bytes 294916
  68.2 5.6 %collective-permute-start.10 = (bf16[192,256]{1,0:T(8,128)(2,1)S(1)}, bf16[192,256]{1,0:T(8,128)(2,1)S(1)}, u32[]{:S(2)}, u32[]{:S(2)}) collective-permute-start(bf16[192,256]{1,0:T(8,128)(2,1)S(1)} %fusion.3.rest_0_), channel_id=1, source_target_pairs={{0,48},{8,56},{16,0},{24,8},{32,16},{40,24},{48,32},{56,40},{1,49}... | collective-permute-start | bytes 294920 | tf_op jit(solution)/shard_map/ppermute | solution.py:371
  68.3 6.4 %collective-permute-start.8 = (bf16[192,256]{1,0:T(8,128)(2,1)S(1)}, bf16[192,256]{1,0:T(8,128)(2,1)S(1)}, u32[]{:S(2)}, u32[]{:S(2)}) collective-permute-start(bf16[192,256]{1,0:T(8,128)(2,1)S(1)} %fusion.3.rest_0_), channel_id=1, source_target_pairs={{0,16},{8,24},{16,32},{24,40},{32,48},{40,56},{48,0},{56,8},{1,17}... | collective-permute-start | bytes 294920 | tf_op jit(solution)/shard_map/ppermute | solution.py:371
  70.6 9.8 %collective-permute-start.13 = (bf16[192,256]{1,0:T(8,128)(2,1)S(1)}, bf16[192,256]{1,0:T(8,128)(2,1)S(1)}, u32[]{:S(2)}, u32[]{:S(2)}) collective-permute-start(bf16[192,256]{1,0:T(8,128)(2,1)S(1)} %fusion.3.rest_0_), channel_id=1, source_target_pairs={{0,56},{8,0},{16,8},{24,16},{32,24},{40,32},{48,40},{56,48},{1,57}... | collective-permute-start | bytes 294920 | tf_op jit(solution)/shard_map/ppermute | solution.py:371
  72.0 8.4 %collective-permute-start.7 = (bf16[192,256]{1,0:T(8,128)(2,1)S(1)}, bf16[192,256]{1,0:T(8,128)(2,1)S(1)}, u32[]{:S(2)}, u32[]{:S(2)}) collective-permute-start(bf16[192,256]{1,0:T(8,128)(2,1)S(1)} %fusion.3.rest_0_), channel_id=1, source_target_pairs={{0,8},{8,16},{16,24},{24,32},{32,40},{40,48},{48,56},{56,0},{1,9},... | collective-permute-start | bytes 294920 | tf_op jit(solution)/shard_map/ppermute | solution.py:371
  73.8 6.7 %collective-permute-start.12 = (bf16[192,256]{1,0:T(8,128)(2,1)S(1)}, bf16[192,256]{1,0:T(8,128)(2,1)S(1)}, u32[]{:S(2)}, u32[]{:S(2)}) collective-permute-start(bf16[192,256]{1,0:T(8,128)(2,1)S(1)} %collective-permute-done.10.rest_6_), channel_id=1, source_target_pairs={{0,56},{8,0},{16,8},{24,16},{32,24},{40,32},{48,40},{56,48},{1,57}... | collective-permute-start | bytes 294920 | tf_op jit(solution)/shard_map/ppermute | solution.py:371
  74.7 6.3 %collective-permute-start.11 = (bf16[192,256]{1,0:T(8,128)(2,1)S(1)}, bf16[192,256]{1,0:T(8,128)(2,1)S(1)}, u32[]{:S(2)}, u32[]{:S(2)}) collective-permute-start(bf16[192,256]{1,0:T(8,128)(2,1)S(1)} %collective-permute-done.10.rest_6_), channel_id=1, source_target_pairs={{0,48},{8,56},{16,0},{24,8},{32,16},{40,24},{48,32},{56,40},{1,49}... | collective-permute-start | bytes 294920 | tf_op jit(solution)/shard_map/ppermute | solution.py:371
  74.7 6.3 %collective-permute-start.9 = (bf16[192,256]{1,0:T(8,128)(2,1)S(1)}, bf16[192,256]{1,0:T(8,128)(2,1)S(1)}, u32[]{:S(2)}, u32[]{:S(2)}) collective-permute-start(bf16[192,256]{1,0:T(8,128)(2,1)S(1)} %collective-permute-done.8.rest_2_), channel_id=1, source_target_pairs={{0,8},{8,16},{16,24},{24,32},{32,40},{40,48},{48,56},{56,0},{1,9},... | collective-permute-start | bytes 294920 | tf_op jit(solution)/shard_map/ppermute | solution.py:371
  81.1 37.2 %copy-start.3 = (bf16[1,512,2048]{2,1,0:T(8,128)(2,1)S(1)}, bf16[1,512,2048]{2,1,0:T(8,128)(2,1)}, u32[]{:S(2)}) copy-start(bf16[1,512,2048]{2,1,0:T(8,128)(2,1)} %param.29) | copy-start | bytes 6291460
  154.7 5.5 %collective-permute-start.14 = (bf16[192,256]{1,0:T(8,128)(2,1)S(1)}, bf16[192,256]{1,0:T(8,128)(2,1)S(1)}, u32[]{:S(2)}, u32[]{:S(2)}) collective-permute-start(bf16[192,256]{1,0:T(8,128)(2,1)S(1)} %get-tuple-element.33), channel_id=1, source_target_pairs={{0,8},{8,16},{16,24},{24,32},{32,40},{40,48},{48,56},{56,0},{1,9},... | collective-permute-start | bytes 294920 | tf_op jit(solution)/shard_map/ppermute | solution.py:371
  156.3 6.3 %collective-permute-start.17 = (bf16[192,256]{1,0:T(8,128)(2,1)S(1)}, bf16[192,256]{1,0:T(8,128)(2,1)S(1)}, u32[]{:S(2)}, u32[]{:S(2)}) collective-permute-start(bf16[192,256]{1,0:T(8,128)(2,1)S(1)} %get-tuple-element.39), channel_id=1, source_target_pairs={{0,56},{8,0},{16,8},{24,16},{32,24},{40,32},{48,40},{56,48},{1,57}... | collective-permute-start | bytes 294920 | tf_op jit(solution)/shard_map/ppermute | solution.py:371
  157.5 7.0 %collective-permute-start.18 = (bf16[192,256]{1,0:T(8,128)(2,1)S(1)}, bf16[192,256]{1,0:T(8,128)(2,1)S(1)}, u32[]{:S(2)}, u32[]{:S(2)}) collective-permute-start(bf16[192,256]{1,0:T(8,128)(2,1)S(1)} %get-tuple-element.40), channel_id=1, source_target_pairs={{0,48},{8,56},{16,0},{24,8},{32,16},{40,24},{48,32},{56,40},{1,49}... | collective-permute-start | bytes 294920 | tf_op jit(solution)/shard_map/ppermute | solution.py:371
  160.3 7.0 %collective-permute-start.15 = (bf16[192,256]{1,0:T(8,128)(2,1)S(1)}, bf16[192,256]{1,0:T(8,128)(2,1)S(1)}, u32[]{:S(2)}, u32[]{:S(2)}) collective-permute-start(bf16[192,256]{1,0:T(8,128)(2,1)S(1)} %get-tuple-element.36), channel_id=1, source_target_pairs={{0,56},{8,0},{16,8},{24,16},{32,24},{40,32},{48,40},{56,48},{1,57}... | collective-permute-start | bytes 294920 | tf_op jit(solution)/shard_map/ppermute | solution.py:371
  160.8 6.4 %collective-permute-start.16 = (bf16[192,256]{1,0:T(8,128)(2,1)S(1)}, bf16[192,256]{1,0:T(8,128)(2,1)S(1)}, u32[]{:S(2)}, u32[]{:S(2)}) collective-permute-start(bf16[192,256]{1,0:T(8,128)(2,1)S(1)} %get-tuple-element.37), channel_id=1, source_target_pairs={{0,8},{8,16},{16,24},{24,32},{32,40},{40,48},{48,56},{56,0},{1,9},... | collective-permute-start | bytes 294920 | tf_op jit(solution)/shard_map/ppermute | solution.py:371
  161.8 7.3 %collective-permute-start.20 = (bf16[192,256]{1,0:T(8,128)(2,1)S(1)}, bf16[192,256]{1,0:T(8,128)(2,1)S(1)}, u32[]{:S(2)}, u32[]{:S(2)}) collective-permute-start(bf16[192,256]{1,0:T(8,128)(2,1)S(1)} %convert_add_fusion.1), channel_id=1, source_target_pairs={{0,16},{8,24},{16,32},{24,40},{32,48},{40,56},{48,0},{56,8},{1,17}... | collective-permute-start | bytes 294920 | tf_op jit(solution)/shard_map/ppermute | solution.py:371
  164.5 7.8 %collective-permute-start.19 = (bf16[192,256]{1,0:T(8,128)(2,1)S(1)}, bf16[192,256]{1,0:T(8,128)(2,1)S(1)}, u32[]{:S(2)}, u32[]{:S(2)}) collective-permute-start(bf16[192,256]{1,0:T(8,128)(2,1)S(1)} %add_convert_fusion.1), channel_id=1, source_target_pairs={{0,48},{8,56},{16,0},{24,8},{32,16},{40,24},{48,32},{56,40},{1,49}... | collective-permute-start | bytes 294920 | tf_op jit(solution)/shard_map/ppermute | solution.py:371
  (18 other events, 274.2 us)

commit v7 on v6

--- a/solution.py
+++ b/solution.py
@@ -378,9 +378,10 @@
 def spread_out(value, axis):
     right = [value, shifted(value, axis, 1), shifted(value, axis, 2)]
     left = [shifted(value, axis, -1), shifted(value, axis, -2)]
+    far = shifted(left[1], axis, -2)
+    left.append(shifted(left[1], axis, -1))
     right.append(shifted(right[2], axis, 1))
-    left.append(shifted(left[1], axis, -1))
-    left.append(shifted(left[1], axis, -2))
+    left.append(far)
     return right + left[::-1]
 
 
@@ -388,7 +389,7 @@
     def passed(value, distance):
         return shifted(value.astype(BF), axis, distance).astype(F32)
 
-    left = parts[2] + passed(parts[3], -1) + passed(parts[4], -2)
+    left = parts[2] + passed(parts[4], -2) + passed(parts[3], -1)
     right = parts[6] + passed(parts[5], 1)
     right, first, last = lax.optimization_barrier((right, parts[1], parts[7]))
     near = passed(first, -1) + passed(last, 1)

time: 174 us -> 173 us (level)
  starting transfers between devices: 36.6 us -> 34.8 us
    ppermute x21, starting transfers between devices: 27.6 us -> 25.8 us  [shifted(): lax.ppermute(value, axis, [(i, (i + distance) % size) for i in range(size)])]
  transfers between devices with their start and end apart: 22 -> 22, of which waited for: 12 -> 14; matrix products, arithmetic and copies ran while one was open for 0% -> 0% of each run, Pallas kernels for 3% -> 3%
where the time goes in v7:
time: 173 us; the launch traced here: 172 us
  blocking collectives  79.8 us (46%)
  starting transfers between devices  34.8 us (20%)
  waiting for transfers between devices  26.4 us (15%)
  Pallas kernels  21.8 us (13%)
  local copies, waits for them, and re-layouts  7.19 us (4%)
    all_to_all x3, blocking collectives, swap(): return lax.all_to_all(value, axes, 0, 0, tiled=True)  79.8 us
    ppermute x21, starting transfers between devices, shifted(): lax.ppermute(value, axis, [(i, (i + distance) % size) for i in range(size)])  25.8 us
    pallas_call x9, Pallas kernels, call(): pl.pallas_call(kernel, out_shape=out_shape, compiler_params=pltpu.Compile...  21.8 us
    ppermute x21, waiting for transfers between devices, shifted(): lax.ppermute(value, axis, [(i, (i + distance) % size) for i in range(size)])  20.1 us
    all_to_all x1, starting transfers between devices, swap(): return lax.all_to_all(value, axes, 0, 0, tiled=True)  9.03 us
    unnamed x40, local copies, waits for them, and re-layouts  7.17 us
    all_to_all x1, waiting for transfers between devices, swap(): return lax.all_to_all(value, axes, 0, 0, tiled=True)  6.3 us
  transfers between devices with their start and end apart: 22, of which 14 were waited for; matrix products, arithmetic and copies ran while one was open for 0% of the time, Pallas kernels for 3%

profile of v7, /device:TPU:1, one launch (start us, length us, event | category | flops | bytes accessed | tf_op | source)
XLA Modules:
  0.0 171.9 jit_solution(8469881159950686055)
XLA Ops:
  0.6 6.4 %shard_map.158 = (bf16[8,208,128]{2,1,0:T(8,128)(2,1)}, f32[4,192,256]{2,1,0:T(8,128)}) custom-call(bf16[192,256]{1,0:T(8,128)(2,1)} %k_ref.1, bf16[192,512]{1,0:T(8,128)(2,1)} %refs_1_.1, f32[4,192]{1,0:T(4,128)} %decay_ref.1, f32[4,192]{1,0:T(4,128)} %logit_ref.1), custom_call_target="tpu_custom_call" | custom-call | tf_op jit(solution)/shard_map/pallas_call | solution.py:78
  7.0 9.0 %all-to-all-start = ((bf16[8,208,128]{2,1,0:T(8,128)(2,1)}), bf16[8,208,128]{2,1,0:T(8,128)(2,1)S(1)}, u32[]{:S(2)}, u32[]{:S(2)}) async-start(bf16[8,208,128]{2,1,0:T(8,128)(2,1)} %get-tuple-element.25), calls=%async_computation | async-start | bytes 851968 | tf_op jit(solution)/shard_map/all_to_all | solution.py:375
  21.8 1.6 shard_map.159
  24.8 6.3 %all-to-all-done.got_ref = bf16[8,208,128]{2,1,0:T(8,128)(2,1)S(1)} async-done(((bf16[8,208,128]{2,1,0:T(8,128)(2,1)}), bf16[8,208,128]{2,1,0:T(8,128)(2,1)S(1)}, u32[]{:S(2)}, u32[]{:S(2)}) %all-to-all-start) | async-done | bytes 426016 | tf_op jit(solution)/shard_map/all_to_all | solution.py:375
  32.2 2.6 %collective-permute-start.2 = (bf16[208,128]{1,0:T(8,128)(2,1)S(1)}, bf16[208,128]{1,0:T(8,128)(2,1)S(1)}, u32[]{:S(2)}, u32[]{:S(2)}) collective-permute-start(bf16[208,128]{1,0:T(8,128)(2,1)S(1)} %shard_map.160), channel_id=1, source_target_pairs={{0,192},{64,0},{128,64},{192,128},{1,193},{65,1},{129,65},{193,129... | collective-permute-start | bytes 159752 | tf_op jit(solution)/shard_map/ppermute | solution.py:371
  36.0 3.3 %collective-permute-done.1.rest_1_ = bf16[208,128]{1,0:T(8,128)(2,1)S(1)} collective-permute-done((bf16[208,128]{1,0:T(8,128)(2,1)S(1)}, bf16[208,128]{1,0:T(8,128)(2,1)S(1)}, u32[]{:S(2)}, u32[]{:S(2)}) %collective-permute-start.1) | collective-permute-done | bytes 53280 | tf_op jit(solution)/shard_map/ppermute | solution.py:371
  39.8 1.9 %shard_map.161 = bf16[8,112,128]{2,1,0:T(8,128)(2,1)S(1)} custom-call(s32[4]{0:T(128)S(1)} %pad_add_fusion.here_ref, bf16[8,208,128]{2,1,0:T(8,128)(2,1)S(1)} %all-to-all-done.got_ref, bf16[8,48,128]{2,1,0:T(8,128)(2,1)S(1)} %get-tuple-element.26.after_ref.route_ref, bf16[208,128]{1,0:T(8,128)(2,1)S(1)} %collective-permute-done.rest_0_, ...), custom_call_target="tpu_custom_call" | custom-call | tf_op jit(solution)/shard_map/pallas_call | solution.py:78
  41.8 11.4 %all_to_all.20.state_ref.got_ref = bf16[8,112,128]{2,1,0:T(8,128)(2,1)S(1)} all-to-all(bf16[8,112,128]{2,1,0:T(8,128)(2,1)S(1)} %shard_map.161), channel_id=1, replica_groups=mesh['x'=4,'z'=8,'y'=4,'c'=2] {'z'}, dimensions={0} | all-to-all | bytes 458752 | tf_op jit(solution)/shard_map/all_to_all | solution.py:375
  53.2 1.4 shard_map.162
  54.7 3.9 %collective-permute-start.3 = (bf16[4,192,256]{2,1,0:T(8,128)(2,1)S(1)}, bf16[4,192,256]{2,1,0:T(8,128)(2,1)S(1)}, u32[]{:S(2)}, u32[]{:S(2)}) collective-permute-start(bf16[4,192,256]{2,1,0:T(8,128)(2,1)S(1)} %get-tuple-element.28), channel_id=1, source_target_pairs={{0,1},{1,0},{2,3},{3,2},{4,5},{5,4},{6,7},{7,6},{8,9},{9,8},{10,11... | collective-permute-start | bytes 1179656 | tf_op jit(solution)/shard_map/ppermute | solution.py:371
  61.4 1.5 collective-permute-start.6
  62.9 1.6 collective-permute-start.5
  65.4 2.7 %collective-permute-done.5 = bf16[192,256]{1,0:T(8,128)(2,1)S(1)} collective-permute-done((bf16[192,256]{1,0:T(8,128)(2,1)S(1)}, bf16[192,256]{1,0:T(8,128)(2,1)S(1)}, u32[]{:S(2)}, u32[]{:S(2)}) %collective-permute-start.5) | collective-permute-done | bytes 98336 | tf_op jit(solution)/shard_map/ppermute | solution.py:371
  68.3 2.4 %collective-permute-start.8 = (bf16[192,256]{1,0:T(8,128)(2,1)S(1)}, bf16[192,256]{1,0:T(8,128)(2,1)S(1)}, u32[]{:S(2)}, u32[]{:S(2)}) collective-permute-start(bf16[192,256]{1,0:T(8,128)(2,1)S(1)} %fusion.3.rest_0_), channel_id=1, source_target_pairs={{0,16},{8,24},{16,32},{24,40},{32,48},{40,56},{48,0},{56,8},{1,17}... | collective-permute-start | bytes 294920 | tf_op jit(solution)/shard_map/ppermute | solution.py:371
  72.1 1.7 collective-permute-done.10.rest_6_
  74.7 1.6 collective-permute-start.9
  76.3 4.1 %shard_map.163 = (bf16[8,512,192]{2,1,0:T(8,128)(2,1)S(1)}, bf16[8,192,512]{2,1,0:T(8,128)(2,1)S(1)}) custom-call(s32[4]{0:T(128)S(1)} %pad_add_fusion.here_ref, bf16[8,112,128]{2,1,0:T(8,128)(2,1)S(1)} %all_to_all.20.state_ref.got_ref), custom_call_target="tpu_custom_call" | custom-call | flops 1000000000 | bytes 4000000 | tf_op jit(solution)/shard_map/pallas_call | solution.py:78
  81.8 36.4 %all_to_all.21 = bf16[32,128,256]{2,1,0:T(8,128)(2,1)S(1)} all-to-all(bf16[32,128,256]{2,1,0:T(8,128)(2,1)S(1)} %shard_map.164), channel_id=1, replica_groups=mesh['x'=4,'z'=8,'y'=4,'c'=2] {'x','y','c'}, dimensions={0} | all-to-all | bytes 4194304 | tf_op jit(solution)/shard_map/all_to_all | solution.py:375
  118.3 3.9 %shard_map.165 = bf16[4,8,128,256]{3,2,1,0:T(8,128)(2,1)S(1)} custom-call(bf16[4,8,128,256]{3,2,1,0:T(8,128)(2,1)S(1)} %bitcast.29, f32[1,2048]{1,0:T(1,128)S(1)} %bitcast.34, bf16[2048,512]{1,0:T(8,128)(2,1)S(1)} %bitcast.31, bf16[2048,512]{1,0:T(8,128)(2,1)S(1)} %bitcast.32, bf16[512,2048]{1,0:T(8,128)(2,1)S(1)} %bitcast.33), custom_call_target="tpu_custom_call" | custom-call | tf_op jit(solution)/shard_map/pallas_call | solution.py:78
  122.2 31.9 %all_to_all.22.rows_ref = bf16[32,128,256]{2,1,0:T(8,128)(2,1)S(1)} all-to-all(bf16[32,128,256]{2,1,0:T(8,128)(2,1)S(1)} %bitcast.30), channel_id=1, replica_groups=mesh['x'=4,'z'=8,'y'=4,'c'=2] {'x','y','c'}, dimensions={0} | all-to-all | bytes 4194304 | tf_op jit(solution)/shard_map/all_to_all | solution.py:375
  154.7 1.6 collective-permute-start.14
  163.9 1.6 collective-permute-done.18
  167.6 1.5 collective-permute-done.20
  169.1 2.0 %collective-permute-done.19 = bf16[192,256]{1,0:T(8,128)(2,1)S(1)} collective-permute-done((bf16[192,256]{1,0:T(8,128)(2,1)S(1)}, bf16[192,256]{1,0:T(8,128)(2,1)S(1)}, u32[]{:S(2)}, u32[]{:S(2)}) %collective-permute-start.19) | collective-permute-done | bytes 98336 | tf_op jit(solution)/shard_map/ppermute | solution.py:371
  (79 shorter events, 28.7 us)
Async XLA Ops:
  7.0 24.1 %all-to-all-start = ((bf16[8,208,128]{2,1,0:T(8,128)(2,1)}), bf16[8,208,128]{2,1,0:T(8,128)(2,1)S(1)}, u32[]{:S(2)}, u32[]{:S(2)}) async-start(bf16[8,208,128]{2,1,0:T(8,128)(2,1)} %get-tuple-element.25), calls=%async_computation | async-start | bytes 851968 | tf_op jit(solution)/shard_map/all_to_all | solution.py:375
  32.2 3.8 %collective-permute-start.2 = (bf16[208,128]{1,0:T(8,128)(2,1)S(1)}, bf16[208,128]{1,0:T(8,128)(2,1)S(1)}, u32[]{:S(2)}, u32[]{:S(2)}) collective-permute-start(bf16[208,128]{1,0:T(8,128)(2,1)S(1)} %shard_map.160), channel_id=1, source_target_pairs={{0,192},{64,0},{128,64},{192,128},{1,193},{65,1},{129,65},{193,129... | collective-permute-start | bytes 159752 | tf_op jit(solution)/shard_map/ppermute | solution.py:371
  34.8 4.5 %collective-permute-start.1 = (bf16[208,128]{1,0:T(8,128)(2,1)S(1)}, bf16[208,128]{1,0:T(8,128)(2,1)S(1)}, u32[]{:S(2)}, u32[]{:S(2)}) collective-permute-start(bf16[208,128]{1,0:T(8,128)(2,1)S(1)} %shard_map.160), channel_id=1, source_target_pairs={{0,128},{64,192},{128,0},{192,64},{1,129},{65,193},{129,1},{193,65... | collective-permute-start | bytes 159752 | tf_op jit(solution)/shard_map/ppermute | solution.py:371
  35.3 4.5 %collective-permute-start = (bf16[208,128]{1,0:T(8,128)(2,1)S(1)}, bf16[208,128]{1,0:T(8,128)(2,1)S(1)}, u32[]{:S(2)}, u32[]{:S(2)}) collective-permute-start(bf16[208,128]{1,0:T(8,128)(2,1)S(1)} %shard_map.160), channel_id=1, source_target_pairs={{0,64},{64,128},{128,192},{192,0},{1,65},{65,129},{129,193},{193,1... | collective-permute-start | bytes 159752 | tf_op jit(solution)/shard_map/ppermute | solution.py:371
  54.7 5.2 %collective-permute-start.3 = (bf16[4,192,256]{2,1,0:T(8,128)(2,1)S(1)}, bf16[4,192,256]{2,1,0:T(8,128)(2,1)S(1)}, u32[]{:S(2)}, u32[]{:S(2)}) collective-permute-start(bf16[4,192,256]{2,1,0:T(8,128)(2,1)S(1)} %get-tuple-element.28), channel_id=1, source_target_pairs={{0,1},{1,0},{2,3},{3,2},{4,5},{5,4},{6,7},{7,6},{8,9},{9,8},{10,11... | collective-permute-start | bytes 1179656 | tf_op jit(solution)/shard_map/ppermute | solution.py:371
  60.0 5.4 %collective-permute-start.4 = (bf16[192,256]{1,0:T(8,128)(2,1)S(1)}, bf16[192,256]{1,0:T(8,128)(2,1)S(1)}, u32[]{:S(2)}, u32[]{:S(2)}) collective-permute-start(bf16[192,256]{1,0:T(8,128)(2,1)S(1)} %get-tuple-element.44), channel_id=1, source_target_pairs={{0,2},{2,4},{4,6},{6,0},{1,3},{3,5},{5,7},{7,1},{8,10},{10,12},{12... | collective-permute-start | bytes 294920 | tf_op jit(solution)/shard_map/ppermute | solution.py:371
  61.4 4.0 %collective-permute-start.6 = (bf16[192,256]{1,0:T(8,128)(2,1)S(1)}, bf16[192,256]{1,0:T(8,128)(2,1)S(1)}, u32[]{:S(2)}, u32[]{:S(2)}) collective-permute-start(bf16[192,256]{1,0:T(8,128)(2,1)S(1)} %get-tuple-element.45), channel_id=1, source_target_pairs={{0,6},{2,0},{4,2},{6,4},{1,7},{3,1},{5,3},{7,5},{8,14},{10,8},{12,... | collective-permute-start | bytes 294920 | tf_op jit(solution)/shard_map/ppermute | solution.py:371
  62.9 5.2 %collective-permute-start.5 = (bf16[192,256]{1,0:T(8,128)(2,1)S(1)}, bf16[192,256]{1,0:T(8,128)(2,1)S(1)}, u32[]{:S(2)}, u32[]{:S(2)}) collective-permute-start(bf16[192,256]{1,0:T(8,128)(2,1)S(1)} %get-tuple-element.46), channel_id=1, source_target_pairs={{0,4},{2,6},{4,0},{6,2},{1,5},{3,7},{5,1},{7,3},{8,12},{10,14},{12... | collective-permute-start | bytes 294920 | tf_op jit(solution)/shard_map/ppermute | solution.py:371
  68.2 103.0 %copy-start.4 = (bf16[192,256]{1,0:T(8,128)(2,1)}, bf16[192,256]{1,0:T(8,128)(2,1)S(1)}, u32[]{:S(2)}) copy-start(bf16[192,256]{1,0:T(8,128)(2,1)S(1)} %fusion.3.rest_0_) | copy-start | bytes 294916
  68.2 5.6 %collective-permute-start.10 = (bf16[192,256]{1,0:T(8,128)(2,1)S(1)}, bf16[192,256]{1,0:T(8,128)(2,1)S(1)}, u32[]{:S(2)}, u32[]{:S(2)}) collective-permute-start(bf16[192,256]{1,0:T(8,128)(2,1)S(1)} %fusion.3.rest_0_), channel_id=1, source_target_pairs={{0,48},{8,56},{16,0},{24,8},{32,16},{40,24},{48,32},{56,40},{1,49}... | collective-permute-start | bytes 294920 | tf_op jit(solution)/shard_map/ppermute | solution.py:371
  68.3 6.4 %collective-permute-start.8 = (bf16[192,256]{1,0:T(8,128)(2,1)S(1)}, bf16[192,256]{1,0:T(8,128)(2,1)S(1)}, u32[]{:S(2)}, u32[]{:S(2)}) collective-permute-start(bf16[192,256]{1,0:T(8,128)(2,1)S(1)} %fusion.3.rest_0_), channel_id=1, source_target_pairs={{0,16},{8,24},{16,32},{24,40},{32,48},{40,56},{48,0},{56,8},{1,17}... | collective-permute-start | bytes 294920 | tf_op jit(solution)/shard_map/ppermute | solution.py:371
  70.6 9.8 %collective-permute-start.13 = (bf16[192,256]{1,0:T(8,128)(2,1)S(1)}, bf16[192,256]{1,0:T(8,128)(2,1)S(1)}, u32[]{:S(2)}, u32[]{:S(2)}) collective-permute-start(bf16[192,256]{1,0:T(8,128)(2,1)S(1)} %fusion.3.rest_0_), channel_id=1, source_target_pairs={{0,56},{8,0},{16,8},{24,16},{32,24},{40,32},{48,40},{56,48},{1,57}... | collective-permute-start | bytes 294920 | tf_op jit(solution)/shard_map/ppermute | solution.py:371
  72.0 8.4 %collective-permute-start.7 = (bf16[192,256]{1,0:T(8,128)(2,1)S(1)}, bf16[192,256]{1,0:T(8,128)(2,1)S(1)}, u32[]{:S(2)}, u32[]{:S(2)}) collective-permute-start(bf16[192,256]{1,0:T(8,128)(2,1)S(1)} %fusion.3.rest_0_), channel_id=1, source_target_pairs={{0,8},{8,16},{16,24},{24,32},{32,40},{40,48},{48,56},{56,0},{1,9},... | collective-permute-start | bytes 294920 | tf_op jit(solution)/shard_map/ppermute | solution.py:371
  73.8 6.7 %collective-permute-start.12 = (bf16[192,256]{1,0:T(8,128)(2,1)S(1)}, bf16[192,256]{1,0:T(8,128)(2,1)S(1)}, u32[]{:S(2)}, u32[]{:S(2)}) collective-permute-start(bf16[192,256]{1,0:T(8,128)(2,1)S(1)} %collective-permute-done.10.rest_6_), channel_id=1, source_target_pairs={{0,56},{8,0},{16,8},{24,16},{32,24},{40,32},{48,40},{56,48},{1,57}... | collective-permute-start | bytes 294920 | tf_op jit(solution)/shard_map/ppermute | solution.py:371
  74.7 6.3 %collective-permute-start.11 = (bf16[192,256]{1,0:T(8,128)(2,1)S(1)}, bf16[192,256]{1,0:T(8,128)(2,1)S(1)}, u32[]{:S(2)}, u32[]{:S(2)}) collective-permute-start(bf16[192,256]{1,0:T(8,128)(2,1)S(1)} %collective-permute-done.10.rest_6_), channel_id=1, source_target_pairs={{0,48},{8,56},{16,0},{24,8},{32,16},{40,24},{48,32},{56,40},{1,49}... | collective-permute-start | bytes 294920 | tf_op jit(solution)/shard_map/ppermute | solution.py:371
  74.7 6.3 %collective-permute-start.9 = (bf16[192,256]{1,0:T(8,128)(2,1)S(1)}, bf16[192,256]{1,0:T(8,128)(2,1)S(1)}, u32[]{:S(2)}, u32[]{:S(2)}) collective-permute-start(bf16[192,256]{1,0:T(8,128)(2,1)S(1)} %collective-permute-done.8.rest_2_), channel_id=1, source_target_pairs={{0,8},{8,16},{16,24},{24,32},{32,40},{40,48},{48,56},{56,0},{1,9},... | collective-permute-start | bytes 294920 | tf_op jit(solution)/shard_map/ppermute | solution.py:371
  81.1 37.2 %copy-start.3 = (bf16[1,512,2048]{2,1,0:T(8,128)(2,1)S(1)}, bf16[1,512,2048]{2,1,0:T(8,128)(2,1)}, u32[]{:S(2)}) copy-start(bf16[1,512,2048]{2,1,0:T(8,128)(2,1)} %param.29) | copy-start | bytes 6291460
  154.7 5.5 %collective-permute-start.14 = (bf16[192,256]{1,0:T(8,128)(2,1)S(1)}, bf16[192,256]{1,0:T(8,128)(2,1)S(1)}, u32[]{:S(2)}, u32[]{:S(2)}) collective-permute-start(bf16[192,256]{1,0:T(8,128)(2,1)S(1)} %get-tuple-element.33), channel_id=1, source_target_pairs={{0,8},{8,16},{16,24},{24,32},{32,40},{40,48},{48,56},{56,0},{1,9},... | collective-permute-start | bytes 294920 | tf_op jit(solution)/shard_map/ppermute | solution.py:371
  156.3 7.6 %collective-permute-start.17 = (bf16[192,256]{1,0:T(8,128)(2,1)S(1)}, bf16[192,256]{1,0:T(8,128)(2,1)S(1)}, u32[]{:S(2)}, u32[]{:S(2)}) collective-permute-start(bf16[192,256]{1,0:T(8,128)(2,1)S(1)} %get-tuple-element.39), channel_id=1, source_target_pairs={{0,48},{8,56},{16,0},{24,8},{32,16},{40,24},{48,32},{56,40},{1,49}... | collective-permute-start | bytes 294920 | tf_op jit(solution)/shard_map/ppermute | solution.py:371
  157.7 7.9 %collective-permute-start.18 = (bf16[192,256]{1,0:T(8,128)(2,1)S(1)}, bf16[192,256]{1,0:T(8,128)(2,1)S(1)}, u32[]{:S(2)}, u32[]{:S(2)}) collective-permute-start(bf16[192,256]{1,0:T(8,128)(2,1)S(1)} %get-tuple-element.40), channel_id=1, source_target_pairs={{0,56},{8,0},{16,8},{24,16},{32,24},{40,32},{48,40},{56,48},{1,57}... | collective-permute-start | bytes 294920 | tf_op jit(solution)/shard_map/ppermute | solution.py:371
  160.3 7.3 %collective-permute-start.15 = (bf16[192,256]{1,0:T(8,128)(2,1)S(1)}, bf16[192,256]{1,0:T(8,128)(2,1)S(1)}, u32[]{:S(2)}, u32[]{:S(2)}) collective-permute-start(bf16[192,256]{1,0:T(8,128)(2,1)S(1)} %get-tuple-element.36), channel_id=1, source_target_pairs={{0,56},{8,0},{16,8},{24,16},{32,24},{40,32},{48,40},{56,48},{1,57}... | collective-permute-start | bytes 294920 | tf_op jit(solution)/shard_map/ppermute | solution.py:371
  160.8 6.8 %collective-permute-start.16 = (bf16[192,256]{1,0:T(8,128)(2,1)S(1)}, bf16[192,256]{1,0:T(8,128)(2,1)S(1)}, u32[]{:S(2)}, u32[]{:S(2)}) collective-permute-start(bf16[192,256]{1,0:T(8,128)(2,1)S(1)} %get-tuple-element.37), channel_id=1, source_target_pairs={{0,8},{8,16},{16,24},{24,32},{32,40},{40,48},{48,56},{56,0},{1,9},... | collective-permute-start | bytes 294920 | tf_op jit(solution)/shard_map/ppermute | solution.py:371
  161.8 7.3 %collective-permute-start.20 = (bf16[192,256]{1,0:T(8,128)(2,1)S(1)}, bf16[192,256]{1,0:T(8,128)(2,1)S(1)}, u32[]{:S(2)}, u32[]{:S(2)}) collective-permute-start(bf16[192,256]{1,0:T(8,128)(2,1)S(1)} %convert_add_fusion.1), channel_id=1, source_target_pairs={{0,16},{8,24},{16,32},{24,40},{32,48},{40,56},{48,0},{56,8},{1,17}... | collective-permute-start | bytes 294920 | tf_op jit(solution)/shard_map/ppermute | solution.py:371
  165.6 5.6 %collective-permute-start.19 = (bf16[192,256]{1,0:T(8,128)(2,1)S(1)}, bf16[192,256]{1,0:T(8,128)(2,1)S(1)}, u32[]{:S(2)}, u32[]{:S(2)}) collective-permute-start(bf16[192,256]{1,0:T(8,128)(2,1)S(1)} %add_convert_fusion.1), channel_id=1, source_target_pairs={{0,48},{8,56},{16,0},{24,8},{32,16},{40,24},{48,32},{56,40},{1,49}... | collective-permute-start | bytes 294920 | tf_op jit(solution)/shard_map/ppermute | solution.py:371
  (18 other events, 274.2 us)

commit v8 on v7

--- a/solution.py
+++ b/solution.py
@@ -269,7 +269,7 @@
 
 
 def output_kernel(
-    here_ref, inside_ref, reach_ref, state_ref, gate_ref, gain_ref, proj_ref, rest_ref, keep_ref, give_ref
+    here_ref, inside_ref, reach_ref, state_ref, gate_ref, gain_ref, proj_ref, gated_ref, give_ref
 ):
     heads = inside_ref.shape[0]
     gated = []
@@ -283,15 +283,27 @@
         opened = silu(gate_ref[:, part].astype(F32))
         gated.append((output * scaling * gain_ref[...] * opened).astype(BF))
     gated = jnp.concatenate(gated, axis=1)
+    gated_ref[...] = gated
+    columns, _, width = give_ref.shape
+    for distance in range(columns):
+        first = column_of(here_ref, distance, 1 - here_ref[3], columns, width)
+        give_ref[distance] = mm(gated, proj_ref[:, pl.ds(first, width)]).astype(BF)
+
+
+def column_of(here_ref, distance, core, columns, width):
+    column = lax.rem(here_ref[2] + distance, columns)
+    return pl.multiple_of((column * 2 + core) * width, width)
+
+
+def keep_kernel(here_ref, gated_ref, proj_ref, rest_ref, keep_ref):
+    gated = gated_ref[...]
     columns, _, width = keep_ref.shape
     for distance in range(columns):
-        column = lax.rem(here_ref[2] + distance, columns)
-        for core, out_ref in ((here_ref[3], keep_ref), (1 - here_ref[3], give_ref)):
-            first = pl.multiple_of((column * 2 + core) * width, width)
-            mixed = mm(gated, proj_ref[:, pl.ds(first, width)])
-            if distance == 0 and out_ref is keep_ref:
-                mixed = mixed + rest_ref[:, pl.ds(first, width)].astype(F32)
-            out_ref[distance] = mixed.astype(out_ref.dtype)
+        first = column_of(here_ref, distance, here_ref[3], columns, width)
+        mixed = mm(gated, proj_ref[:, pl.ds(first, width)])
+        if distance == 0:
+            mixed = mixed + rest_ref[:, pl.ds(first, width)].astype(F32)
+        keep_ref[distance] = mixed
 
 
 def route_kernel(here_ref, got_ref, pick_ref, mix_ref):
@@ -353,11 +365,11 @@
             out_ref[group, share] = produced[group * count : (group + 1) * count]
 
 
-def combine_kernel(mix_ref, rows_ref, *outs):
+def combine_kernel(chosen, mix_ref, rows_ref, *outs):
     targets, _, width = rows_ref.shape
-    for block in range(mix_ref.shape[0]):
+    for block, out_ref in zip(chosen, outs):
         rows = rows_ref[:, block * SLOTS : (block + 1) * SLOTS, :].reshape(targets * SLOTS, width)
-        outs[block][...] = mm(mix_ref[block], rows).astype(outs[block].dtype)
+        out_ref[...] = mm(mix_ref[block], rows).astype(out_ref.dtype)
 
 
 SCALAR = pl.BlockSpec(memory_space=pltpu.SMEM)
@@ -493,9 +505,9 @@
     )
 
     columns = lax.axis_size("y")
-    keep, give = call(
+    gated, give = call(
         output_kernel,
-        (shape((columns, length, width), F32), shape((columns, length, width), BF)),
+        (shape((length, heads * DV), BF), shape((columns, length, width), BF)),
         here,
         inside,
         reach,
@@ -503,9 +515,20 @@
         gate_in,
         head_gain.reshape(1, DV),
         out_proj,
+        vmem=16,
+        in_specs=[SCALAR] + [VECTOR] * 6,
+    )
+    keep = call(
+        keep_kernel,
+        shape((columns, length, width), F32),
+        here,
+        gated,
+        out_proj,
         residual_in,
         vmem=16,
-        in_specs=[SCALAR] + [VECTOR] * 7,
+        flops=2 * 10**8,
+        moved=10**6,
+        in_specs=[SCALAR] + [VECTOR] * 3,
     )
     both = keep + shifted(give, "c", 1).astype(F32)
     mixed = both[0]
@@ -528,13 +551,18 @@
         scratch_shapes=[pltpu.VMEM((groups * count, shares * width), BF)],
     )
     returned = swap(produced.reshape(targets, count, width), ("x", "y", "c"))
-    mixes = call(
-        combine_kernel,
-        tuple(shape((length, width), F32 if i in (0, 2, 6) else BF) for i in range(blocks)),
-        mix,
-        returned,
-        vmem=16,
-    )
+    mixes = {}
+    for chosen in ((4, 3, 5), (0, 1, 2, 6, 7)):
+        outs = call(
+            functools.partial(combine_kernel, chosen),
+            tuple(shape((length, width), F32 if i in (0, 2, 6) else BF) for i in chosen),
+            mix,
+            returned,
+            vmem=16,
+            flops=10**8,
+            moved=10**6,
+        )
+        mixes.update(zip(chosen, outs))
     expert_mix = gathered_sum(mixes, "z")
     layer_out = (middle.astype(F32) + expert_mix).astype(BF)
     return (middle, layer_out)

time: 173 us -> 172 us (level)
    ppermute x21, waiting for transfers between devices: 20.1 us -> 17.6 us  [shifted(): lax.ppermute(value, axis, [(i, (i + distance) % size) for i in range(size)])]
    unnamed x40 -> x32, local copies, waits for them, and re-layouts: 7.17 us -> 5.77 us
    pallas_call x9 -> x11, Pallas kernels: 21.8 us -> 22.7 us  [call(): pl.pallas_call(kernel, out_shape=out_shape, compiler_params=pltpu.Compile...]
  transfers between devices with their start and end apart: 22 -> 22, of which waited for: 14 -> 14; matrix products, arithmetic and copies ran while one was open for 0% -> 0% of each run, Pallas kernels for 3% -> 4%
where the time goes in v8:
time: 172 us; the launch traced here: 171 us
  blocking collectives  79.9 us (46%)
  starting transfers between devices  35.7 us (21%)
  waiting for transfers between devices  25.3 us (15%)
  Pallas kernels  22.7 us (13%)
  local copies, waits for them, and re-layouts  5.79 us (3%)
    all_to_all x3, blocking collectives, swap(): return lax.all_to_all(value, axes, 0, 0, tiled=True)  79.9 us
    ppermute x21, starting transfers between devices, shifted(): lax.ppermute(value, axis, [(i, (i + distance) % size) for i in range(size)])  26.7 us
    pallas_call x11, Pallas kernels, call(): pl.pallas_call(kernel, out_shape=out_shape, compiler_params=pltpu.Compile...  22.7 us
    ppermute x21, waiting for transfers between devices, shifted(): lax.ppermute(value, axis, [(i, (i + distance) % size) for i in range(size)])  17.6 us
    all_to_all x1, starting transfers between devices, swap(): return lax.all_to_all(value, axes, 0, 0, tiled=True)  9.03 us
    all_to_all x1, waiting for transfers between devices, swap(): return lax.all_to_all(value, axes, 0, 0, tiled=True)  7.71 us
    unnamed x32, local copies, waits for them, and re-layouts  5.77 us
  transfers between devices with their start and end apart: 22, of which 14 were waited for; matrix products, arithmetic and copies ran while one was open for 0% of the time, Pallas kernels for 4%

profile of v8, /device:TPU:1, one launch (start us, length us, event | category | flops | bytes accessed | tf_op | source)
XLA Modules:
  0.0 171.2 jit_solution(12727331931957865436)
XLA Ops:
  0.6 6.3 %shard_map.158 = (bf16[8,208,128]{2,1,0:T(8,128)(2,1)}, f32[4,192,256]{2,1,0:T(8,128)}) custom-call(bf16[192,256]{1,0:T(8,128)(2,1)} %k_ref.1, bf16[192,512]{1,0:T(8,128)(2,1)} %refs_1_.1, f32[4,192]{1,0:T(4,128)} %decay_ref.1, f32[4,192]{1,0:T(4,128)} %logit_ref.1), custom_call_target="tpu_custom_call" | custom-call | tf_op jit(solution)/shard_map/pallas_call | solution.py:78
  7.0 9.0 %all-to-all-start = ((bf16[8,208,128]{2,1,0:T(8,128)(2,1)}), bf16[8,208,128]{2,1,0:T(8,128)(2,1)S(1)}, u32[]{:S(2)}, u32[]{:S(2)}) async-start(bf16[8,208,128]{2,1,0:T(8,128)(2,1)} %get-tuple-element.25), calls=%async_computation | async-start | bytes 851968 | tf_op jit(solution)/shard_map/all_to_all | solution.py:387
  21.7 1.6 shard_map.159
  23.4 7.7 %all-to-all-done.got_ref = bf16[8,208,128]{2,1,0:T(8,128)(2,1)S(1)} async-done(((bf16[8,208,128]{2,1,0:T(8,128)(2,1)}), bf16[8,208,128]{2,1,0:T(8,128)(2,1)S(1)}, u32[]{:S(2)}, u32[]{:S(2)}) %all-to-all-start) | async-done | bytes 426016 | tf_op jit(solution)/shard_map/all_to_all | solution.py:387
  32.2 2.6 %collective-permute-start.2 = (bf16[208,128]{1,0:T(8,128)(2,1)S(1)}, bf16[208,128]{1,0:T(8,128)(2,1)S(1)}, u32[]{:S(2)}, u32[]{:S(2)}) collective-permute-start(bf16[208,128]{1,0:T(8,128)(2,1)S(1)} %shard_map.160), channel_id=1, source_target_pairs={{0,192},{64,0},{128,64},{192,128},{1,193},{65,1},{129,65},{193,129... | collective-permute-start | bytes 159752 | tf_op jit(solution)/shard_map/ppermute | solution.py:383
  36.0 3.3 %collective-permute-done.1.rest_1_ = bf16[208,128]{1,0:T(8,128)(2,1)S(1)} collective-permute-done((bf16[208,128]{1,0:T(8,128)(2,1)S(1)}, bf16[208,128]{1,0:T(8,128)(2,1)S(1)}, u32[]{:S(2)}, u32[]{:S(2)}) %collective-permute-start.1) | collective-permute-done | bytes 53280 | tf_op jit(solution)/shard_map/ppermute | solution.py:383
  39.8 1.9 %shard_map.161 = bf16[8,112,128]{2,1,0:T(8,128)(2,1)S(1)} custom-call(s32[4]{0:T(128)S(1)} %pad_add_fusion.here_ref, bf16[8,208,128]{2,1,0:T(8,128)(2,1)S(1)} %all-to-all-done.got_ref, bf16[8,48,128]{2,1,0:T(8,128)(2,1)S(1)} %get-tuple-element.26.after_ref.route_ref, bf16[208,128]{1,0:T(8,128)(2,1)S(1)} %collective-permute-done.rest_0_, ...), custom_call_target="tpu_custom_call" | custom-call | tf_op jit(solution)/shard_map/pallas_call | solution.py:78
  41.8 11.4 %all_to_all.20.state_ref.got_ref = bf16[8,112,128]{2,1,0:T(8,128)(2,1)S(1)} all-to-all(bf16[8,112,128]{2,1,0:T(8,128)(2,1)S(1)} %shard_map.161), channel_id=1, replica_groups=mesh['x'=4,'z'=8,'y'=4,'c'=2] {'z'}, dimensions={0} | all-to-all | bytes 458752 | tf_op jit(solution)/shard_map/all_to_all | solution.py:387
  54.4 3.9 %collective-permute-start.3 = (bf16[4,192,256]{2,1,0:T(8,128)(2,1)S(1)}, bf16[4,192,256]{2,1,0:T(8,128)(2,1)S(1)}, u32[]{:S(2)}, u32[]{:S(2)}) collective-permute-start(bf16[4,192,256]{2,1,0:T(8,128)(2,1)S(1)} %get-tuple-element.28), channel_id=1, source_target_pairs={{0,1},{1,0},{2,3},{3,2},{4,5},{5,4},{6,7},{7,6},{8,9},{9,8},{10,11... | collective-permute-start | bytes 1179656 | tf_op jit(solution)/shard_map/ppermute | solution.py:383
  61.2 1.5 collective-permute-start.6
  62.7 1.6 collective-permute-start.5
  65.2 2.7 %collective-permute-done.5 = bf16[192,256]{1,0:T(8,128)(2,1)S(1)} collective-permute-done((bf16[192,256]{1,0:T(8,128)(2,1)S(1)}, bf16[192,256]{1,0:T(8,128)(2,1)S(1)}, u32[]{:S(2)}, u32[]{:S(2)}) %collective-permute-start.5) | collective-permute-done | bytes 98336 | tf_op jit(solution)/shard_map/ppermute | solution.py:383
  68.0 2.4 %collective-permute-start.8 = (bf16[192,256]{1,0:T(8,128)(2,1)S(1)}, bf16[192,256]{1,0:T(8,128)(2,1)S(1)}, u32[]{:S(2)}, u32[]{:S(2)}) collective-permute-start(bf16[192,256]{1,0:T(8,128)(2,1)S(1)} %fusion.3.rest_0_), channel_id=1, source_target_pairs={{0,16},{8,24},{16,32},{24,40},{32,48},{40,56},{48,0},{56,8},{1,17}... | collective-permute-start | bytes 294920 | tf_op jit(solution)/shard_map/ppermute | solution.py:383
  71.8 1.4 collective-permute-done.10.rest_6_
  74.8 1.5 collective-permute-start.9
  76.2 4.1 %shard_map.164 = (bf16[8,512,192]{2,1,0:T(8,128)(2,1)S(1)}, bf16[8,192,512]{2,1,0:T(8,128)(2,1)S(1)}) custom-call(s32[4]{0:T(128)S(1)} %pad_add_fusion.here_ref, bf16[8,112,128]{2,1,0:T(8,128)(2,1)S(1)} %all_to_all.20.state_ref.got_ref), custom_call_target="tpu_custom_call" | custom-call | flops 1000000000 | bytes 4000000 | tf_op jit(solution)/shard_map/pallas_call | solution.py:78
  81.4 36.6 %all_to_all.21 = bf16[32,128,256]{2,1,0:T(8,128)(2,1)S(1)} all-to-all(bf16[32,128,256]{2,1,0:T(8,128)(2,1)S(1)} %shard_map.165), channel_id=1, replica_groups=mesh['x'=4,'z'=8,'y'=4,'c'=2] {'x','y','c'}, dimensions={0} | all-to-all | bytes 4194304 | tf_op jit(solution)/shard_map/all_to_all | solution.py:387
  118.0 3.9 %shard_map.166 = bf16[4,8,128,256]{3,2,1,0:T(8,128)(2,1)S(1)} custom-call(bf16[4,8,128,256]{3,2,1,0:T(8,128)(2,1)S(1)} %bitcast.29, f32[1,2048]{1,0:T(1,128)S(1)} %bitcast.34, bf16[2048,512]{1,0:T(8,128)(2,1)S(1)} %bitcast.31, bf16[2048,512]{1,0:T(8,128)(2,1)S(1)} %bitcast.32, bf16[512,2048]{1,0:T(8,128)(2,1)S(1)} %bitcast.33), custom_call_target="tpu_custom_call" | custom-call | tf_op jit(solution)/shard_map/pallas_call | solution.py:78
  121.9 31.9 %all_to_all.22.rows_ref = bf16[32,128,256]{2,1,0:T(8,128)(2,1)S(1)} all-to-all(bf16[32,128,256]{2,1,0:T(8,128)(2,1)S(1)} %bitcast.30), channel_id=1, replica_groups=mesh['x'=4,'z'=8,'y'=4,'c'=2] {'x','y','c'}, dimensions={0} | all-to-all | bytes 4194304 | tf_op jit(solution)/shard_map/all_to_all | solution.py:387
  154.2 1.6 collective-permute-start.14
  161.9 1.5 collective-permute-done.17
  164.9 1.5 collective-permute-start.19
  167.0 1.7 %collective-permute-done.20 = bf16[192,256]{1,0:T(8,128)(2,1)S(1)} collective-permute-done((bf16[192,256]{1,0:T(8,128)(2,1)S(1)}, bf16[192,256]{1,0:T(8,128)(2,1)S(1)}, u32[]{:S(2)}, u32[]{:S(2)}) %collective-permute-start.20) | collective-permute-done | bytes 98336 | tf_op jit(solution)/shard_map/ppermute | solution.py:383
  168.7 1.8 %collective-permute-done.19 = bf16[192,256]{1,0:T(8,128)(2,1)S(1)} collective-permute-done((bf16[192,256]{1,0:T(8,128)(2,1)S(1)}, bf16[192,256]{1,0:T(8,128)(2,1)S(1)}, u32[]{:S(2)}, u32[]{:S(2)}) %collective-permute-start.19) | collective-permute-done | bytes 98336 | tf_op jit(solution)/shard_map/ppermute | solution.py:383
  (73 shorter events, 26.9 us)
Async XLA Ops:
  7.0 24.1 %all-to-all-start = ((bf16[8,208,128]{2,1,0:T(8,128)(2,1)}), bf16[8,208,128]{2,1,0:T(8,128)(2,1)S(1)}, u32[]{:S(2)}, u32[]{:S(2)}) async-start(bf16[8,208,128]{2,1,0:T(8,128)(2,1)} %get-tuple-element.25), calls=%async_computation | async-start | bytes 851968 | tf_op jit(solution)/shard_map/all_to_all | solution.py:387
  32.2 3.8 %collective-permute-start.2 = (bf16[208,128]{1,0:T(8,128)(2,1)S(1)}, bf16[208,128]{1,0:T(8,128)(2,1)S(1)}, u32[]{:S(2)}, u32[]{:S(2)}) collective-permute-start(bf16[208,128]{1,0:T(8,128)(2,1)S(1)} %shard_map.160), channel_id=1, source_target_pairs={{0,192},{64,0},{128,64},{192,128},{1,193},{65,1},{129,65},{193,129... | collective-permute-start | bytes 159752 | tf_op jit(solution)/shard_map/ppermute | solution.py:383
  34.7 4.5 %collective-permute-start.1 = (bf16[208,128]{1,0:T(8,128)(2,1)S(1)}, bf16[208,128]{1,0:T(8,128)(2,1)S(1)}, u32[]{:S(2)}, u32[]{:S(2)}) collective-permute-start(bf16[208,128]{1,0:T(8,128)(2,1)S(1)} %shard_map.160), channel_id=1, source_target_pairs={{0,128},{64,192},{128,0},{192,64},{1,129},{65,193},{129,1},{193,65... | collective-permute-start | bytes 159752 | tf_op jit(solution)/shard_map/ppermute | solution.py:383
  35.3 4.5 %collective-permute-start = (bf16[208,128]{1,0:T(8,128)(2,1)S(1)}, bf16[208,128]{1,0:T(8,128)(2,1)S(1)}, u32[]{:S(2)}, u32[]{:S(2)}) collective-permute-start(bf16[208,128]{1,0:T(8,128)(2,1)S(1)} %shard_map.160), channel_id=1, source_target_pairs={{0,64},{64,128},{128,192},{192,0},{1,65},{65,129},{129,193},{193,1... | collective-permute-start | bytes 159752 | tf_op jit(solution)/shard_map/ppermute | solution.py:383
  54.4 5.2 %collective-permute-start.3 = (bf16[4,192,256]{2,1,0:T(8,128)(2,1)S(1)}, bf16[4,192,256]{2,1,0:T(8,128)(2,1)S(1)}, u32[]{:S(2)}, u32[]{:S(2)}) collective-permute-start(bf16[4,192,256]{2,1,0:T(8,128)(2,1)S(1)} %get-tuple-element.28), channel_id=1, source_target_pairs={{0,1},{1,0},{2,3},{3,2},{4,5},{5,4},{6,7},{7,6},{8,9},{9,8},{10,11... | collective-permute-start | bytes 1179656 | tf_op jit(solution)/shard_map/ppermute | solution.py:383
  59.8 5.4 %collective-permute-start.4 = (bf16[192,256]{1,0:T(8,128)(2,1)S(1)}, bf16[192,256]{1,0:T(8,128)(2,1)S(1)}, u32[]{:S(2)}, u32[]{:S(2)}) collective-permute-start(bf16[192,256]{1,0:T(8,128)(2,1)S(1)} %get-tuple-element.44), channel_id=1, source_target_pairs={{0,2},{2,4},{4,6},{6,0},{1,3},{3,5},{5,7},{7,1},{8,10},{10,12},{12... | collective-permute-start | bytes 294920 | tf_op jit(solution)/shard_map/ppermute | solution.py:383
  61.2 4.0 %collective-permute-start.6 = (bf16[192,256]{1,0:T(8,128)(2,1)S(1)}, bf16[192,256]{1,0:T(8,128)(2,1)S(1)}, u32[]{:S(2)}, u32[]{:S(2)}) collective-permute-start(bf16[192,256]{1,0:T(8,128)(2,1)S(1)} %get-tuple-element.45), channel_id=1, source_target_pairs={{0,6},{2,0},{4,2},{6,4},{1,7},{3,1},{5,3},{7,5},{8,14},{10,8},{12,... | collective-permute-start | bytes 294920 | tf_op jit(solution)/shard_map/ppermute | solution.py:383
  62.7 5.2 %collective-permute-start.5 = (bf16[192,256]{1,0:T(8,128)(2,1)S(1)}, bf16[192,256]{1,0:T(8,128)(2,1)S(1)}, u32[]{:S(2)}, u32[]{:S(2)}) collective-permute-start(bf16[192,256]{1,0:T(8,128)(2,1)S(1)} %get-tuple-element.46), channel_id=1, source_target_pairs={{0,4},{2,6},{4,0},{6,2},{1,5},{3,7},{5,1},{7,3},{8,12},{10,14},{12... | collective-permute-start | bytes 294920 | tf_op jit(solution)/shard_map/ppermute | solution.py:383
  67.9 102.6 %copy-start.4 = (bf16[192,256]{1,0:T(8,128)(2,1)}, bf16[192,256]{1,0:T(8,128)(2,1)S(1)}, u32[]{:S(2)}) copy-start(bf16[192,256]{1,0:T(8,128)(2,1)S(1)} %fusion.3.rest_0_) | copy-start | bytes 294916
  67.9 5.4 %collective-permute-start.10 = (bf16[192,256]{1,0:T(8,128)(2,1)S(1)}, bf16[192,256]{1,0:T(8,128)(2,1)S(1)}, u32[]{:S(2)}, u32[]{:S(2)}) collective-permute-start(bf16[192,256]{1,0:T(8,128)(2,1)S(1)} %fusion.3.rest_0_), channel_id=1, source_target_pairs={{0,48},{8,56},{16,0},{24,8},{32,16},{40,24},{48,32},{56,40},{1,49}... | collective-permute-start | bytes 294920 | tf_op jit(solution)/shard_map/ppermute | solution.py:383
  68.0 6.7 %collective-permute-start.8 = (bf16[192,256]{1,0:T(8,128)(2,1)S(1)}, bf16[192,256]{1,0:T(8,128)(2,1)S(1)}, u32[]{:S(2)}, u32[]{:S(2)}) collective-permute-start(bf16[192,256]{1,0:T(8,128)(2,1)S(1)} %fusion.3.rest_0_), channel_id=1, source_target_pairs={{0,16},{8,24},{16,32},{24,40},{32,48},{40,56},{48,0},{56,8},{1,17}... | collective-permute-start | bytes 294920 | tf_op jit(solution)/shard_map/ppermute | solution.py:383
  70.4 10.0 %collective-permute-start.13 = (bf16[192,256]{1,0:T(8,128)(2,1)S(1)}, bf16[192,256]{1,0:T(8,128)(2,1)S(1)}, u32[]{:S(2)}, u32[]{:S(2)}) collective-permute-start(bf16[192,256]{1,0:T(8,128)(2,1)S(1)} %fusion.3.rest_0_), channel_id=1, source_target_pairs={{0,56},{8,0},{16,8},{24,16},{32,24},{40,32},{48,40},{56,48},{1,57}... | collective-permute-start | bytes 294920 | tf_op jit(solution)/shard_map/ppermute | solution.py:383
  71.5 8.9 %collective-permute-start.7 = (bf16[192,256]{1,0:T(8,128)(2,1)S(1)}, bf16[192,256]{1,0:T(8,128)(2,1)S(1)}, u32[]{:S(2)}, u32[]{:S(2)}) collective-permute-start(bf16[192,256]{1,0:T(8,128)(2,1)S(1)} %fusion.3.rest_0_), channel_id=1, source_target_pairs={{0,8},{8,16},{16,24},{24,32},{32,40},{40,48},{48,56},{56,0},{1,9},... | collective-permute-start | bytes 294920 | tf_op jit(solution)/shard_map/ppermute | solution.py:383
  73.3 7.1 %collective-permute-start.12 = (bf16[192,256]{1,0:T(8,128)(2,1)S(1)}, bf16[192,256]{1,0:T(8,128)(2,1)S(1)}, u32[]{:S(2)}, u32[]{:S(2)}) collective-permute-start(bf16[192,256]{1,0:T(8,128)(2,1)S(1)} %collective-permute-done.10.rest_6_), channel_id=1, source_target_pairs={{0,56},{8,0},{16,8},{24,16},{32,24},{40,32},{48,40},{56,48},{1,57}... | collective-permute-start | bytes 294920 | tf_op jit(solution)/shard_map/ppermute | solution.py:383
  74.1 6.5 %collective-permute-start.11 = (bf16[192,256]{1,0:T(8,128)(2,1)S(1)}, bf16[192,256]{1,0:T(8,128)(2,1)S(1)}, u32[]{:S(2)}, u32[]{:S(2)}) collective-permute-start(bf16[192,256]{1,0:T(8,128)(2,1)S(1)} %collective-permute-done.10.rest_6_), channel_id=1, source_target_pairs={{0,48},{8,56},{16,0},{24,8},{32,16},{40,24},{48,32},{56,40},{1,49}... | collective-permute-start | bytes 294920 | tf_op jit(solution)/shard_map/ppermute | solution.py:383
  74.8 5.9 %collective-permute-start.9 = (bf16[192,256]{1,0:T(8,128)(2,1)S(1)}, bf16[192,256]{1,0:T(8,128)(2,1)S(1)}, u32[]{:S(2)}, u32[]{:S(2)}) collective-permute-start(bf16[192,256]{1,0:T(8,128)(2,1)S(1)} %collective-permute-done.8.rest_2_), channel_id=1, source_target_pairs={{0,8},{8,16},{16,24},{24,32},{32,40},{40,48},{48,56},{56,0},{1,9},... | collective-permute-start | bytes 294920 | tf_op jit(solution)/shard_map/ppermute | solution.py:383
  80.7 37.3 %copy-start.3 = (bf16[1,512,2048]{2,1,0:T(8,128)(2,1)S(1)}, bf16[1,512,2048]{2,1,0:T(8,128)(2,1)}, u32[]{:S(2)}) copy-start(bf16[1,512,2048]{2,1,0:T(8,128)(2,1)} %param.29) | copy-start | bytes 6291460
  154.2 5.5 %collective-permute-start.14 = (bf16[192,256]{1,0:T(8,128)(2,1)S(1)}, bf16[192,256]{1,0:T(8,128)(2,1)S(1)}, u32[]{:S(2)}, u32[]{:S(2)}) collective-permute-start(bf16[192,256]{1,0:T(8,128)(2,1)S(1)} %get-tuple-element.33), channel_id=1, source_target_pairs={{0,8},{8,16},{16,24},{24,32},{32,40},{40,48},{48,56},{56,0},{1,9},... | collective-permute-start | bytes 294920 | tf_op jit(solution)/shard_map/ppermute | solution.py:383
  155.8 7.7 %collective-permute-start.17 = (bf16[192,256]{1,0:T(8,128)(2,1)S(1)}, bf16[192,256]{1,0:T(8,128)(2,1)S(1)}, u32[]{:S(2)}, u32[]{:S(2)}) collective-permute-start(bf16[192,256]{1,0:T(8,128)(2,1)S(1)} %get-tuple-element.39), channel_id=1, source_target_pairs={{0,48},{8,56},{16,0},{24,8},{32,16},{40,24},{48,32},{56,40},{1,49}... | collective-permute-start | bytes 294920 | tf_op jit(solution)/shard_map/ppermute | solution.py:383
  157.0 7.9 %collective-permute-start.18 = (bf16[192,256]{1,0:T(8,128)(2,1)S(1)}, bf16[192,256]{1,0:T(8,128)(2,1)S(1)}, u32[]{:S(2)}, u32[]{:S(2)}) collective-permute-start(bf16[192,256]{1,0:T(8,128)(2,1)S(1)} %get-tuple-element.40), channel_id=1, source_target_pairs={{0,56},{8,0},{16,8},{24,16},{32,24},{40,32},{48,40},{56,48},{1,57}... | collective-permute-start | bytes 294920 | tf_op jit(solution)/shard_map/ppermute | solution.py:383
  159.7 7.2 %collective-permute-start.15 = (bf16[192,256]{1,0:T(8,128)(2,1)S(1)}, bf16[192,256]{1,0:T(8,128)(2,1)S(1)}, u32[]{:S(2)}, u32[]{:S(2)}) collective-permute-start(bf16[192,256]{1,0:T(8,128)(2,1)S(1)} %get-tuple-element.36), channel_id=1, source_target_pairs={{0,56},{8,0},{16,8},{24,16},{32,24},{40,32},{48,40},{56,48},{1,57}... | collective-permute-start | bytes 294920 | tf_op jit(solution)/shard_map/ppermute | solution.py:383
  160.3 6.7 %collective-permute-start.16 = (bf16[192,256]{1,0:T(8,128)(2,1)S(1)}, bf16[192,256]{1,0:T(8,128)(2,1)S(1)}, u32[]{:S(2)}, u32[]{:S(2)}) collective-permute-start(bf16[192,256]{1,0:T(8,128)(2,1)S(1)} %get-tuple-element.37), channel_id=1, source_target_pairs={{0,8},{8,16},{16,24},{24,32},{32,40},{40,48},{48,56},{56,0},{1,9},... | collective-permute-start | bytes 294920 | tf_op jit(solution)/shard_map/ppermute | solution.py:383
  161.3 7.4 %collective-permute-start.20 = (bf16[192,256]{1,0:T(8,128)(2,1)S(1)}, bf16[192,256]{1,0:T(8,128)(2,1)S(1)}, u32[]{:S(2)}, u32[]{:S(2)}) collective-permute-start(bf16[192,256]{1,0:T(8,128)(2,1)S(1)} %convert_add_fusion.1), channel_id=1, source_target_pairs={{0,16},{8,24},{16,32},{24,40},{32,48},{40,56},{48,0},{56,8},{1,17}... | collective-permute-start | bytes 294920 | tf_op jit(solution)/shard_map/ppermute | solution.py:383
  164.9 5.6 %collective-permute-start.19 = (bf16[192,256]{1,0:T(8,128)(2,1)S(1)}, bf16[192,256]{1,0:T(8,128)(2,1)S(1)}, u32[]{:S(2)}, u32[]{:S(2)}) collective-permute-start(bf16[192,256]{1,0:T(8,128)(2,1)S(1)} %add_convert_fusion.1), channel_id=1, source_target_pairs={{0,48},{8,56},{16,0},{24,8},{32,16},{40,24},{48,32},{56,40},{1,49}... | collective-permute-start | bytes 294920 | tf_op jit(solution)/shard_map/ppermute | solution.py:383
  (14 other events, 230.6 us)
